TPU v7x, 256 devices: a whole 4x4x8 slice. The times are simulated.
256 devices in a mesh: row: 16 (over z, x_lo), col: 16 (over y, x_hi, core).
Axes of the slice: x: 4 (x_hi: 2, x_lo: 2; x = x_hi * 2 + x_lo), y: 4, z: 8, core: 2. Of those that a mesh axis runs over, the one named last changes fastest.
Arguments:
- tokens: bfloat16 [512, 12288], P('col', 'row'), may hold values from -6 to 6
- up_weight: bfloat16 [12288, 24576], P('row', 'col'), may hold values from -0.0546875 to 0.0546875
- down_weight: bfloat16 [24576, 12288], P('col', 'row'), may hold values from -0.0390625 to 0.0390625
- out_grad: bfloat16 [512, 12288], P('col', 'row'), may hold values from -6 to 6
Outputs:
- output: bfloat16 [512, 12288], P('col', 'row')
- token_grad: bfloat16 [512, 12288], P('col', 'row')
- up_grad: bfloat16 [12288, 24576], P('row', 'col')
- down_grad: bfloat16 [24576, 12288], P('col', 'row')
All inputs are finite; a program needn't handle non-finite values.
Results may differ from a plain program's by a relative error of at most 0.005.
Values may be sent and summed in bfloat16 or wider, within the bound.
No kernel may reach another device: no remote copies, remote signals or barrier semaphores. Data moves between devices by JAX's collectives and lax.ppermute only.
A program may use at most 64 MiB of HBM per device.

v0:
```python
import math

import jax
import jax.numpy as jnp
from jax import lax
from jax.sharding import PartitionSpec as P

bf16, f32 = jnp.bfloat16, jnp.float32
tanh_scale = math.sqrt(2.0 / math.pi)

Z, XL, Y, XH, CORE = 8, 2, 4, 2, 2


def gelu_parts(value):
    tangent = jnp.tanh(tanh_scale * (value + 0.044715 * value * value * value))
    result = 0.5 * value * (1.0 + tangent)
    slope = 0.5 * (1.0 + tangent) + 0.5 * value * (1.0 - tangent * tangent) * tanh_scale * (
        1.0 + 3.0 * 0.044715 * value * value
    )
    return (result, slope)


def contract_rows(left, right):
    return lax.dot_general(
        left, right, (((0,), (0,)), ((), ())), preferred_element_type=f32
    )


def contract_cols(left, right):
    return lax.dot_general(
        left, right, (((1,), (1,)), ((), ())), preferred_element_type=f32
    )


def even(i, n):
    return i ^ 1


def odd(i, n):
    return (i + 1) % n if i % 2 else (i - 1) % n


def swap_z(x, pairs):
    return lax.ppermute(
        x, "row", [(pairs(z, Z) * XL + k, z * XL + k) for z in range(Z) for k in range(XL)]
    )


def swap_xl(x):
    return lax.ppermute(x, "row", [(i ^ 1, i) for i in range(Z * XL)])


def exchange_col(x):
    n = Y * XH
    groups = [[k * CORE + c for k in range(n)] for c in range(CORE)]
    return lax.all_to_all(x, "col", 0, 0, axis_index_groups=groups, tiled=True)


def swap_core(x):
    return lax.ppermute(x, "col", [(i ^ 1, i) for i in range(Y * XH * CORE)])


def gather_col(x):
    n = Y * XH
    x = jnp.broadcast_to(x[None], (n,) + x.shape).reshape(n * x.shape[0], x.shape[1])
    x = exchange_col(x)
    return jnp.concatenate([x, swap_core(x)], axis=0)


def scatter_col(x):
    n = x.shape[0] // 2
    x = x[:n] + swap_core(x[n:])
    x = exchange_col(x.astype(bf16)).astype(f32)
    return jnp.sum(x.reshape(Y * XH, -1, x.shape[1]), axis=0).astype(bf16)


def block_at(r, n):
    z = lax.axis_index("row") // XL
    return lax.rem(z + r * (1 - 2 * lax.rem(z, 2)) + Z, Z) * n


def scatter_row(x):
    n, m, h = x.shape[0] // Z, x.shape[1] // 2, Z // 2

    def block(r):
        return lax.dynamic_slice_in_dim(x, block_at(r, n), n, axis=0)

    far = block(h)
    ways = (even, odd)
    one = swap_z(far[:, :m].astype(bf16), ways[0]).astype(f32)
    two = swap_z(far[:, m:].astype(bf16), ways[1]).astype(f32)
    one = lax.pad(one, 0.0, ((0, 0, 0), (0, m, 0)))
    two = lax.pad(two, 0.0, ((0, 0, 0), (m, 0, 0)))
    sign = 1
    for s in range(h - 1, 0, -1):
        ways, sign = ways[::-1], -sign
        one = swap_z((block(sign * s) + one).astype(bf16), ways[0])
        two = swap_z((block(-sign * s) + two).astype(bf16), ways[1])
        one, two = lax.optimization_barrier((one, two))
        one, two = one.astype(f32), two.astype(f32)
    total = block(0) + one + two
    return total + swap_xl(total.astype(bf16)).astype(f32)


def gather_row(own):
    n, cols = own.shape
    m, h = cols // 2, Z // 2
    panel = jnp.zeros((Z * n, cols), own.dtype)

    def put(panel, piece, r, col=0):
        return lax.dynamic_update_slice(panel, piece, (block_at(r, n), col))

    panel = put(panel, own, 0)
    one, two = own, own
    ways, sign = (even, odd), 1
    for s in range(1, h):
        one, two = swap_z(one, ways[0]), swap_z(two, ways[1])
        panel = put(panel, one, sign * s)
        panel = put(panel, two, -sign * s)
        ways, sign = ways[::-1], -sign
    panel = put(panel, swap_z(one[:, :m], ways[0]), h)
    return put(panel, swap_z(two[:, m:], ways[1]), h, m)


def local(tokens, up_weight, down_weight, out_grad):
    total = tokens.shape[0] * Y * XH * CORE
    scale = 1.0 / math.sqrt(total)
    width = tokens.shape[1]
    panel = gather_col(jnp.concatenate([tokens, out_grad], axis=1))
    token_panel, grad_panel = panel[:, :width], panel[:, width:]
    hidden = scatter_row(jnp.dot(token_panel, up_weight, preferred_element_type=f32))
    act_grad = scatter_row(contract_cols(grad_panel, down_weight))
    activ, slope = gelu_parts(hidden)
    act_panel = gather_row(activ.astype(bf16))
    dh_panel = gather_row((act_grad * slope).astype(bf16))
    output = jnp.dot(act_panel, down_weight, preferred_element_type=f32)
    token_grad = contract_cols(dh_panel, up_weight)
    both = scatter_col(jnp.concatenate([output, token_grad], axis=1))
    down_grad = (contract_rows(act_panel, grad_panel) * scale).astype(bf16)
    up_grad = (contract_rows(token_panel, dh_panel) * scale).astype(bf16)
    return (both[:, :width], both[:, width:], up_grad, down_grad)


def solution(mesh):
    placed = (P("col", "row"), P("row", "col"), P("col", "row"), P("col", "row"))
    return jax.shard_map(
        local,
        mesh=mesh,
        in_specs=placed,
        out_specs=(P("col", "row"), P("col", "row"), P("row", "col"), P("col", "row")),
        check_vma=False,
    )
```

profile of v0, /device:TPU:1, one launch (start us, length us, event | category | flops | bytes accessed | tf_op | source)
XLA Modules:
  0.0 136.2 jit_solution(5866332326478290861)
XLA Ops:
  0.6 1.0 pad_maximum_fusion.4
  1.7 20.8 %all_to_all.18 = bf16[8,32,1536]{2,1,0:T(8,128)(2,1)S(1)} all-to-all(bf16[8,32,1536]{2,1,0:T(8,128)(2,1)S(1)} %broadcast_in_dim.2), channel_id=1, replica_groups={{0,2,4,6,8,10,12,14},{1,3,5,7,9,11,13,15},{16,18,20,22,24,26,28,30},{17..., dimensions={0} | all-to-all | bytes 1572864 | tf_op jit(solution)/shard_map/all_to_all | solution.py:56
  22.5 1.9 %collective-permute-start = (bf16[256,1536]{1,0:T(8,128)(2,1)S(1)}, bf16[256,1536]{1,0:T(8,128)(2,1)}, u32[]{:S(2)}, u32[]{:S(2)}) collective-permute-start(bf16[256,1536]{1,0:T(8,128)(2,1)S(1)} %bitcast.11), channel_id=1, source_target_pairs={{1,0},{0,1},{3,2},{2,3},{5,4},{4,5},{7,6},{6,7},{9,8},{8,9},{11,10... | collective-permute-start | bytes 2359304 | tf_op jit(solution)/shard_map/ppermute | solution.py:60
  24.3 2.0 %collective-permute-done = bf16[256,1536]{1,0:T(8,128)(2,1)} collective-permute-done((bf16[256,1536]{1,0:T(8,128)(2,1)S(1)}, bf16[256,1536]{1,0:T(8,128)(2,1)}, u32[]{:S(2)}, u32[]{:S(2)}) %collective-permute-start) | collective-permute-done | bytes 786464 | tf_op jit(solution)/shard_map/ppermute | solution.py:60
  26.4 2.4 %fusion.16 = f32[512,1536]{1,0:T(8,128)S(1)} fusion(bf16[768,1536]{1,0:T(8,128)(2,1)S(1)} %copy-done, bf16[256,1536]{1,0:T(8,128)(2,1)S(1)} %bitcast.12, bf16[256,1536]{1,0:T(8,128)(2,1)} %collective-permute-done), kind=kOutput, calls=%fused_computation.62 | convolution fusion | flops 1209532416 | bytes 7077888 | tf_op jit(solution)/shard_map/dot_general | solution.py:131
  28.8 5.7 %collective-permute-start.3 = (bf16[64,768]{1,0:T(8,128)(2,1)S(1)}, bf16[64,768]{1,0:T(8,128)(2,1)S(1)}, u32[]{:S(2)}, u32[]{:S(2)}) collective-permute-start(bf16[64,768]{1,0:T(8,128)(2,1)S(1)} %get-tuple-element.48), channel_id=1, source_target_pairs={{224,0},{240,16},{64,32},{80,48},{32,64},{48,80},{128,96},{144,112... | collective-permute-start | bytes 294920 | tf_op jit(solution)/shard_map/ppermute | solution.py:44
  34.5 2.4 %fusion.12 = f32[512,1536]{1,0:T(8,128)S(1)} fusion(bf16[1536,768]{1,0:T(8,128)(2,1)S(1)} %copy-done.6, bf16[256,1536]{1,0:T(8,128)(2,1)} %collective-permute-done, bf16[256,1536]{1,0:T(8,128)(2,1)S(1)} %bitcast.13), kind=kOutput, calls=%fused_computation.40 | convolution fusion | flops 1209532416 | bytes 7077888 | tf_op jit(solution)/shard_map/dot_general | solution.py:30
  37.0 1.5 %collective-permute-start.20 = (bf16[64,768]{1,0:T(8,128)(2,1)S(1)}, bf16[64,768]{1,0:T(8,128)(2,1)S(1)}, u32[]{:S(2)}, u32[]{:S(2)}) collective-permute-start(bf16[64,768]{1,0:T(8,128)(2,1)S(1)} %get-tuple-element.46), channel_id=1, source_target_pairs={{224,0},{240,16},{64,32},{80,48},{32,64},{48,80},{128,96},{144,112... | collective-permute-start | bytes 294920 | tf_op jit(solution)/shard_map/ppermute | solution.py:44
  38.5 0.7 collective-permute-start.18
  39.3 0.6 collective-permute-start.2
  39.9 1.0 collective-permute-start.4
  40.9 0.9 collective-permute-done.20
  41.7 0.5 collective-permute-done.18
  42.3 1.0 collective-permute-start.19
  43.4 0.5 collective-permute-start.21
  43.9 1.6 %collective-permute-done.2 = bf16[64,1536]{1,0:T(8,128)(2,1)S(1)} collective-permute-done((bf16[64,1536]{1,0:T(8,128)(2,1)S(1)}, bf16[64,1536]{1,0:T(8,128)(2,1)S(1)}, u32[]{:S(2)}, u32[]{:S(2)}) %collective-permute-start.2) | collective-permute-done | bytes 196640 | tf_op jit(solution)/shard_map/ppermute | solution.py:44
  45.5 1.0 collective-permute-done.4
  46.6 1.1 collective-permute-start.5
  47.8 0.5 collective-permute-start.6
  48.3 1.0 collective-permute-done.19
  49.3 0.7 collective-permute-done.21
  50.1 1.5 %collective-permute-start.22 = (bf16[64,1536]{1,0:T(8,128)(2,1)S(1)}, bf16[64,1536]{1,0:T(8,128)(2,1)S(1)}, u32[]{:S(2)}, u32[]{:S(2)}) collective-permute-start(bf16[64,1536]{1,0:T(8,128)(2,1)S(1)} %get-tuple-element.37), channel_id=1, source_target_pairs={{32,0},{48,16},{0,32},{16,48},{96,64},{112,80},{64,96},{80,112},{1... | collective-permute-start | bytes 589832 | tf_op jit(solution)/shard_map/ppermute | solution.py:44
  51.7 2.4 %collective-permute-done.5 = bf16[64,1536]{1,0:T(8,128)(2,1)S(1)} collective-permute-done((bf16[64,1536]{1,0:T(8,128)(2,1)S(1)}, bf16[64,1536]{1,0:T(8,128)(2,1)S(1)}, u32[]{:S(2)}, u32[]{:S(2)}) %collective-permute-start.5) | collective-permute-done | bytes 196640 | tf_op jit(solution)/shard_map/ppermute | solution.py:44
  54.3 1.0 collective-permute-start.7
  55.3 1.2 collective-permute-start.8
  56.5 1.9 %collective-permute-done.22 = bf16[64,1536]{1,0:T(8,128)(2,1)S(1)} collective-permute-done((bf16[64,1536]{1,0:T(8,128)(2,1)S(1)}, bf16[64,1536]{1,0:T(8,128)(2,1)S(1)}, u32[]{:S(2)}, u32[]{:S(2)}) %collective-permute-start.22) | collective-permute-done | bytes 196640 | tf_op jit(solution)/shard_map/ppermute | solution.py:44
  58.4 1.0 collective-permute-done.23
  59.7 0.9 collective-permute-start.25
  60.7 2.5 %collective-permute-done.7 = bf16[64,1536]{1,0:T(8,128)(2,1)S(1)} collective-permute-done((bf16[64,1536]{1,0:T(8,128)(2,1)S(1)}, bf16[64,1536]{1,0:T(8,128)(2,1)S(1)}, u32[]{:S(2)}, u32[]{:S(2)}) %collective-permute-start.7) | collective-permute-done | bytes 196640 | tf_op jit(solution)/shard_map/ppermute | solution.py:44
  63.3 0.4 collective-permute-start.9
  63.7 3.6 %collective-permute-done.24 = bf16[64,1536]{1,0:T(8,128)(2,1)S(1)} collective-permute-done((bf16[64,1536]{1,0:T(8,128)(2,1)S(1)}, bf16[64,1536]{1,0:T(8,128)(2,1)S(1)}, u32[]{:S(2)}, u32[]{:S(2)}) %collective-permute-start.24) | collective-permute-done | bytes 196640 | tf_op jit(solution)/shard_map/ppermute | solution.py:44
  67.5 0.4 collective-permute-start.26
  68.2 4.8 %collective-permute-done.26 = bf16[64,1536]{1,0:T(8,128)(2,1)S(1)} collective-permute-done((bf16[64,1536]{1,0:T(8,128)(2,1)S(1)}, bf16[64,1536]{1,0:T(8,128)(2,1)S(1)}, u32[]{:S(2)}, u32[]{:S(2)}) %collective-permute-start.26) | collective-permute-done | bytes 196640 | tf_op jit(solution)/shard_map/ppermute | solution.py:50
  73.1 0.4 constant_dynamic-update-slice_fusion.7
  73.5 0.7 collective-permute-start.27
  74.5 1.6 %collective-permute-start.10 = (bf16[64,1536]{1,0:T(8,128)(2,1)S(1)}, bf16[64,1536]{1,0:T(8,128)(2,1)S(1)}, u32[]{:S(2)}, u32[]{:S(2)}) collective-permute-start(bf16[64,1536]{1,0:T(8,128)(2,1)S(1)} %get-tuple-element.29), channel_id=1, source_target_pairs={{32,0},{48,16},{0,32},{16,48},{96,64},{112,80},{64,96},{80,112},{1... | collective-permute-start | bytes 589832 | tf_op jit(solution)/shard_map/ppermute | solution.py:44
  76.1 1.3 collective-permute-start.11
  77.3 0.7 collective-permute-done.27
  78.1 0.7 collective-permute-start.29
  78.8 1.2 collective-permute-done.28
  80.2 1.6 %collective-permute-start.12 = (bf16[64,1536]{1,0:T(8,128)(2,1)S(1)}, bf16[64,1536]{1,0:T(8,128)(2,1)S(1)}, u32[]{:S(2)}, u32[]{:S(2)}) collective-permute-start(bf16[64,1536]{1,0:T(8,128)(2,1)S(1)} %collective-permute-done.10), channel_id=1, source_target_pairs={{224,0},{240,16},{64,32},{80,48},{32,64},{48,80},{128,96},{144,112... | collective-permute-start | bytes 589832 | tf_op jit(solution)/shard_map/ppermute | solution.py:44
  82.3 4.1 %collective-permute-done.29 = bf16[64,1536]{1,0:T(8,128)(2,1)S(1)} collective-permute-done((bf16[64,1536]{1,0:T(8,128)(2,1)S(1)}, bf16[64,1536]{1,0:T(8,128)(2,1)S(1)}, u32[]{:S(2)}, u32[]{:S(2)}) %collective-permute-start.29) | collective-permute-done | bytes 196640 | tf_op jit(solution)/shard_map/ppermute | solution.py:44
  86.4 0.5 collective-permute-done.30
  86.9 0.8 collective-permute-start.32
  87.8 2.8 %collective-permute-done.12 = bf16[64,1536]{1,0:T(8,128)(2,1)S(1)} collective-permute-done((bf16[64,1536]{1,0:T(8,128)(2,1)S(1)}, bf16[64,1536]{1,0:T(8,128)(2,1)S(1)}, u32[]{:S(2)}, u32[]{:S(2)}) %collective-permute-start.12) | collective-permute-done | bytes 196640 | tf_op jit(solution)/shard_map/ppermute | solution.py:44
  90.6 0.5 collective-permute-start.15
  91.2 1.4 %collective-permute-done.31 = bf16[64,1536]{1,0:T(8,128)(2,1)S(1)} collective-permute-done((bf16[64,1536]{1,0:T(8,128)(2,1)S(1)}, bf16[64,1536]{1,0:T(8,128)(2,1)S(1)}, u32[]{:S(2)}, u32[]{:S(2)}) %collective-permute-start.31) | collective-permute-done | bytes 196640 | tf_op jit(solution)/shard_map/ppermute | solution.py:44
  92.7 2.0 %collective-permute-start.33 = (bf16[64,768]{1,0:T(8,128)(2,1)S(1)}, bf16[64,768]{1,0:T(8,128)(2,1)S(1)}, u32[]{:S(2)}, u32[]{:S(2)}) collective-permute-start(bf16[64,768]{1,0:T(8,128)(2,1)S(1)} %slice.68), channel_id=1, source_target_pairs={{224,0},{240,16},{64,32},{80,48},{32,64},{48,80},{128,96},{144,112... | collective-permute-start | bytes 294920 | tf_op jit(solution)/shard_map/ppermute | solution.py:44
  94.6 0.5 collective-permute-done.32
  95.2 1.8 %collective-permute-done.14 = bf16[64,1536]{1,0:T(8,128)(2,1)S(1)} collective-permute-done((bf16[64,1536]{1,0:T(8,128)(2,1)S(1)}, bf16[64,1536]{1,0:T(8,128)(2,1)S(1)}, u32[]{:S(2)}, u32[]{:S(2)}) %collective-permute-start.14) | collective-permute-done | bytes 196640 | tf_op jit(solution)/shard_map/ppermute | solution.py:44
  97.1 1.8 %collective-permute-start.16 = (bf16[64,768]{1,0:T(8,128)(2,1)S(1)}, bf16[64,768]{1,0:T(8,128)(2,1)S(1)}, u32[]{:S(2)}, u32[]{:S(2)}) collective-permute-start(bf16[64,768]{1,0:T(8,128)(2,1)S(1)} %slice.64), channel_id=1, source_target_pairs={{224,0},{240,16},{64,32},{80,48},{32,64},{48,80},{128,96},{144,112... | collective-permute-start | bytes 294920 | tf_op jit(solution)/shard_map/ppermute | solution.py:44
  99.5 1.2 collective-permute-done.33
  100.8 1.4 %fusion.24 = f32[512,768]{1,0:T(8,128)S(1)} fusion(bf16[512,1536]{1,0:T(8,128)(2,1)S(1)} %constant_dynamic-update-slice_fusion.16, bf16[768,1536]{1,0:T(8,128)(2,1)S(1)} %copy-done), kind=kOutput, calls=%fused_computation.68 | convolution fusion | flops 1207959552 | bytes 5505024 | tf_op jit(solution)/shard_map/dot_general | solution.py:30
  102.2 1.1 collective-permute-done.16
  103.3 0.5 collective-permute-done.17
  103.7 1.4 %fusion.23 = f32[512,768]{1,0:T(8,128)S(1)} fusion(bf16[512,1536]{1,0:T(8,128)(2,1)S(1)} %constant_dynamic-update-slice_fusion.17, bf16[1536,768]{1,0:T(8,128)(2,1)S(1)} %copy-done.6), kind=kOutput, calls=%fused_computation.67 | convolution fusion | flops 1207959552 | bytes 5505024 | tf_op jit(solution)/shard_map/dot_general | solution.py:136
  105.3 8.4 %collective-permute-start.35 = (f32[256,1536]{1,0:T(8,128)S(1)}, f32[256,1536]{1,0:T(8,128)S(1)}, u32[]{:S(2)}, u32[]{:S(2)}) collective-permute-start(f32[256,1536]{1,0:T(8,128)S(1)} %pad_maximum_fusion), channel_id=1, source_target_pairs={{1,0},{0,1},{3,2},{2,3},{5,4},{4,5},{7,6},{6,7},{9,8},{8,9},{11,10... | collective-permute-start | bytes 4718600 | tf_op jit(solution)/shard_map/ppermute | solution.py:60
  113.8 3.0 %collective-permute-done.35 = f32[256,1536]{1,0:T(8,128)S(1)} collective-permute-done((f32[256,1536]{1,0:T(8,128)S(1)}, f32[256,1536]{1,0:T(8,128)S(1)}, u32[]{:S(2)}, u32[]{:S(2)}) %collective-permute-start.35) | collective-permute-done | bytes 1572896 | tf_op jit(solution)/shard_map/ppermute | solution.py:60
  116.8 1.0 fusion.2
  117.8 3.5 %all-to-all-start.1 = ((bf16[8,32,1536]{2,1,0:T(8,128)(2,1)}), bf16[8,32,1536]{2,1,0:T(8,128)(2,1)S(1)}, u32[]{:S(2)}, u32[]{:S(2)}) async-start(bf16[8,32,1536]{2,1,0:T(8,128)(2,1)} %bitcast.10), calls=%async_computation.1 | async-start | bytes 1572864 | tf_op jit(solution)/shard_map/all_to_all | solution.py:56
  121.4 4.6 %multiply_convert_fusion = bf16[1536,768]{1,0:T(8,128)(2,1)} fusion(bf16[512,1536]{1,0:T(8,128)(2,1)} %copy-done.3, bf16[256,1536]{1,0:T(8,128)(2,1)} %collective-permute-done, bf16[256,1536]{1,0:T(8,128)(2,1)} %bitcast.14), kind=kOutput, calls=%fused_computation | convolution fusion | flops 1211891712 | bytes 5505024 | tf_op jit(solution)/shard_map/dot_general | solution.py:24
  126.0 3.8 %multiply_convert_fusion.1 = bf16[768,1536]{1,0:T(8,128)(2,1)} fusion(bf16[512,1536]{1,0:T(8,128)(2,1)S(1)} %copy-done.2, bf16[256,1536]{1,0:T(8,128)(2,1)S(1)} %bitcast.15, bf16[256,1536]{1,0:T(8,128)(2,1)} %collective-permute-done), kind=kOutput, calls=%fused_computation.1 | convolution fusion | flops 1211891712 | bytes 5505024 | tf_op jit(solution)/shard_map/dot_general | solution.py:24
  129.8 5.7 %all-to-all-done.1 = bf16[8,32,1536]{2,1,0:T(8,128)(2,1)S(1)} async-done(((bf16[8,32,1536]{2,1,0:T(8,128)(2,1)}), bf16[8,32,1536]{2,1,0:T(8,128)(2,1)S(1)}, u32[]{:S(2)}, u32[]{:S(2)}) %all-to-all-start.1) | async-done | bytes 786464 | tf_op jit(solution)/shard_map/all_to_all | solution.py:56
  135.6 0.6 fusion.22
  (73 shorter events, 3.9 us)
Async XLA Ops:
  0.6 25.7 %copy-start = (bf16[768,1536]{1,0:T(8,128)(2,1)S(1)}, bf16[768,1536]{1,0:T(8,128)(2,1)}, u32[]{:S(2)}) copy-start(bf16[768,1536]{1,0:T(8,128)(2,1)} %param.5) | copy-start | bytes 7077892
  22.5 12.0 %copy-start.4 = (bf16[8,32,1536]{2,1,0:T(8,128)(2,1)}, bf16[8,32,1536]{2,1,0:T(8,128)(2,1)S(1)}, u32[]{:S(2)}) copy-start(bf16[8,32,1536]{2,1,0:T(8,128)(2,1)S(1)} %all_to_all.18) | copy-start | bytes 2359300
  22.5 3.9 %collective-permute-start = (bf16[256,1536]{1,0:T(8,128)(2,1)S(1)}, bf16[256,1536]{1,0:T(8,128)(2,1)}, u32[]{:S(2)}, u32[]{:S(2)}) collective-permute-start(bf16[256,1536]{1,0:T(8,128)(2,1)S(1)} %bitcast.11), channel_id=1, source_target_pairs={{1,0},{0,1},{3,2},{2,3},{5,4},{4,5},{7,6},{6,7},{9,8},{8,9},{11,10... | collective-permute-start | bytes 2359304 | tf_op jit(solution)/shard_map/ppermute | solution.py:60
  24.3 10.2 %copy-start.6 = (bf16[1536,768]{1,0:T(8,128)(2,1)S(1)}, bf16[1536,768]{1,0:T(8,128)(2,1)}, u32[]{:S(2)}) copy-start(bf16[1536,768]{1,0:T(8,128)(2,1)} %param.6) | copy-start | bytes 7077892
  28.8 10.4 %collective-permute-start.3 = (bf16[64,768]{1,0:T(8,128)(2,1)S(1)}, bf16[64,768]{1,0:T(8,128)(2,1)S(1)}, u32[]{:S(2)}, u32[]{:S(2)}) collective-permute-start(bf16[64,768]{1,0:T(8,128)(2,1)S(1)} %get-tuple-element.48), channel_id=1, source_target_pairs={{224,0},{240,16},{64,32},{80,48},{32,64},{48,80},{128,96},{144,112... | collective-permute-start | bytes 294920 | tf_op jit(solution)/shard_map/ppermute | solution.py:44
  34.5 4.8 %collective-permute-start.1 = (bf16[64,768]{1,0:T(8,128)(2,1)S(1)}, bf16[64,768]{1,0:T(8,128)(2,1)S(1)}, u32[]{:S(2)}, u32[]{:S(2)}) collective-permute-start(bf16[64,768]{1,0:T(8,128)(2,1)S(1)} %get-tuple-element.49), channel_id=1, source_target_pairs={{32,0},{48,16},{0,32},{16,48},{96,64},{112,80},{64,96},{80,112},{1... | collective-permute-start | bytes 294920 | tf_op jit(solution)/shard_map/ppermute | solution.py:44
  37.0 4.8 %collective-permute-start.20 = (bf16[64,768]{1,0:T(8,128)(2,1)S(1)}, bf16[64,768]{1,0:T(8,128)(2,1)S(1)}, u32[]{:S(2)}, u32[]{:S(2)}) collective-permute-start(bf16[64,768]{1,0:T(8,128)(2,1)S(1)} %get-tuple-element.46), channel_id=1, source_target_pairs={{224,0},{240,16},{64,32},{80,48},{32,64},{48,80},{128,96},{144,112... | collective-permute-start | bytes 294920 | tf_op jit(solution)/shard_map/ppermute | solution.py:44
  38.5 3.8 %collective-permute-start.18 = (bf16[64,768]{1,0:T(8,128)(2,1)S(1)}, bf16[64,768]{1,0:T(8,128)(2,1)S(1)}, u32[]{:S(2)}, u32[]{:S(2)}) collective-permute-start(bf16[64,768]{1,0:T(8,128)(2,1)S(1)} %get-tuple-element.47), channel_id=1, source_target_pairs={{32,0},{48,16},{0,32},{16,48},{96,64},{112,80},{64,96},{80,112},{1... | collective-permute-start | bytes 294920 | tf_op jit(solution)/shard_map/ppermute | solution.py:44
  39.3 6.2 %collective-permute-start.2 = (bf16[64,1536]{1,0:T(8,128)(2,1)S(1)}, bf16[64,1536]{1,0:T(8,128)(2,1)S(1)}, u32[]{:S(2)}, u32[]{:S(2)}) collective-permute-start(bf16[64,1536]{1,0:T(8,128)(2,1)S(1)} %get-tuple-element.45), channel_id=1, source_target_pairs={{224,0},{240,16},{64,32},{80,48},{32,64},{48,80},{128,96},{144,112... | collective-permute-start | bytes 589832 | tf_op jit(solution)/shard_map/ppermute | solution.py:44
  39.9 6.6 %collective-permute-start.4 = (bf16[64,1536]{1,0:T(8,128)(2,1)S(1)}, bf16[64,1536]{1,0:T(8,128)(2,1)S(1)}, u32[]{:S(2)}, u32[]{:S(2)}) collective-permute-start(bf16[64,1536]{1,0:T(8,128)(2,1)S(1)} %get-tuple-element.44), channel_id=1, source_target_pairs={{32,0},{48,16},{0,32},{16,48},{96,64},{112,80},{64,96},{80,112},{1... | collective-permute-start | bytes 589832 | tf_op jit(solution)/shard_map/ppermute | solution.py:44
  42.3 7.0 %collective-permute-start.19 = (bf16[64,1536]{1,0:T(8,128)(2,1)S(1)}, bf16[64,1536]{1,0:T(8,128)(2,1)S(1)}, u32[]{:S(2)}, u32[]{:S(2)}) collective-permute-start(bf16[64,1536]{1,0:T(8,128)(2,1)S(1)} %get-tuple-element.39), channel_id=1, source_target_pairs={{224,0},{240,16},{64,32},{80,48},{32,64},{48,80},{128,96},{144,112... | collective-permute-start | bytes 589832 | tf_op jit(solution)/shard_map/ppermute | solution.py:44
  43.4 6.6 %collective-permute-start.21 = (bf16[64,1536]{1,0:T(8,128)(2,1)S(1)}, bf16[64,1536]{1,0:T(8,128)(2,1)S(1)}, u32[]{:S(2)}, u32[]{:S(2)}) collective-permute-start(bf16[64,1536]{1,0:T(8,128)(2,1)S(1)} %get-tuple-element.38), channel_id=1, source_target_pairs={{32,0},{48,16},{0,32},{16,48},{96,64},{112,80},{64,96},{80,112},{1... | collective-permute-start | bytes 589832 | tf_op jit(solution)/shard_map/ppermute | solution.py:44
  46.6 7.6 %collective-permute-start.5 = (bf16[64,1536]{1,0:T(8,128)(2,1)S(1)}, bf16[64,1536]{1,0:T(8,128)(2,1)S(1)}, u32[]{:S(2)}, u32[]{:S(2)}) collective-permute-start(bf16[64,1536]{1,0:T(8,128)(2,1)S(1)} %get-tuple-element.43), channel_id=1, source_target_pairs={{32,0},{48,16},{0,32},{16,48},{96,64},{112,80},{64,96},{80,112},{1... | collective-permute-start | bytes 589832 | tf_op jit(solution)/shard_map/ppermute | solution.py:44
  47.8 6.4 %collective-permute-start.6 = (bf16[64,1536]{1,0:T(8,128)(2,1)S(1)}, bf16[64,1536]{1,0:T(8,128)(2,1)S(1)}, u32[]{:S(2)}, u32[]{:S(2)}) collective-permute-start(bf16[64,1536]{1,0:T(8,128)(2,1)S(1)} %get-tuple-element.42), channel_id=1, source_target_pairs={{224,0},{240,16},{64,32},{80,48},{32,64},{48,80},{128,96},{144,112... | collective-permute-start | bytes 589832 | tf_op jit(solution)/shard_map/ppermute | solution.py:44
  50.1 8.3 %collective-permute-start.22 = (bf16[64,1536]{1,0:T(8,128)(2,1)S(1)}, bf16[64,1536]{1,0:T(8,128)(2,1)S(1)}, u32[]{:S(2)}, u32[]{:S(2)}) collective-permute-start(bf16[64,1536]{1,0:T(8,128)(2,1)S(1)} %get-tuple-element.37), channel_id=1, source_target_pairs={{32,0},{48,16},{0,32},{16,48},{96,64},{112,80},{64,96},{80,112},{1... | collective-permute-start | bytes 589832 | tf_op jit(solution)/shard_map/ppermute | solution.py:44
  51.5 7.8 %collective-permute-start.23 = (bf16[64,1536]{1,0:T(8,128)(2,1)S(1)}, bf16[64,1536]{1,0:T(8,128)(2,1)S(1)}, u32[]{:S(2)}, u32[]{:S(2)}) collective-permute-start(bf16[64,1536]{1,0:T(8,128)(2,1)S(1)} %get-tuple-element.36), channel_id=1, source_target_pairs={{224,0},{240,16},{64,32},{80,48},{32,64},{48,80},{128,96},{144,112... | collective-permute-start | bytes 589832 | tf_op jit(solution)/shard_map/ppermute | solution.py:44
  54.3 8.9 %collective-permute-start.7 = (bf16[64,1536]{1,0:T(8,128)(2,1)S(1)}, bf16[64,1536]{1,0:T(8,128)(2,1)S(1)}, u32[]{:S(2)}, u32[]{:S(2)}) collective-permute-start(bf16[64,1536]{1,0:T(8,128)(2,1)S(1)} %get-tuple-element.41), channel_id=1, source_target_pairs={{224,0},{240,16},{64,32},{80,48},{32,64},{48,80},{128,96},{144,112... | collective-permute-start | bytes 589832 | tf_op jit(solution)/shard_map/ppermute | solution.py:44
  55.3 7.9 %collective-permute-start.8 = (bf16[64,1536]{1,0:T(8,128)(2,1)S(1)}, bf16[64,1536]{1,0:T(8,128)(2,1)S(1)}, u32[]{:S(2)}, u32[]{:S(2)}) collective-permute-start(bf16[64,1536]{1,0:T(8,128)(2,1)S(1)} %get-tuple-element.40), channel_id=1, source_target_pairs={{32,0},{48,16},{0,32},{16,48},{96,64},{112,80},{64,96},{80,112},{1... | collective-permute-start | bytes 589832 | tf_op jit(solution)/shard_map/ppermute | solution.py:44
  59.5 7.9 %collective-permute-start.24 = (bf16[64,1536]{1,0:T(8,128)(2,1)S(1)}, bf16[64,1536]{1,0:T(8,128)(2,1)S(1)}, u32[]{:S(2)}, u32[]{:S(2)}) collective-permute-start(bf16[64,1536]{1,0:T(8,128)(2,1)S(1)} %get-tuple-element.35), channel_id=1, source_target_pairs={{224,0},{240,16},{64,32},{80,48},{32,64},{48,80},{128,96},{144,112... | collective-permute-start | bytes 589832 | tf_op jit(solution)/shard_map/ppermute | solution.py:44
  59.7 7.6 %collective-permute-start.25 = (bf16[64,1536]{1,0:T(8,128)(2,1)S(1)}, bf16[64,1536]{1,0:T(8,128)(2,1)S(1)}, u32[]{:S(2)}, u32[]{:S(2)}) collective-permute-start(bf16[64,1536]{1,0:T(8,128)(2,1)S(1)} %get-tuple-element.34), channel_id=1, source_target_pairs={{32,0},{48,16},{0,32},{16,48},{96,64},{112,80},{64,96},{80,112},{1... | collective-permute-start | bytes 589832 | tf_op jit(solution)/shard_map/ppermute | solution.py:44
  63.3 4.9 %collective-permute-start.9 = (bf16[64,1536]{1,0:T(8,128)(2,1)S(1)}, bf16[64,1536]{1,0:T(8,128)(2,1)S(1)}, u32[]{:S(2)}, u32[]{:S(2)}) collective-permute-start(bf16[64,1536]{1,0:T(8,128)(2,1)S(1)} %get-tuple-element.32), channel_id=1, source_target_pairs={{16,0},{0,16},{48,32},{32,48},{80,64},{64,80},{112,96},{96,112},{1... | collective-permute-start | bytes 589832 | tf_op jit(solution)/shard_map/ppermute | solution.py:50
  67.5 5.5 %collective-permute-start.26 = (bf16[64,1536]{1,0:T(8,128)(2,1)S(1)}, bf16[64,1536]{1,0:T(8,128)(2,1)S(1)}, u32[]{:S(2)}, u32[]{:S(2)}) collective-permute-start(bf16[64,1536]{1,0:T(8,128)(2,1)S(1)} %fusion.11), channel_id=1, source_target_pairs={{16,0},{0,16},{48,32},{32,48},{80,64},{64,80},{112,96},{96,112},{1... | collective-permute-start | bytes 589832 | tf_op jit(solution)/shard_map/ppermute | solution.py:50
  73.5 4.6 %collective-permute-start.27 = (bf16[64,1536]{1,0:T(8,128)(2,1)S(1)}, bf16[64,1536]{1,0:T(8,128)(2,1)S(1)}, u32[]{:S(2)}, u32[]{:S(2)}) collective-permute-start(bf16[64,1536]{1,0:T(8,128)(2,1)S(1)} %get-tuple-element.31), channel_id=1, source_target_pairs={{32,0},{48,16},{0,32},{16,48},{96,64},{112,80},{64,96},{80,112},{1... | collective-permute-start | bytes 589832 | tf_op jit(solution)/shard_map/ppermute | solution.py:44
  74.2 5.7 %collective-permute-start.28 = (bf16[64,1536]{1,0:T(8,128)(2,1)S(1)}, bf16[64,1536]{1,0:T(8,128)(2,1)S(1)}, u32[]{:S(2)}, u32[]{:S(2)}) collective-permute-start(bf16[64,1536]{1,0:T(8,128)(2,1)S(1)} %get-tuple-element.31), channel_id=1, source_target_pairs={{224,0},{240,16},{64,32},{80,48},{32,64},{48,80},{128,96},{144,112... | collective-permute-start | bytes 589832 | tf_op jit(solution)/shard_map/ppermute | solution.py:44
  74.5 5.7 %collective-permute-start.10 = (bf16[64,1536]{1,0:T(8,128)(2,1)S(1)}, bf16[64,1536]{1,0:T(8,128)(2,1)S(1)}, u32[]{:S(2)}, u32[]{:S(2)}) collective-permute-start(bf16[64,1536]{1,0:T(8,128)(2,1)S(1)} %get-tuple-element.29), channel_id=1, source_target_pairs={{32,0},{48,16},{0,32},{16,48},{96,64},{112,80},{64,96},{80,112},{1... | collective-permute-start | bytes 589832 | tf_op jit(solution)/shard_map/ppermute | solution.py:44
  76.1 6.0 %collective-permute-start.11 = (bf16[64,1536]{1,0:T(8,128)(2,1)S(1)}, bf16[64,1536]{1,0:T(8,128)(2,1)S(1)}, u32[]{:S(2)}, u32[]{:S(2)}) collective-permute-start(bf16[64,1536]{1,0:T(8,128)(2,1)S(1)} %get-tuple-element.29), channel_id=1, source_target_pairs={{224,0},{240,16},{64,32},{80,48},{32,64},{48,80},{128,96},{144,112... | collective-permute-start | bytes 589832 | tf_op jit(solution)/shard_map/ppermute | solution.py:44
  78.1 8.3 %collective-permute-start.29 = (bf16[64,1536]{1,0:T(8,128)(2,1)S(1)}, bf16[64,1536]{1,0:T(8,128)(2,1)S(1)}, u32[]{:S(2)}, u32[]{:S(2)}) collective-permute-start(bf16[64,1536]{1,0:T(8,128)(2,1)S(1)} %collective-permute-done.27), channel_id=1, source_target_pairs={{224,0},{240,16},{64,32},{80,48},{32,64},{48,80},{128,96},{144,112... | collective-permute-start | bytes 589832 | tf_op jit(solution)/shard_map/ppermute | solution.py:44
  79.9 7.0 %collective-permute-start.30 = (bf16[64,1536]{1,0:T(8,128)(2,1)S(1)}, bf16[64,1536]{1,0:T(8,128)(2,1)S(1)}, u32[]{:S(2)}, u32[]{:S(2)}) collective-permute-start(bf16[64,1536]{1,0:T(8,128)(2,1)S(1)} %collective-permute-done.28), channel_id=1, source_target_pairs={{32,0},{48,16},{0,32},{16,48},{96,64},{112,80},{64,96},{80,112},{1... | collective-permute-start | bytes 589832 | tf_op jit(solution)/shard_map/ppermute | solution.py:44
  80.2 10.4 %collective-permute-start.12 = (bf16[64,1536]{1,0:T(8,128)(2,1)S(1)}, bf16[64,1536]{1,0:T(8,128)(2,1)S(1)}, u32[]{:S(2)}, u32[]{:S(2)}) collective-permute-start(bf16[64,1536]{1,0:T(8,128)(2,1)S(1)} %collective-permute-done.10), channel_id=1, source_target_pairs={{224,0},{240,16},{64,32},{80,48},{32,64},{48,80},{128,96},{144,112... | collective-permute-start | bytes 589832 | tf_op jit(solution)/shard_map/ppermute | solution.py:44
  82.0 8.6 %collective-permute-start.13 = (bf16[64,1536]{1,0:T(8,128)(2,1)S(1)}, bf16[64,1536]{1,0:T(8,128)(2,1)S(1)}, u32[]{:S(2)}, u32[]{:S(2)}) collective-permute-start(bf16[64,1536]{1,0:T(8,128)(2,1)S(1)} %collective-permute-done.11), channel_id=1, source_target_pairs={{32,0},{48,16},{0,32},{16,48},{96,64},{112,80},{64,96},{80,112},{1... | collective-permute-start | bytes 589832 | tf_op jit(solution)/shard_map/ppermute | solution.py:44
  86.4 6.3 %collective-permute-start.31 = (bf16[64,1536]{1,0:T(8,128)(2,1)S(1)}, bf16[64,1536]{1,0:T(8,128)(2,1)S(1)}, u32[]{:S(2)}, u32[]{:S(2)}) collective-permute-start(bf16[64,1536]{1,0:T(8,128)(2,1)S(1)} %collective-permute-done.29), channel_id=1, source_target_pairs={{32,0},{48,16},{0,32},{16,48},{96,64},{112,80},{64,96},{80,112},{1... | collective-permute-start | bytes 589832 | tf_op jit(solution)/shard_map/ppermute | solution.py:44
  86.9 8.2 %collective-permute-start.32 = (bf16[64,1536]{1,0:T(8,128)(2,1)S(1)}, bf16[64,1536]{1,0:T(8,128)(2,1)S(1)}, u32[]{:S(2)}, u32[]{:S(2)}) collective-permute-start(bf16[64,1536]{1,0:T(8,128)(2,1)S(1)} %collective-permute-done.30), channel_id=1, source_target_pairs={{224,0},{240,16},{64,32},{80,48},{32,64},{48,80},{128,96},{144,112... | collective-permute-start | bytes 589832 | tf_op jit(solution)/shard_map/ppermute | solution.py:44
  90.6 6.5 %collective-permute-start.14 = (bf16[64,1536]{1,0:T(8,128)(2,1)S(1)}, bf16[64,1536]{1,0:T(8,128)(2,1)S(1)}, u32[]{:S(2)}, u32[]{:S(2)}) collective-permute-start(bf16[64,1536]{1,0:T(8,128)(2,1)S(1)} %collective-permute-done.12), channel_id=1, source_target_pairs={{32,0},{48,16},{0,32},{16,48},{96,64},{112,80},{64,96},{80,112},{1... | collective-permute-start | bytes 589832 | tf_op jit(solution)/shard_map/ppermute | solution.py:44
  90.6 8.4 %collective-permute-start.15 = (bf16[64,1536]{1,0:T(8,128)(2,1)S(1)}, bf16[64,1536]{1,0:T(8,128)(2,1)S(1)}, u32[]{:S(2)}, u32[]{:S(2)}) collective-permute-start(bf16[64,1536]{1,0:T(8,128)(2,1)S(1)} %collective-permute-done.13), channel_id=1, source_target_pairs={{224,0},{240,16},{64,32},{80,48},{32,64},{48,80},{128,96},{144,112... | collective-permute-start | bytes 589832 | tf_op jit(solution)/shard_map/ppermute | solution.py:44
  92.7 8.0 %collective-permute-start.33 = (bf16[64,768]{1,0:T(8,128)(2,1)S(1)}, bf16[64,768]{1,0:T(8,128)(2,1)S(1)}, u32[]{:S(2)}, u32[]{:S(2)}) collective-permute-start(bf16[64,768]{1,0:T(8,128)(2,1)S(1)} %slice.68), channel_id=1, source_target_pairs={{224,0},{240,16},{64,32},{80,48},{32,64},{48,80},{128,96},{144,112... | collective-permute-start | bytes 294920 | tf_op jit(solution)/shard_map/ppermute | solution.py:44
  95.1 5.6 %collective-permute-start.34 = (bf16[64,768]{1,0:T(8,128)(2,1)S(1)}, bf16[64,768]{1,0:T(8,128)(2,1)S(1)}, u32[]{:S(2)}, u32[]{:S(2)}) collective-permute-start(bf16[64,768]{1,0:T(8,128)(2,1)S(1)} %slice.69), channel_id=1, source_target_pairs={{32,0},{48,16},{0,32},{16,48},{96,64},{112,80},{64,96},{80,112},{1... | collective-permute-start | bytes 294920 | tf_op jit(solution)/shard_map/ppermute | solution.py:44
  97.1 6.2 %collective-permute-start.16 = (bf16[64,768]{1,0:T(8,128)(2,1)S(1)}, bf16[64,768]{1,0:T(8,128)(2,1)S(1)}, u32[]{:S(2)}, u32[]{:S(2)}) collective-permute-start(bf16[64,768]{1,0:T(8,128)(2,1)S(1)} %slice.64), channel_id=1, source_target_pairs={{224,0},{240,16},{64,32},{80,48},{32,64},{48,80},{128,96},{144,112... | collective-permute-start | bytes 294920 | tf_op jit(solution)/shard_map/ppermute | solution.py:44
  99.0 4.7 %collective-permute-start.17 = (bf16[64,768]{1,0:T(8,128)(2,1)S(1)}, bf16[64,768]{1,0:T(8,128)(2,1)S(1)}, u32[]{:S(2)}, u32[]{:S(2)}) collective-permute-start(bf16[64,768]{1,0:T(8,128)(2,1)S(1)} %slice.65), channel_id=1, source_target_pairs={{32,0},{48,16},{0,32},{16,48},{96,64},{112,80},{64,96},{80,112},{1... | collective-permute-start | bytes 294920 | tf_op jit(solution)/shard_map/ppermute | solution.py:44
  100.7 1.4 %copy-start.1 = (bf16[512,1536]{1,0:T(8,128)(2,1)}, bf16[512,1536]{1,0:T(8,128)(2,1)S(1)}, u32[]{:S(2)}) copy-start(bf16[512,1536]{1,0:T(8,128)(2,1)S(1)} %constant_dynamic-update-slice_fusion.16) | copy-start | bytes 4718596
  103.7 1.4 %copy-start.3 = (bf16[512,1536]{1,0:T(8,128)(2,1)}, bf16[512,1536]{1,0:T(8,128)(2,1)S(1)}, u32[]{:S(2)}) copy-start(bf16[512,1536]{1,0:T(8,128)(2,1)S(1)} %constant_dynamic-update-slice_fusion.17) | copy-start | bytes 4718596
  105.3 11.5 %collective-permute-start.35 = (f32[256,1536]{1,0:T(8,128)S(1)}, f32[256,1536]{1,0:T(8,128)S(1)}, u32[]{:S(2)}, u32[]{:S(2)}) collective-permute-start(f32[256,1536]{1,0:T(8,128)S(1)} %pad_maximum_fusion), channel_id=1, source_target_pairs={{1,0},{0,1},{3,2},{2,3},{5,4},{4,5},{7,6},{6,7},{9,8},{8,9},{11,10... | collective-permute-start | bytes 4718600 | tf_op jit(solution)/shard_map/ppermute | solution.py:60
  117.8 17.6 %all-to-all-start.1 = ((bf16[8,32,1536]{2,1,0:T(8,128)(2,1)}), bf16[8,32,1536]{2,1,0:T(8,128)(2,1)S(1)}, u32[]{:S(2)}, u32[]{:S(2)}) async-start(bf16[8,32,1536]{2,1,0:T(8,128)(2,1)} %bitcast.10), calls=%async_computation.1 | async-start | bytes 1572864 | tf_op jit(solution)/shard_map/all_to_all | solution.py:56
  121.4 4.6 %copy-start.2 = (bf16[512,1536]{1,0:T(8,128)(2,1)S(1)}, bf16[512,1536]{1,0:T(8,128)(2,1)}, u32[]{:S(2)}) copy-start(bf16[512,1536]{1,0:T(8,128)(2,1)} %copy-done.1) | copy-start | bytes 4718596
  121.4 4.6 %copy-start.5 = (bf16[8,32,1536]{2,1,0:T(8,128)(2,1)S(1)}, bf16[8,32,1536]{2,1,0:T(8,128)(2,1)}, u32[]{:S(2)}) copy-start(bf16[8,32,1536]{2,1,0:T(8,128)(2,1)} %copy-done.4) | copy-start | bytes 2359300
where the time goes:
time: 137 us; the launch traced here: 136 us
  waiting for transfers between devices  49.5 us (36%)
  starting transfers between devices  44.2 us (32%)
  blocking collectives  20.8 us (15%)
  matrix products  16 us (12%)
  other arithmetic  3.42 us (2%)
    ppermute x32, waiting for transfers between devices, swap_z(): lax.ppermute(x, 'row', [(pairs(z, Z) * XL + k, z * XL + k) for z in range...  33.7 us
    ppermute x32, starting transfers between devices, swap_z(): lax.ppermute(x, 'row', [(pairs(z, Z) * XL + k, z * XL + k) for z in range...  29.5 us
    all_to_all x1, blocking collectives, exchange_col(): return lax.all_to_all(x, 'col', 0, 0, axis_index_groups=groups, tiled=True)  20.8 us
    ppermute x2, starting transfers between devices, swap_core(): return lax.ppermute(x, 'col', [(i ^ 1, i) for i in range(Y * XH * CORE)])  10.3 us
    dot_general x2, matrix products, contract_rows(): lax.dot_general(left, right, (((0,), (0,)), ((), ())), preferred_element_...  8.39 us
    all_to_all x1, waiting for transfers between devices, exchange_col(): return lax.all_to_all(x, 'col', 0, 0, axis_index_groups=groups, tiled=True)  5.66 us
    ppermute x2, waiting for transfers between devices, swap_xl(): return lax.ppermute(x, 'row', [(i ^ 1, i) for i in range(Z * XL)])  5.09 us
    ppermute x2, waiting for transfers between devices, swap_core(): return lax.ppermute(x, 'col', [(i ^ 1, i) for i in range(Y * XH * CORE)])  5.08 us
  transfers between devices with their start and end apart: 37, of which 30 were waited for; matrix products, arithmetic and copies ran while one was open for 10% of the time, Pallas kernels for 0%

commit v1 on v0

--- a/solution.py
+++ b/solution.py
@@ -67,10 +67,13 @@
     return jnp.concatenate([x, swap_core(x)], axis=0)
 
 
+def add_core(x):
+    n = x.shape[0] // 2
+    return (x[:n] + swap_core(x[n:])).astype(bf16)
+
+
 def scatter_col(x):
-    n = x.shape[0] // 2
-    x = x[:n] + swap_core(x[n:])
-    x = exchange_col(x.astype(bf16)).astype(f32)
+    x = exchange_col(x).astype(f32)
     return jnp.sum(x.reshape(Y * XH, -1, x.shape[1]), axis=0).astype(bf16)
 
 
@@ -133,8 +136,8 @@
     activ, slope = gelu_parts(hidden)
     act_panel = gather_row(activ.astype(bf16))
     dh_panel = gather_row((act_grad * slope).astype(bf16))
-    output = jnp.dot(act_panel, down_weight, preferred_element_type=f32)
-    token_grad = contract_cols(dh_panel, up_weight)
+    output = add_core(jnp.dot(act_panel, down_weight, preferred_element_type=f32))
+    token_grad = add_core(contract_cols(dh_panel, up_weight))
     both = scatter_col(jnp.concatenate([output, token_grad], axis=1))
     down_grad = (contract_rows(act_panel, grad_panel) * scale).astype(bf16)
     up_grad = (contract_rows(token_panel, dh_panel) * scale).astype(bf16)

time: 137 us -> 135 us (0.985)
  waiting for transfers between devices: 49.5 us -> 47 us
    ppermute x2 -> x3, waiting for transfers between devices: 5.08 us -> 3.84 us  [swap_core(): return lax.ppermute(x, 'col', [(i ^ 1, i) for i in range(Y * XH * CORE)])]
    ppermute x2 -> x3, starting transfers between devices: 10.3 us -> 11.3 us  [swap_core(): return lax.ppermute(x, 'col', [(i ^ 1, i) for i in range(Y * XH * CORE)])]
  transfers between devices with their start and end apart: 37 -> 38, of which waited for: 30 -> 28; matrix products, arithmetic and copies ran while one was open for 10% -> 11% of each run, Pallas kernels for 0% -> 0%
where the time goes in v1:
time: 135 us
  waiting for transfers between devices  47 us (35%)
  starting transfers between devices  45 us (33%)
  blocking collectives  20.8 us (15%)
  matrix products  16 us (12%)
  other arithmetic  3.37 us (2%)
  local copies, waits for them, and re-layouts  1.45 us (1%)
    ppermute x32, waiting for transfers between devices, swap_z(): lax.ppermute(x, 'row', [(pairs(z, Z) * XL + k, z * XL + k) for z in range...  32.4 us
    ppermute x32, starting transfers between devices, swap_z(): lax.ppermute(x, 'row', [(pairs(z, Z) * XL + k, z * XL + k) for z in range...  29.3 us
    all_to_all x1, blocking collectives, exchange_col(): return lax.all_to_all(x, 'col', 0, 0, axis_index_groups=groups, tiled=True)  20.8 us
    ppermute x3, starting transfers between devices, swap_core(): return lax.ppermute(x, 'col', [(i ^ 1, i) for i in range(Y * XH * CORE)])  11.3 us
    dot_general x2, matrix products, contract_rows(): lax.dot_general(left, right, (((0,), (0,)), ((), ())), preferred_element_...  8.39 us
    all_to_all x1, waiting for transfers between devices, exchange_col(): return lax.all_to_all(x, 'col', 0, 0, axis_index_groups=groups, tiled=True)  5.67 us
    ppermute x2, waiting for transfers between devices, swap_xl(): return lax.ppermute(x, 'row', [(i ^ 1, i) for i in range(Z * XL)])  5.09 us
    ppermute x3, waiting for transfers between devices, swap_core(): return lax.ppermute(x, 'col', [(i ^ 1, i) for i in range(Y * XH * CORE)])  3.84 us
  transfers between devices with their start and end apart: 38, of which 28 were waited for; matrix products, arithmetic and copies ran while one was open for 11% of the time, Pallas kernels for 0%

profile of v1, /device:TPU:1, one launch (start us, length us, event | category | flops | bytes accessed | tf_op | source)
XLA Modules:
  0.0 134.6 jit_solution(7573505093918882648)
XLA Ops:
  0.6 1.0 pad_maximum_fusion.4
  1.7 20.8 %all_to_all.18 = bf16[8,32,1536]{2,1,0:T(8,128)(2,1)S(1)} all-to-all(bf16[8,32,1536]{2,1,0:T(8,128)(2,1)S(1)} %broadcast_in_dim.2), channel_id=1, replica_groups={{0,2,4,6,8,10,12,14},{1,3,5,7,9,11,13,15},{16,18,20,22,24,26,28,30},{17..., dimensions={0} | all-to-all | bytes 1572864 | tf_op jit(solution)/shard_map/all_to_all | solution.py:56
  22.5 1.9 %collective-permute-start = (bf16[256,1536]{1,0:T(8,128)(2,1)S(1)}, bf16[256,1536]{1,0:T(8,128)(2,1)}, u32[]{:S(2)}, u32[]{:S(2)}) collective-permute-start(bf16[256,1536]{1,0:T(8,128)(2,1)S(1)} %bitcast.11), channel_id=1, source_target_pairs={{1,0},{0,1},{3,2},{2,3},{5,4},{4,5},{7,6},{6,7},{9,8},{8,9},{11,10... | collective-permute-start | bytes 2359304 | tf_op jit(solution)/shard_map/ppermute | solution.py:60
  24.3 2.0 %collective-permute-done = bf16[256,1536]{1,0:T(8,128)(2,1)} collective-permute-done((bf16[256,1536]{1,0:T(8,128)(2,1)S(1)}, bf16[256,1536]{1,0:T(8,128)(2,1)}, u32[]{:S(2)}, u32[]{:S(2)}) %collective-permute-start) | collective-permute-done | bytes 786464 | tf_op jit(solution)/shard_map/ppermute | solution.py:60
  26.4 2.4 %fusion.15 = f32[512,1536]{1,0:T(8,128)S(1)} fusion(bf16[768,1536]{1,0:T(8,128)(2,1)S(1)} %copy-done, bf16[256,1536]{1,0:T(8,128)(2,1)S(1)} %bitcast.12, bf16[256,1536]{1,0:T(8,128)(2,1)} %collective-permute-done), kind=kOutput, calls=%fused_computation.61 | convolution fusion | flops 1209532416 | bytes 7077888 | tf_op jit(solution)/shard_map/dot_general | solution.py:134
  28.8 5.7 %collective-permute-start.3 = (bf16[64,768]{1,0:T(8,128)(2,1)S(1)}, bf16[64,768]{1,0:T(8,128)(2,1)S(1)}, u32[]{:S(2)}, u32[]{:S(2)}) collective-permute-start(bf16[64,768]{1,0:T(8,128)(2,1)S(1)} %get-tuple-element.48), channel_id=1, source_target_pairs={{224,0},{240,16},{64,32},{80,48},{32,64},{48,80},{128,96},{144,112... | collective-permute-start | bytes 294920 | tf_op jit(solution)/shard_map/ppermute | solution.py:44
  34.5 2.4 %fusion.11 = f32[512,1536]{1,0:T(8,128)S(1)} fusion(bf16[1536,768]{1,0:T(8,128)(2,1)S(1)} %copy-done.6, bf16[256,1536]{1,0:T(8,128)(2,1)} %collective-permute-done, bf16[256,1536]{1,0:T(8,128)(2,1)S(1)} %bitcast.13), kind=kOutput, calls=%fused_computation.39 | convolution fusion | flops 1209532416 | bytes 7077888 | tf_op jit(solution)/shard_map/dot_general | solution.py:30
  37.0 1.5 %collective-permute-start.21 = (bf16[64,768]{1,0:T(8,128)(2,1)S(1)}, bf16[64,768]{1,0:T(8,128)(2,1)S(1)}, u32[]{:S(2)}, u32[]{:S(2)}) collective-permute-start(bf16[64,768]{1,0:T(8,128)(2,1)S(1)} %get-tuple-element.46), channel_id=1, source_target_pairs={{224,0},{240,16},{64,32},{80,48},{32,64},{48,80},{128,96},{144,112... | collective-permute-start | bytes 294920 | tf_op jit(solution)/shard_map/ppermute | solution.py:44
  38.5 0.7 collective-permute-start.19
  39.3 0.6 collective-permute-start.2
  39.9 1.0 collective-permute-start.4
  40.9 0.9 collective-permute-done.21
  41.7 0.5 collective-permute-done.19
  42.3 1.0 collective-permute-start.20
  43.4 0.5 collective-permute-start.22
  43.9 1.6 %collective-permute-done.2 = bf16[64,1536]{1,0:T(8,128)(2,1)S(1)} collective-permute-done((bf16[64,1536]{1,0:T(8,128)(2,1)S(1)}, bf16[64,1536]{1,0:T(8,128)(2,1)S(1)}, u32[]{:S(2)}, u32[]{:S(2)}) %collective-permute-start.2) | collective-permute-done | bytes 196640 | tf_op jit(solution)/shard_map/ppermute | solution.py:44
  45.5 1.0 collective-permute-done.4
  46.6 1.1 collective-permute-start.5
  47.8 0.5 collective-permute-start.6
  48.3 1.0 collective-permute-done.20
  49.3 0.7 collective-permute-done.22
  50.1 1.5 %collective-permute-start.23 = (bf16[64,1536]{1,0:T(8,128)(2,1)S(1)}, bf16[64,1536]{1,0:T(8,128)(2,1)S(1)}, u32[]{:S(2)}, u32[]{:S(2)}) collective-permute-start(bf16[64,1536]{1,0:T(8,128)(2,1)S(1)} %get-tuple-element.37), channel_id=1, source_target_pairs={{32,0},{48,16},{0,32},{16,48},{96,64},{112,80},{64,96},{80,112},{1... | collective-permute-start | bytes 589832 | tf_op jit(solution)/shard_map/ppermute | solution.py:44
  51.7 2.4 %collective-permute-done.5 = bf16[64,1536]{1,0:T(8,128)(2,1)S(1)} collective-permute-done((bf16[64,1536]{1,0:T(8,128)(2,1)S(1)}, bf16[64,1536]{1,0:T(8,128)(2,1)S(1)}, u32[]{:S(2)}, u32[]{:S(2)}) %collective-permute-start.5) | collective-permute-done | bytes 196640 | tf_op jit(solution)/shard_map/ppermute | solution.py:44
  54.3 1.0 collective-permute-start.7
  55.3 1.2 collective-permute-start.8
  56.5 1.9 %collective-permute-done.23 = bf16[64,1536]{1,0:T(8,128)(2,1)S(1)} collective-permute-done((bf16[64,1536]{1,0:T(8,128)(2,1)S(1)}, bf16[64,1536]{1,0:T(8,128)(2,1)S(1)}, u32[]{:S(2)}, u32[]{:S(2)}) %collective-permute-start.23) | collective-permute-done | bytes 196640 | tf_op jit(solution)/shard_map/ppermute | solution.py:44
  58.4 1.0 collective-permute-done.24
  59.7 0.9 collective-permute-start.26
  60.7 2.5 %collective-permute-done.7 = bf16[64,1536]{1,0:T(8,128)(2,1)S(1)} collective-permute-done((bf16[64,1536]{1,0:T(8,128)(2,1)S(1)}, bf16[64,1536]{1,0:T(8,128)(2,1)S(1)}, u32[]{:S(2)}, u32[]{:S(2)}) %collective-permute-start.7) | collective-permute-done | bytes 196640 | tf_op jit(solution)/shard_map/ppermute | solution.py:44
  63.3 0.4 collective-permute-start.9
  63.7 3.6 %collective-permute-done.25 = bf16[64,1536]{1,0:T(8,128)(2,1)S(1)} collective-permute-done((bf16[64,1536]{1,0:T(8,128)(2,1)S(1)}, bf16[64,1536]{1,0:T(8,128)(2,1)S(1)}, u32[]{:S(2)}, u32[]{:S(2)}) %collective-permute-start.25) | collective-permute-done | bytes 196640 | tf_op jit(solution)/shard_map/ppermute | solution.py:44
  67.5 0.4 collective-permute-start.27
  67.9 0.3 collective-permute-done.9
  68.2 4.8 %collective-permute-done.27 = bf16[64,1536]{1,0:T(8,128)(2,1)S(1)} collective-permute-done((bf16[64,1536]{1,0:T(8,128)(2,1)S(1)}, bf16[64,1536]{1,0:T(8,128)(2,1)S(1)}, u32[]{:S(2)}, u32[]{:S(2)}) %collective-permute-start.27) | collective-permute-done | bytes 196640 | tf_op jit(solution)/shard_map/ppermute | solution.py:50
  73.1 0.4 constant_dynamic-update-slice_fusion.7
  73.5 0.7 collective-permute-start.28
  74.5 1.6 %collective-permute-start.10 = (bf16[64,1536]{1,0:T(8,128)(2,1)S(1)}, bf16[64,1536]{1,0:T(8,128)(2,1)S(1)}, u32[]{:S(2)}, u32[]{:S(2)}) collective-permute-start(bf16[64,1536]{1,0:T(8,128)(2,1)S(1)} %get-tuple-element.29), channel_id=1, source_target_pairs={{32,0},{48,16},{0,32},{16,48},{96,64},{112,80},{64,96},{80,112},{1... | collective-permute-start | bytes 589832 | tf_op jit(solution)/shard_map/ppermute | solution.py:44
  76.1 1.3 collective-permute-start.11
  77.3 0.7 collective-permute-done.28
  78.1 0.7 collective-permute-start.30
  78.8 1.2 collective-permute-done.29
  80.2 1.6 %collective-permute-start.12 = (bf16[64,1536]{1,0:T(8,128)(2,1)S(1)}, bf16[64,1536]{1,0:T(8,128)(2,1)S(1)}, u32[]{:S(2)}, u32[]{:S(2)}) collective-permute-start(bf16[64,1536]{1,0:T(8,128)(2,1)S(1)} %collective-permute-done.10), channel_id=1, source_target_pairs={{224,0},{240,16},{64,32},{80,48},{32,64},{48,80},{128,96},{144,112... | collective-permute-start | bytes 589832 | tf_op jit(solution)/shard_map/ppermute | solution.py:44
  82.3 4.1 %collective-permute-done.30 = bf16[64,1536]{1,0:T(8,128)(2,1)S(1)} collective-permute-done((bf16[64,1536]{1,0:T(8,128)(2,1)S(1)}, bf16[64,1536]{1,0:T(8,128)(2,1)S(1)}, u32[]{:S(2)}, u32[]{:S(2)}) %collective-permute-start.30) | collective-permute-done | bytes 196640 | tf_op jit(solution)/shard_map/ppermute | solution.py:44
  86.4 0.5 collective-permute-done.31
  86.9 0.8 collective-permute-start.33
  87.8 2.8 %collective-permute-done.12 = bf16[64,1536]{1,0:T(8,128)(2,1)S(1)} collective-permute-done((bf16[64,1536]{1,0:T(8,128)(2,1)S(1)}, bf16[64,1536]{1,0:T(8,128)(2,1)S(1)}, u32[]{:S(2)}, u32[]{:S(2)}) %collective-permute-start.12) | collective-permute-done | bytes 196640 | tf_op jit(solution)/shard_map/ppermute | solution.py:44
  90.6 0.5 collective-permute-start.15
  91.2 1.4 %collective-permute-done.32 = bf16[64,1536]{1,0:T(8,128)(2,1)S(1)} collective-permute-done((bf16[64,1536]{1,0:T(8,128)(2,1)S(1)}, bf16[64,1536]{1,0:T(8,128)(2,1)S(1)}, u32[]{:S(2)}, u32[]{:S(2)}) %collective-permute-start.32) | collective-permute-done | bytes 196640 | tf_op jit(solution)/shard_map/ppermute | solution.py:44
  92.7 2.0 %collective-permute-start.34 = (bf16[64,768]{1,0:T(8,128)(2,1)S(1)}, bf16[64,768]{1,0:T(8,128)(2,1)S(1)}, u32[]{:S(2)}, u32[]{:S(2)}) collective-permute-start(bf16[64,768]{1,0:T(8,128)(2,1)S(1)} %slice.78), channel_id=1, source_target_pairs={{224,0},{240,16},{64,32},{80,48},{32,64},{48,80},{128,96},{144,112... | collective-permute-start | bytes 294920 | tf_op jit(solution)/shard_map/ppermute | solution.py:44
  94.6 0.5 collective-permute-done.33
  95.2 1.8 %collective-permute-done.14 = bf16[64,1536]{1,0:T(8,128)(2,1)S(1)} collective-permute-done((bf16[64,1536]{1,0:T(8,128)(2,1)S(1)}, bf16[64,1536]{1,0:T(8,128)(2,1)S(1)}, u32[]{:S(2)}, u32[]{:S(2)}) %collective-permute-start.14) | collective-permute-done | bytes 196640 | tf_op jit(solution)/shard_map/ppermute | solution.py:44
  97.1 1.8 %collective-permute-start.16 = (bf16[64,768]{1,0:T(8,128)(2,1)S(1)}, bf16[64,768]{1,0:T(8,128)(2,1)S(1)}, u32[]{:S(2)}, u32[]{:S(2)}) collective-permute-start(bf16[64,768]{1,0:T(8,128)(2,1)S(1)} %slice.72), channel_id=1, source_target_pairs={{224,0},{240,16},{64,32},{80,48},{32,64},{48,80},{128,96},{144,112... | collective-permute-start | bytes 294920 | tf_op jit(solution)/shard_map/ppermute | solution.py:44
  99.3 1.4 %collective-permute-done.34 = bf16[64,768]{1,0:T(8,128)(2,1)S(1)} collective-permute-done((bf16[64,768]{1,0:T(8,128)(2,1)S(1)}, bf16[64,768]{1,0:T(8,128)(2,1)S(1)}, u32[]{:S(2)}, u32[]{:S(2)}) %collective-permute-start.34) | collective-permute-done | bytes 98336 | tf_op jit(solution)/shard_map/ppermute | solution.py:44
  100.8 1.4 %fusion.23 = f32[512,768]{1,0:T(8,128)S(1)} fusion(bf16[512,1536]{1,0:T(8,128)(2,1)S(1)} %constant_dynamic-update-slice_fusion.16, bf16[768,1536]{1,0:T(8,128)(2,1)S(1)} %copy-done), kind=kOutput, calls=%fused_computation.67 | convolution fusion | flops 1207959552 | bytes 5505024 | tf_op jit(solution)/shard_map/dot_general | solution.py:30
  102.2 8.1 %collective-permute-start.36 = (f32[256,768]{1,0:T(8,128)S(1)}, f32[256,768]{1,0:T(8,128)S(1)}, u32[]{:S(2)}, u32[]{:S(2)}) collective-permute-start(f32[256,768]{1,0:T(8,128)S(1)} %slice.81), channel_id=1, source_target_pairs={{1,0},{0,1},{3,2},{2,3},{5,4},{4,5},{7,6},{6,7},{9,8},{8,9},{11,10... | collective-permute-start | bytes 2359304 | tf_op jit(solution)/shard_map/ppermute | solution.py:60
  110.4 1.4 %fusion.22 = f32[512,768]{1,0:T(8,128)S(1)} fusion(bf16[512,1536]{1,0:T(8,128)(2,1)S(1)} %constant_dynamic-update-slice_fusion.17, bf16[1536,768]{1,0:T(8,128)(2,1)S(1)} %copy-done.6), kind=kOutput, calls=%fused_computation.66 | convolution fusion | flops 1207959552 | bytes 5505024 | tf_op jit(solution)/shard_map/dot_general | solution.py:139
  111.9 1.4 %collective-permute-start.18 = (f32[256,768]{1,0:T(8,128)S(1)}, f32[256,768]{1,0:T(8,128)S(1)}, u32[]{:S(2)}, u32[]{:S(2)}) collective-permute-start(f32[256,768]{1,0:T(8,128)S(1)} %slice.75), channel_id=1, source_target_pairs={{1,0},{0,1},{3,2},{2,3},{5,4},{4,5},{7,6},{6,7},{9,8},{8,9},{11,10... | collective-permute-start | bytes 2359304 | tf_op jit(solution)/shard_map/ppermute | solution.py:60
  113.3 1.8 %collective-permute-done.18 = f32[256,768]{1,0:T(8,128)S(1)} collective-permute-done((f32[256,768]{1,0:T(8,128)S(1)}, f32[256,768]{1,0:T(8,128)S(1)}, u32[]{:S(2)}, u32[]{:S(2)}) %collective-permute-start.18) | collective-permute-done | bytes 786464 | tf_op jit(solution)/shard_map/ppermute | solution.py:60
  115.2 0.9 pad_maximum_fusion.1
  116.2 3.5 %all-to-all-start.1 = ((bf16[8,32,1536]{2,1,0:T(8,128)(2,1)}), bf16[8,32,1536]{2,1,0:T(8,128)(2,1)S(1)}, u32[]{:S(2)}, u32[]{:S(2)}) async-start(bf16[8,32,1536]{2,1,0:T(8,128)(2,1)} %bitcast.10), calls=%async_computation.1 | async-start | bytes 1572864 | tf_op jit(solution)/shard_map/all_to_all | solution.py:56
  119.8 4.6 %multiply_convert_fusion = bf16[1536,768]{1,0:T(8,128)(2,1)} fusion(bf16[512,1536]{1,0:T(8,128)(2,1)} %copy-done.3, bf16[256,1536]{1,0:T(8,128)(2,1)} %collective-permute-done, bf16[256,1536]{1,0:T(8,128)(2,1)} %bitcast.14), kind=kOutput, calls=%fused_computation | convolution fusion | flops 1211891712 | bytes 5505024 | tf_op jit(solution)/shard_map/dot_general | solution.py:24
  124.3 3.8 %multiply_convert_fusion.1 = bf16[768,1536]{1,0:T(8,128)(2,1)} fusion(bf16[512,1536]{1,0:T(8,128)(2,1)S(1)} %copy-done.2, bf16[256,1536]{1,0:T(8,128)(2,1)S(1)} %bitcast.15, bf16[256,1536]{1,0:T(8,128)(2,1)} %collective-permute-done), kind=kOutput, calls=%fused_computation.1 | convolution fusion | flops 1211891712 | bytes 5505024 | tf_op jit(solution)/shard_map/dot_general | solution.py:24
  128.1 5.7 %all-to-all-done.1 = bf16[8,32,1536]{2,1,0:T(8,128)(2,1)S(1)} async-done(((bf16[8,32,1536]{2,1,0:T(8,128)(2,1)}), bf16[8,32,1536]{2,1,0:T(8,128)(2,1)S(1)}, u32[]{:S(2)}, u32[]{:S(2)}) %all-to-all-start.1) | async-done | bytes 786464 | tf_op jit(solution)/shard_map/all_to_all | solution.py:56
  133.9 0.6 fusion.21
  (78 shorter events, 3.5 us)
Async XLA Ops:
  0.6 25.7 %copy-start = (bf16[768,1536]{1,0:T(8,128)(2,1)S(1)}, bf16[768,1536]{1,0:T(8,128)(2,1)}, u32[]{:S(2)}) copy-start(bf16[768,1536]{1,0:T(8,128)(2,1)} %param.5) | copy-start | bytes 7077892
  22.5 12.0 %copy-start.4 = (bf16[8,32,1536]{2,1,0:T(8,128)(2,1)}, bf16[8,32,1536]{2,1,0:T(8,128)(2,1)S(1)}, u32[]{:S(2)}) copy-start(bf16[8,32,1536]{2,1,0:T(8,128)(2,1)S(1)} %all_to_all.18) | copy-start | bytes 2359300
  22.5 3.9 %collective-permute-start = (bf16[256,1536]{1,0:T(8,128)(2,1)S(1)}, bf16[256,1536]{1,0:T(8,128)(2,1)}, u32[]{:S(2)}, u32[]{:S(2)}) collective-permute-start(bf16[256,1536]{1,0:T(8,128)(2,1)S(1)} %bitcast.11), channel_id=1, source_target_pairs={{1,0},{0,1},{3,2},{2,3},{5,4},{4,5},{7,6},{6,7},{9,8},{8,9},{11,10... | collective-permute-start | bytes 2359304 | tf_op jit(solution)/shard_map/ppermute | solution.py:60
  24.3 10.2 %copy-start.6 = (bf16[1536,768]{1,0:T(8,128)(2,1)S(1)}, bf16[1536,768]{1,0:T(8,128)(2,1)}, u32[]{:S(2)}) copy-start(bf16[1536,768]{1,0:T(8,128)(2,1)} %param.6) | copy-start | bytes 7077892
  28.8 10.4 %collective-permute-start.3 = (bf16[64,768]{1,0:T(8,128)(2,1)S(1)}, bf16[64,768]{1,0:T(8,128)(2,1)S(1)}, u32[]{:S(2)}, u32[]{:S(2)}) collective-permute-start(bf16[64,768]{1,0:T(8,128)(2,1)S(1)} %get-tuple-element.48), channel_id=1, source_target_pairs={{224,0},{240,16},{64,32},{80,48},{32,64},{48,80},{128,96},{144,112... | collective-permute-start | bytes 294920 | tf_op jit(solution)/shard_map/ppermute | solution.py:44
  34.5 4.8 %collective-permute-start.1 = (bf16[64,768]{1,0:T(8,128)(2,1)S(1)}, bf16[64,768]{1,0:T(8,128)(2,1)S(1)}, u32[]{:S(2)}, u32[]{:S(2)}) collective-permute-start(bf16[64,768]{1,0:T(8,128)(2,1)S(1)} %get-tuple-element.49), channel_id=1, source_target_pairs={{32,0},{48,16},{0,32},{16,48},{96,64},{112,80},{64,96},{80,112},{1... | collective-permute-start | bytes 294920 | tf_op jit(solution)/shard_map/ppermute | solution.py:44
  37.0 4.8 %collective-permute-start.21 = (bf16[64,768]{1,0:T(8,128)(2,1)S(1)}, bf16[64,768]{1,0:T(8,128)(2,1)S(1)}, u32[]{:S(2)}, u32[]{:S(2)}) collective-permute-start(bf16[64,768]{1,0:T(8,128)(2,1)S(1)} %get-tuple-element.46), channel_id=1, source_target_pairs={{224,0},{240,16},{64,32},{80,48},{32,64},{48,80},{128,96},{144,112... | collective-permute-start | bytes 294920 | tf_op jit(solution)/shard_map/ppermute | solution.py:44
  38.5 3.8 %collective-permute-start.19 = (bf16[64,768]{1,0:T(8,128)(2,1)S(1)}, bf16[64,768]{1,0:T(8,128)(2,1)S(1)}, u32[]{:S(2)}, u32[]{:S(2)}) collective-permute-start(bf16[64,768]{1,0:T(8,128)(2,1)S(1)} %get-tuple-element.47), channel_id=1, source_target_pairs={{32,0},{48,16},{0,32},{16,48},{96,64},{112,80},{64,96},{80,112},{1... | collective-permute-start | bytes 294920 | tf_op jit(solution)/shard_map/ppermute | solution.py:44
  39.3 6.2 %collective-permute-start.2 = (bf16[64,1536]{1,0:T(8,128)(2,1)S(1)}, bf16[64,1536]{1,0:T(8,128)(2,1)S(1)}, u32[]{:S(2)}, u32[]{:S(2)}) collective-permute-start(bf16[64,1536]{1,0:T(8,128)(2,1)S(1)} %get-tuple-element.45), channel_id=1, source_target_pairs={{224,0},{240,16},{64,32},{80,48},{32,64},{48,80},{128,96},{144,112... | collective-permute-start | bytes 589832 | tf_op jit(solution)/shard_map/ppermute | solution.py:44
  39.9 6.6 %collective-permute-start.4 = (bf16[64,1536]{1,0:T(8,128)(2,1)S(1)}, bf16[64,1536]{1,0:T(8,128)(2,1)S(1)}, u32[]{:S(2)}, u32[]{:S(2)}) collective-permute-start(bf16[64,1536]{1,0:T(8,128)(2,1)S(1)} %get-tuple-element.44), channel_id=1, source_target_pairs={{32,0},{48,16},{0,32},{16,48},{96,64},{112,80},{64,96},{80,112},{1... | collective-permute-start | bytes 589832 | tf_op jit(solution)/shard_map/ppermute | solution.py:44
  42.3 7.0 %collective-permute-start.20 = (bf16[64,1536]{1,0:T(8,128)(2,1)S(1)}, bf16[64,1536]{1,0:T(8,128)(2,1)S(1)}, u32[]{:S(2)}, u32[]{:S(2)}) collective-permute-start(bf16[64,1536]{1,0:T(8,128)(2,1)S(1)} %get-tuple-element.39), channel_id=1, source_target_pairs={{224,0},{240,16},{64,32},{80,48},{32,64},{48,80},{128,96},{144,112... | collective-permute-start | bytes 589832 | tf_op jit(solution)/shard_map/ppermute | solution.py:44
  43.4 6.6 %collective-permute-start.22 = (bf16[64,1536]{1,0:T(8,128)(2,1)S(1)}, bf16[64,1536]{1,0:T(8,128)(2,1)S(1)}, u32[]{:S(2)}, u32[]{:S(2)}) collective-permute-start(bf16[64,1536]{1,0:T(8,128)(2,1)S(1)} %get-tuple-element.38), channel_id=1, source_target_pairs={{32,0},{48,16},{0,32},{16,48},{96,64},{112,80},{64,96},{80,112},{1... | collective-permute-start | bytes 589832 | tf_op jit(solution)/shard_map/ppermute | solution.py:44
  46.6 7.6 %collective-permute-start.5 = (bf16[64,1536]{1,0:T(8,128)(2,1)S(1)}, bf16[64,1536]{1,0:T(8,128)(2,1)S(1)}, u32[]{:S(2)}, u32[]{:S(2)}) collective-permute-start(bf16[64,1536]{1,0:T(8,128)(2,1)S(1)} %get-tuple-element.43), channel_id=1, source_target_pairs={{32,0},{48,16},{0,32},{16,48},{96,64},{112,80},{64,96},{80,112},{1... | collective-permute-start | bytes 589832 | tf_op jit(solution)/shard_map/ppermute | solution.py:44
  47.8 6.4 %collective-permute-start.6 = (bf16[64,1536]{1,0:T(8,128)(2,1)S(1)}, bf16[64,1536]{1,0:T(8,128)(2,1)S(1)}, u32[]{:S(2)}, u32[]{:S(2)}) collective-permute-start(bf16[64,1536]{1,0:T(8,128)(2,1)S(1)} %get-tuple-element.42), channel_id=1, source_target_pairs={{224,0},{240,16},{64,32},{80,48},{32,64},{48,80},{128,96},{144,112... | collective-permute-start | bytes 589832 | tf_op jit(solution)/shard_map/ppermute | solution.py:44
  50.1 8.3 %collective-permute-start.23 = (bf16[64,1536]{1,0:T(8,128)(2,1)S(1)}, bf16[64,1536]{1,0:T(8,128)(2,1)S(1)}, u32[]{:S(2)}, u32[]{:S(2)}) collective-permute-start(bf16[64,1536]{1,0:T(8,128)(2,1)S(1)} %get-tuple-element.37), channel_id=1, source_target_pairs={{32,0},{48,16},{0,32},{16,48},{96,64},{112,80},{64,96},{80,112},{1... | collective-permute-start | bytes 589832 | tf_op jit(solution)/shard_map/ppermute | solution.py:44
  51.5 7.8 %collective-permute-start.24 = (bf16[64,1536]{1,0:T(8,128)(2,1)S(1)}, bf16[64,1536]{1,0:T(8,128)(2,1)S(1)}, u32[]{:S(2)}, u32[]{:S(2)}) collective-permute-start(bf16[64,1536]{1,0:T(8,128)(2,1)S(1)} %get-tuple-element.36), channel_id=1, source_target_pairs={{224,0},{240,16},{64,32},{80,48},{32,64},{48,80},{128,96},{144,112... | collective-permute-start | bytes 589832 | tf_op jit(solution)/shard_map/ppermute | solution.py:44
  54.3 8.9 %collective-permute-start.7 = (bf16[64,1536]{1,0:T(8,128)(2,1)S(1)}, bf16[64,1536]{1,0:T(8,128)(2,1)S(1)}, u32[]{:S(2)}, u32[]{:S(2)}) collective-permute-start(bf16[64,1536]{1,0:T(8,128)(2,1)S(1)} %get-tuple-element.41), channel_id=1, source_target_pairs={{224,0},{240,16},{64,32},{80,48},{32,64},{48,80},{128,96},{144,112... | collective-permute-start | bytes 589832 | tf_op jit(solution)/shard_map/ppermute | solution.py:44
  55.3 7.9 %collective-permute-start.8 = (bf16[64,1536]{1,0:T(8,128)(2,1)S(1)}, bf16[64,1536]{1,0:T(8,128)(2,1)S(1)}, u32[]{:S(2)}, u32[]{:S(2)}) collective-permute-start(bf16[64,1536]{1,0:T(8,128)(2,1)S(1)} %get-tuple-element.40), channel_id=1, source_target_pairs={{32,0},{48,16},{0,32},{16,48},{96,64},{112,80},{64,96},{80,112},{1... | collective-permute-start | bytes 589832 | tf_op jit(solution)/shard_map/ppermute | solution.py:44
  59.5 7.9 %collective-permute-start.25 = (bf16[64,1536]{1,0:T(8,128)(2,1)S(1)}, bf16[64,1536]{1,0:T(8,128)(2,1)S(1)}, u32[]{:S(2)}, u32[]{:S(2)}) collective-permute-start(bf16[64,1536]{1,0:T(8,128)(2,1)S(1)} %get-tuple-element.35), channel_id=1, source_target_pairs={{224,0},{240,16},{64,32},{80,48},{32,64},{48,80},{128,96},{144,112... | collective-permute-start | bytes 589832 | tf_op jit(solution)/shard_map/ppermute | solution.py:44
  59.7 7.6 %collective-permute-start.26 = (bf16[64,1536]{1,0:T(8,128)(2,1)S(1)}, bf16[64,1536]{1,0:T(8,128)(2,1)S(1)}, u32[]{:S(2)}, u32[]{:S(2)}) collective-permute-start(bf16[64,1536]{1,0:T(8,128)(2,1)S(1)} %get-tuple-element.34), channel_id=1, source_target_pairs={{32,0},{48,16},{0,32},{16,48},{96,64},{112,80},{64,96},{80,112},{1... | collective-permute-start | bytes 589832 | tf_op jit(solution)/shard_map/ppermute | solution.py:44
  63.3 4.9 %collective-permute-start.9 = (bf16[64,1536]{1,0:T(8,128)(2,1)S(1)}, bf16[64,1536]{1,0:T(8,128)(2,1)S(1)}, u32[]{:S(2)}, u32[]{:S(2)}) collective-permute-start(bf16[64,1536]{1,0:T(8,128)(2,1)S(1)} %get-tuple-element.32), channel_id=1, source_target_pairs={{16,0},{0,16},{48,32},{32,48},{80,64},{64,80},{112,96},{96,112},{1... | collective-permute-start | bytes 589832 | tf_op jit(solution)/shard_map/ppermute | solution.py:50
  67.5 5.5 %collective-permute-start.27 = (bf16[64,1536]{1,0:T(8,128)(2,1)S(1)}, bf16[64,1536]{1,0:T(8,128)(2,1)S(1)}, u32[]{:S(2)}, u32[]{:S(2)}) collective-permute-start(bf16[64,1536]{1,0:T(8,128)(2,1)S(1)} %fusion.10), channel_id=1, source_target_pairs={{16,0},{0,16},{48,32},{32,48},{80,64},{64,80},{112,96},{96,112},{1... | collective-permute-start | bytes 589832 | tf_op jit(solution)/shard_map/ppermute | solution.py:50
  73.5 4.6 %collective-permute-start.28 = (bf16[64,1536]{1,0:T(8,128)(2,1)S(1)}, bf16[64,1536]{1,0:T(8,128)(2,1)S(1)}, u32[]{:S(2)}, u32[]{:S(2)}) collective-permute-start(bf16[64,1536]{1,0:T(8,128)(2,1)S(1)} %get-tuple-element.31), channel_id=1, source_target_pairs={{32,0},{48,16},{0,32},{16,48},{96,64},{112,80},{64,96},{80,112},{1... | collective-permute-start | bytes 589832 | tf_op jit(solution)/shard_map/ppermute | solution.py:44
  74.2 5.7 %collective-permute-start.29 = (bf16[64,1536]{1,0:T(8,128)(2,1)S(1)}, bf16[64,1536]{1,0:T(8,128)(2,1)S(1)}, u32[]{:S(2)}, u32[]{:S(2)}) collective-permute-start(bf16[64,1536]{1,0:T(8,128)(2,1)S(1)} %get-tuple-element.31), channel_id=1, source_target_pairs={{224,0},{240,16},{64,32},{80,48},{32,64},{48,80},{128,96},{144,112... | collective-permute-start | bytes 589832 | tf_op jit(solution)/shard_map/ppermute | solution.py:44
  74.5 5.7 %collective-permute-start.10 = (bf16[64,1536]{1,0:T(8,128)(2,1)S(1)}, bf16[64,1536]{1,0:T(8,128)(2,1)S(1)}, u32[]{:S(2)}, u32[]{:S(2)}) collective-permute-start(bf16[64,1536]{1,0:T(8,128)(2,1)S(1)} %get-tuple-element.29), channel_id=1, source_target_pairs={{32,0},{48,16},{0,32},{16,48},{96,64},{112,80},{64,96},{80,112},{1... | collective-permute-start | bytes 589832 | tf_op jit(solution)/shard_map/ppermute | solution.py:44
  76.1 6.0 %collective-permute-start.11 = (bf16[64,1536]{1,0:T(8,128)(2,1)S(1)}, bf16[64,1536]{1,0:T(8,128)(2,1)S(1)}, u32[]{:S(2)}, u32[]{:S(2)}) collective-permute-start(bf16[64,1536]{1,0:T(8,128)(2,1)S(1)} %get-tuple-element.29), channel_id=1, source_target_pairs={{224,0},{240,16},{64,32},{80,48},{32,64},{48,80},{128,96},{144,112... | collective-permute-start | bytes 589832 | tf_op jit(solution)/shard_map/ppermute | solution.py:44
  78.1 8.3 %collective-permute-start.30 = (bf16[64,1536]{1,0:T(8,128)(2,1)S(1)}, bf16[64,1536]{1,0:T(8,128)(2,1)S(1)}, u32[]{:S(2)}, u32[]{:S(2)}) collective-permute-start(bf16[64,1536]{1,0:T(8,128)(2,1)S(1)} %collective-permute-done.28), channel_id=1, source_target_pairs={{224,0},{240,16},{64,32},{80,48},{32,64},{48,80},{128,96},{144,112... | collective-permute-start | bytes 589832 | tf_op jit(solution)/shard_map/ppermute | solution.py:44
  79.9 7.0 %collective-permute-start.31 = (bf16[64,1536]{1,0:T(8,128)(2,1)S(1)}, bf16[64,1536]{1,0:T(8,128)(2,1)S(1)}, u32[]{:S(2)}, u32[]{:S(2)}) collective-permute-start(bf16[64,1536]{1,0:T(8,128)(2,1)S(1)} %collective-permute-done.29), channel_id=1, source_target_pairs={{32,0},{48,16},{0,32},{16,48},{96,64},{112,80},{64,96},{80,112},{1... | collective-permute-start | bytes 589832 | tf_op jit(solution)/shard_map/ppermute | solution.py:44
  80.2 10.4 %collective-permute-start.12 = (bf16[64,1536]{1,0:T(8,128)(2,1)S(1)}, bf16[64,1536]{1,0:T(8,128)(2,1)S(1)}, u32[]{:S(2)}, u32[]{:S(2)}) collective-permute-start(bf16[64,1536]{1,0:T(8,128)(2,1)S(1)} %collective-permute-done.10), channel_id=1, source_target_pairs={{224,0},{240,16},{64,32},{80,48},{32,64},{48,80},{128,96},{144,112... | collective-permute-start | bytes 589832 | tf_op jit(solution)/shard_map/ppermute | solution.py:44
  82.0 8.6 %collective-permute-start.13 = (bf16[64,1536]{1,0:T(8,128)(2,1)S(1)}, bf16[64,1536]{1,0:T(8,128)(2,1)S(1)}, u32[]{:S(2)}, u32[]{:S(2)}) collective-permute-start(bf16[64,1536]{1,0:T(8,128)(2,1)S(1)} %collective-permute-done.11), channel_id=1, source_target_pairs={{32,0},{48,16},{0,32},{16,48},{96,64},{112,80},{64,96},{80,112},{1... | collective-permute-start | bytes 589832 | tf_op jit(solution)/shard_map/ppermute | solution.py:44
  86.4 6.3 %collective-permute-start.32 = (bf16[64,1536]{1,0:T(8,128)(2,1)S(1)}, bf16[64,1536]{1,0:T(8,128)(2,1)S(1)}, u32[]{:S(2)}, u32[]{:S(2)}) collective-permute-start(bf16[64,1536]{1,0:T(8,128)(2,1)S(1)} %collective-permute-done.30), channel_id=1, source_target_pairs={{32,0},{48,16},{0,32},{16,48},{96,64},{112,80},{64,96},{80,112},{1... | collective-permute-start | bytes 589832 | tf_op jit(solution)/shard_map/ppermute | solution.py:44
  86.9 8.2 %collective-permute-start.33 = (bf16[64,1536]{1,0:T(8,128)(2,1)S(1)}, bf16[64,1536]{1,0:T(8,128)(2,1)S(1)}, u32[]{:S(2)}, u32[]{:S(2)}) collective-permute-start(bf16[64,1536]{1,0:T(8,128)(2,1)S(1)} %collective-permute-done.31), channel_id=1, source_target_pairs={{224,0},{240,16},{64,32},{80,48},{32,64},{48,80},{128,96},{144,112... | collective-permute-start | bytes 589832 | tf_op jit(solution)/shard_map/ppermute | solution.py:44
  90.6 6.5 %collective-permute-start.14 = (bf16[64,1536]{1,0:T(8,128)(2,1)S(1)}, bf16[64,1536]{1,0:T(8,128)(2,1)S(1)}, u32[]{:S(2)}, u32[]{:S(2)}) collective-permute-start(bf16[64,1536]{1,0:T(8,128)(2,1)S(1)} %collective-permute-done.12), channel_id=1, source_target_pairs={{32,0},{48,16},{0,32},{16,48},{96,64},{112,80},{64,96},{80,112},{1... | collective-permute-start | bytes 589832 | tf_op jit(solution)/shard_map/ppermute | solution.py:44
  90.6 8.4 %collective-permute-start.15 = (bf16[64,1536]{1,0:T(8,128)(2,1)S(1)}, bf16[64,1536]{1,0:T(8,128)(2,1)S(1)}, u32[]{:S(2)}, u32[]{:S(2)}) collective-permute-start(bf16[64,1536]{1,0:T(8,128)(2,1)S(1)} %collective-permute-done.13), channel_id=1, source_target_pairs={{224,0},{240,16},{64,32},{80,48},{32,64},{48,80},{128,96},{144,112... | collective-permute-start | bytes 589832 | tf_op jit(solution)/shard_map/ppermute | solution.py:44
  92.7 8.0 %collective-permute-start.34 = (bf16[64,768]{1,0:T(8,128)(2,1)S(1)}, bf16[64,768]{1,0:T(8,128)(2,1)S(1)}, u32[]{:S(2)}, u32[]{:S(2)}) collective-permute-start(bf16[64,768]{1,0:T(8,128)(2,1)S(1)} %slice.78), channel_id=1, source_target_pairs={{224,0},{240,16},{64,32},{80,48},{32,64},{48,80},{128,96},{144,112... | collective-permute-start | bytes 294920 | tf_op jit(solution)/shard_map/ppermute | solution.py:44
  95.1 5.6 %collective-permute-start.35 = (bf16[64,768]{1,0:T(8,128)(2,1)S(1)}, bf16[64,768]{1,0:T(8,128)(2,1)S(1)}, u32[]{:S(2)}, u32[]{:S(2)}) collective-permute-start(bf16[64,768]{1,0:T(8,128)(2,1)S(1)} %slice.79), channel_id=1, source_target_pairs={{32,0},{48,16},{0,32},{16,48},{96,64},{112,80},{64,96},{80,112},{1... | collective-permute-start | bytes 294920 | tf_op jit(solution)/shard_map/ppermute | solution.py:44
  97.1 13.3 %collective-permute-start.16 = (bf16[64,768]{1,0:T(8,128)(2,1)S(1)}, bf16[64,768]{1,0:T(8,128)(2,1)S(1)}, u32[]{:S(2)}, u32[]{:S(2)}) collective-permute-start(bf16[64,768]{1,0:T(8,128)(2,1)S(1)} %slice.72), channel_id=1, source_target_pairs={{224,0},{240,16},{64,32},{80,48},{32,64},{48,80},{128,96},{144,112... | collective-permute-start | bytes 294920 | tf_op jit(solution)/shard_map/ppermute | solution.py:44
  99.0 11.3 %collective-permute-start.17 = (bf16[64,768]{1,0:T(8,128)(2,1)S(1)}, bf16[64,768]{1,0:T(8,128)(2,1)S(1)}, u32[]{:S(2)}, u32[]{:S(2)}) collective-permute-start(bf16[64,768]{1,0:T(8,128)(2,1)S(1)} %slice.73), channel_id=1, source_target_pairs={{32,0},{48,16},{0,32},{16,48},{96,64},{112,80},{64,96},{80,112},{1... | collective-permute-start | bytes 294920 | tf_op jit(solution)/shard_map/ppermute | solution.py:44
  100.7 1.4 %copy-start.1 = (bf16[512,1536]{1,0:T(8,128)(2,1)}, bf16[512,1536]{1,0:T(8,128)(2,1)S(1)}, u32[]{:S(2)}) copy-start(bf16[512,1536]{1,0:T(8,128)(2,1)S(1)} %constant_dynamic-update-slice_fusion.16) | copy-start | bytes 4718596
  102.2 11.0 %collective-permute-start.36 = (f32[256,768]{1,0:T(8,128)S(1)}, f32[256,768]{1,0:T(8,128)S(1)}, u32[]{:S(2)}, u32[]{:S(2)}) collective-permute-start(f32[256,768]{1,0:T(8,128)S(1)} %slice.81), channel_id=1, source_target_pairs={{1,0},{0,1},{3,2},{2,3},{5,4},{4,5},{7,6},{6,7},{9,8},{8,9},{11,10... | collective-permute-start | bytes 2359304 | tf_op jit(solution)/shard_map/ppermute | solution.py:60
  110.4 1.4 %copy-start.3 = (bf16[512,1536]{1,0:T(8,128)(2,1)}, bf16[512,1536]{1,0:T(8,128)(2,1)S(1)}, u32[]{:S(2)}) copy-start(bf16[512,1536]{1,0:T(8,128)(2,1)S(1)} %constant_dynamic-update-slice_fusion.17) | copy-start | bytes 4718596
  111.9 3.3 %collective-permute-start.18 = (f32[256,768]{1,0:T(8,128)S(1)}, f32[256,768]{1,0:T(8,128)S(1)}, u32[]{:S(2)}, u32[]{:S(2)}) collective-permute-start(f32[256,768]{1,0:T(8,128)S(1)} %slice.75), channel_id=1, source_target_pairs={{1,0},{0,1},{3,2},{2,3},{5,4},{4,5},{7,6},{6,7},{9,8},{8,9},{11,10... | collective-permute-start | bytes 2359304 | tf_op jit(solution)/shard_map/ppermute | solution.py:60
  116.2 17.6 %all-to-all-start.1 = ((bf16[8,32,1536]{2,1,0:T(8,128)(2,1)}), bf16[8,32,1536]{2,1,0:T(8,128)(2,1)S(1)}, u32[]{:S(2)}, u32[]{:S(2)}) async-start(bf16[8,32,1536]{2,1,0:T(8,128)(2,1)} %bitcast.10), calls=%async_computation.1 | async-start | bytes 1572864 | tf_op jit(solution)/shard_map/all_to_all | solution.py:56
  119.7 4.6 %copy-start.2 = (bf16[512,1536]{1,0:T(8,128)(2,1)S(1)}, bf16[512,1536]{1,0:T(8,128)(2,1)}, u32[]{:S(2)}) copy-start(bf16[512,1536]{1,0:T(8,128)(2,1)} %copy-done.1) | copy-start | bytes 4718596
  119.7 4.6 %copy-start.5 = (bf16[8,32,1536]{2,1,0:T(8,128)(2,1)S(1)}, bf16[8,32,1536]{2,1,0:T(8,128)(2,1)}, u32[]{:S(2)}) copy-start(bf16[8,32,1536]{2,1,0:T(8,128)(2,1)} %copy-done.4) | copy-start | bytes 2359300

commit v2 on v1

--- a/solution.py
+++ b/solution.py
@@ -64,7 +64,8 @@
     n = Y * XH
     x = jnp.broadcast_to(x[None], (n,) + x.shape).reshape(n * x.shape[0], x.shape[1])
     x = exchange_col(x)
-    return jnp.concatenate([x, swap_core(x)], axis=0)
+    m = x.shape[1] // 2
+    return [jnp.concatenate([y, swap_core(y)], axis=0) for y in (x[:, :m], x[:, m:])]
 
 
 def add_core(x):
@@ -129,8 +130,7 @@
     total = tokens.shape[0] * Y * XH * CORE
     scale = 1.0 / math.sqrt(total)
     width = tokens.shape[1]
-    panel = gather_col(jnp.concatenate([tokens, out_grad], axis=1))
-    token_panel, grad_panel = panel[:, :width], panel[:, width:]
+    token_panel, grad_panel = gather_col(jnp.concatenate([tokens, out_grad], axis=1))
     hidden = scatter_row(jnp.dot(token_panel, up_weight, preferred_element_type=f32))
     act_grad = scatter_row(contract_cols(grad_panel, down_weight))
     activ, slope = gelu_parts(hidden)

time: 135 us -> 133 us (0.985)
  matrix products: 16 us -> 13 us
  waiting for transfers between devices: 47 us -> 48.4 us
    ppermute x32, starting transfers between devices: 29.3 us -> 27.7 us  [swap_z(): lax.ppermute(x, 'row', [(pairs(z, Z) * XL + k, z * XL + k) for z in range...]
    ppermute x32, waiting for transfers between devices: 32.4 us -> 33.8 us  [swap_z(): lax.ppermute(x, 'row', [(pairs(z, Z) * XL + k, z * XL + k) for z in range...]
    ppermute x3 -> x4, waiting for transfers between devices: 3.84 us -> 2.9 us  [swap_core(): return lax.ppermute(x, 'col', [(i ^ 1, i) for i in range(Y * XH * CORE)])]
    ppermute x3 -> x4, starting transfers between devices: 11.3 us -> 12.1 us  [swap_core(): return lax.ppermute(x, 'col', [(i ^ 1, i) for i in range(Y * XH * CORE)])]
  transfers between devices with their start and end apart: 38 -> 39, of which waited for: 28 -> 27; matrix products, arithmetic and copies ran while one was open for 11% -> 11% of each run, Pallas kernels for 0% -> 0%
where the time goes in v2:
time: 133 us; the launch traced here: 132 us
  waiting for transfers between devices  48.4 us (36%)
  starting transfers between devices  44.3 us (33%)
  blocking collectives  20.8 us (16%)
  matrix products  13 us (10%)
  other arithmetic  3.36 us (3%)
  local copies, waits for them, and re-layouts  1.51 us (1%)
    ppermute x32, waiting for transfers between devices, swap_z(): lax.ppermute(x, 'row', [(pairs(z, Z) * XL + k, z * XL + k) for z in range...  33.8 us
    ppermute x32, starting transfers between devices, swap_z(): lax.ppermute(x, 'row', [(pairs(z, Z) * XL + k, z * XL + k) for z in range...  27.7 us
    all_to_all x1, blocking collectives, exchange_col(): return lax.all_to_all(x, 'col', 0, 0, axis_index_groups=groups, tiled=True)  20.8 us
    ppermute x4, starting transfers between devices, swap_core(): return lax.ppermute(x, 'col', [(i ^ 1, i) for i in range(Y * XH * CORE)])  12.1 us
    dot_general x2, matrix products, contract_rows(): lax.dot_general(left, right, (((0,), (0,)), ((), ())), preferred_element_...  7.44 us
    all_to_all x1, waiting for transfers between devices, exchange_col(): return lax.all_to_all(x, 'col', 0, 0, axis_index_groups=groups, tiled=True)  6.62 us
    ppermute x2, waiting for transfers between devices, swap_xl(): return lax.ppermute(x, 'row', [(i ^ 1, i) for i in range(Z * XL)])  5.07 us
    all_to_all x1, starting transfers between devices, exchange_col(): return lax.all_to_all(x, 'col', 0, 0, axis_index_groups=groups, tiled=True)  3.55 us
  transfers between devices with their start and end apart: 39, of which 27 were waited for; matrix products, arithmetic and copies ran while one was open for 11% of the time, Pallas kernels for 0%

profile of v2, /device:TPU:1, one launch (start us, length us, event | category | flops | bytes accessed | tf_op | source)
XLA Modules:
  0.0 132.5 jit_solution(1898192351684478305)
XLA Ops:
  0.6 1.0 pad_maximum_fusion.7
  1.7 20.8 %all_to_all.18 = bf16[8,32,1536]{2,1,0:T(8,128)(2,1)S(1)} all-to-all(bf16[8,32,1536]{2,1,0:T(8,128)(2,1)S(1)} %broadcast_in_dim.2), channel_id=1, replica_groups={{0,2,4,6,8,10,12,14},{1,3,5,7,9,11,13,15},{16,18,20,22,24,26,28,30},{17..., dimensions={0} | all-to-all | bytes 1572864 | tf_op jit(solution)/shard_map/all_to_all | solution.py:56
  22.5 2.0 %collective-permute-start = (bf16[256,768]{1,0:T(8,128)(2,1)S(1)}, bf16[256,768]{1,0:T(8,128)(2,1)S(1)}, u32[]{:S(2)}, u32[]{:S(2)}) collective-permute-start(bf16[256,768]{1,0:T(8,128)(2,1)S(1)} %get-tuple-element.47), channel_id=1, source_target_pairs={{1,0},{0,1},{3,2},{2,3},{5,4},{4,5},{7,6},{6,7},{9,8},{8,9},{11,10... | collective-permute-start | bytes 1179656 | tf_op jit(solution)/shard_map/ppermute | solution.py:60
  24.7 1.1 collective-permute-done
  25.8 1.4 %fusion.3 = f32[512,1536]{1,0:T(8,128)S(1)} fusion(bf16[768,1536]{1,0:T(8,128)(2,1)S(1)} %copy-done, bf16[256,768]{1,0:T(8,128)(2,1)S(1)} %collective-permute-done, bf16[256,768]{1,0:T(8,128)(2,1)S(1)} %get-tuple-element.47), kind=kOutput, calls=%fused_computation.12 | convolution fusion | flops 1209532416 | bytes 6291456 | tf_op jit(solution)/shard_map/dot_general | solution.py:134
  27.3 5.7 %collective-permute-start.3 = (bf16[64,768]{1,0:T(8,128)(2,1)S(1)}, bf16[64,768]{1,0:T(8,128)(2,1)S(1)}, u32[]{:S(2)}, u32[]{:S(2)}) collective-permute-start(bf16[64,768]{1,0:T(8,128)(2,1)S(1)} %get-tuple-element.50), channel_id=1, source_target_pairs={{224,0},{240,16},{64,32},{80,48},{32,64},{48,80},{128,96},{144,112... | collective-permute-start | bytes 294920 | tf_op jit(solution)/shard_map/ppermute | solution.py:44
  33.0 1.4 %fusion.2 = f32[512,1536]{1,0:T(8,128)S(1)} fusion(bf16[1536,768]{1,0:T(8,128)(2,1)S(1)} %copy-done.5, bf16[256,768]{1,0:T(8,128)(2,1)S(1)} %collective-permute-done.19, bf16[256,768]{1,0:T(8,128)(2,1)S(1)} %get-tuple-element.46), kind=kOutput, calls=%fused_computation.11 | convolution fusion | flops 1209532416 | bytes 6291456 | tf_op jit(solution)/shard_map/dot_general | solution.py:30
  34.5 1.5 %collective-permute-start.22 = (bf16[64,768]{1,0:T(8,128)(2,1)S(1)}, bf16[64,768]{1,0:T(8,128)(2,1)S(1)}, u32[]{:S(2)}, u32[]{:S(2)}) collective-permute-start(bf16[64,768]{1,0:T(8,128)(2,1)S(1)} %get-tuple-element.48), channel_id=1, source_target_pairs={{224,0},{240,16},{64,32},{80,48},{32,64},{48,80},{128,96},{144,112... | collective-permute-start | bytes 294920 | tf_op jit(solution)/shard_map/ppermute | solution.py:44
  36.0 0.7 collective-permute-start.20
  36.8 1.5 %collective-permute-start.2 = (bf16[64,1536]{1,0:T(8,128)(2,1)S(1)}, bf16[64,1536]{1,0:T(8,128)(2,1)S(1)}, u32[]{:S(2)}, u32[]{:S(2)}) collective-permute-start(bf16[64,1536]{1,0:T(8,128)(2,1)S(1)} %get-tuple-element.45), channel_id=1, source_target_pairs={{224,0},{240,16},{64,32},{80,48},{32,64},{48,80},{128,96},{144,112... | collective-permute-start | bytes 589832 | tf_op jit(solution)/shard_map/ppermute | solution.py:44
  38.4 0.9 collective-permute-done.22
  39.2 0.5 collective-permute-done.20
  39.8 1.0 collective-permute-start.21
  40.9 0.5 collective-permute-start.23
  41.4 1.6 %collective-permute-done.2 = bf16[64,1536]{1,0:T(8,128)(2,1)S(1)} collective-permute-done((bf16[64,1536]{1,0:T(8,128)(2,1)S(1)}, bf16[64,1536]{1,0:T(8,128)(2,1)S(1)}, u32[]{:S(2)}, u32[]{:S(2)}) %collective-permute-start.2) | collective-permute-done | bytes 196640 | tf_op jit(solution)/shard_map/ppermute | solution.py:44
  43.0 1.1 collective-permute-done.4
  44.1 1.1 collective-permute-start.5
  45.3 2.1 %collective-permute-done.21 = bf16[64,1536]{1,0:T(8,128)(2,1)S(1)} collective-permute-done((bf16[64,1536]{1,0:T(8,128)(2,1)S(1)}, bf16[64,1536]{1,0:T(8,128)(2,1)S(1)}, u32[]{:S(2)}, u32[]{:S(2)}) %collective-permute-start.21) | collective-permute-done | bytes 196640 | tf_op jit(solution)/shard_map/ppermute | solution.py:44
  47.4 0.9 collective-permute-done.23
  48.4 0.7 collective-permute-start.24
  49.0 0.4 collective-permute-start.25
  49.5 3.0 %collective-permute-done.5 = bf16[64,1536]{1,0:T(8,128)(2,1)S(1)} collective-permute-done((bf16[64,1536]{1,0:T(8,128)(2,1)S(1)}, bf16[64,1536]{1,0:T(8,128)(2,1)S(1)}, u32[]{:S(2)}, u32[]{:S(2)}) %collective-permute-start.5) | collective-permute-done | bytes 196640 | tf_op jit(solution)/shard_map/ppermute | solution.py:44
  52.6 0.6 collective-permute-start.7
  53.2 0.8 collective-permute-start.8
  54.0 2.7 %collective-permute-done.24 = bf16[64,1536]{1,0:T(8,128)(2,1)S(1)} collective-permute-done((bf16[64,1536]{1,0:T(8,128)(2,1)S(1)}, bf16[64,1536]{1,0:T(8,128)(2,1)S(1)}, u32[]{:S(2)}, u32[]{:S(2)}) %collective-permute-start.24) | collective-permute-done | bytes 196640 | tf_op jit(solution)/shard_map/ppermute | solution.py:44
  57.0 0.5 collective-permute-start.26
  57.5 0.7 collective-permute-start.27
  58.2 2.5 %collective-permute-done.7 = bf16[64,1536]{1,0:T(8,128)(2,1)S(1)} collective-permute-done((bf16[64,1536]{1,0:T(8,128)(2,1)S(1)}, bf16[64,1536]{1,0:T(8,128)(2,1)S(1)}, u32[]{:S(2)}, u32[]{:S(2)}) %collective-permute-start.7) | collective-permute-done | bytes 196640 | tf_op jit(solution)/shard_map/ppermute | solution.py:44
  60.8 0.5 collective-permute-start.9
  61.3 3.6 %collective-permute-done.26 = bf16[64,1536]{1,0:T(8,128)(2,1)S(1)} collective-permute-done((bf16[64,1536]{1,0:T(8,128)(2,1)S(1)}, bf16[64,1536]{1,0:T(8,128)(2,1)S(1)}, u32[]{:S(2)}, u32[]{:S(2)}) %collective-permute-start.26) | collective-permute-done | bytes 196640 | tf_op jit(solution)/shard_map/ppermute | solution.py:44
  65.0 0.4 collective-permute-start.28
  65.5 5.0 %collective-permute-done.28 = bf16[64,1536]{1,0:T(8,128)(2,1)S(1)} collective-permute-done((bf16[64,1536]{1,0:T(8,128)(2,1)S(1)}, bf16[64,1536]{1,0:T(8,128)(2,1)S(1)}, u32[]{:S(2)}, u32[]{:S(2)}) %collective-permute-start.28) | collective-permute-done | bytes 196640 | tf_op jit(solution)/shard_map/ppermute | solution.py:50
  70.6 0.4 constant_dynamic-update-slice_fusion.7
  70.9 0.7 collective-permute-start.29
  72.0 1.6 %collective-permute-start.10 = (bf16[64,1536]{1,0:T(8,128)(2,1)S(1)}, bf16[64,1536]{1,0:T(8,128)(2,1)S(1)}, u32[]{:S(2)}, u32[]{:S(2)}) collective-permute-start(bf16[64,1536]{1,0:T(8,128)(2,1)S(1)} %get-tuple-element.29), channel_id=1, source_target_pairs={{32,0},{48,16},{0,32},{16,48},{96,64},{112,80},{64,96},{80,112},{1... | collective-permute-start | bytes 589832 | tf_op jit(solution)/shard_map/ppermute | solution.py:44
  73.6 1.2 collective-permute-start.11
  74.8 0.8 collective-permute-done.29
  75.6 0.7 collective-permute-start.31
  76.3 1.1 collective-permute-done.30
  77.7 1.5 %collective-permute-start.12 = (bf16[64,1536]{1,0:T(8,128)(2,1)S(1)}, bf16[64,1536]{1,0:T(8,128)(2,1)S(1)}, u32[]{:S(2)}, u32[]{:S(2)}) collective-permute-start(bf16[64,1536]{1,0:T(8,128)(2,1)S(1)} %collective-permute-done.10), channel_id=1, source_target_pairs={{224,0},{240,16},{64,32},{80,48},{32,64},{48,80},{128,96},{144,112... | collective-permute-start | bytes 589832 | tf_op jit(solution)/shard_map/ppermute | solution.py:44
  79.5 0.5 collective-permute-start.13
  79.9 3.8 %collective-permute-done.31 = bf16[64,1536]{1,0:T(8,128)(2,1)S(1)} collective-permute-done((bf16[64,1536]{1,0:T(8,128)(2,1)S(1)}, bf16[64,1536]{1,0:T(8,128)(2,1)S(1)}, u32[]{:S(2)}, u32[]{:S(2)}) %collective-permute-start.31) | collective-permute-done | bytes 196640 | tf_op jit(solution)/shard_map/ppermute | solution.py:44
  83.8 0.5 collective-permute-done.32
  84.3 0.9 collective-permute-start.34
  85.3 2.7 %collective-permute-done.12 = bf16[64,1536]{1,0:T(8,128)(2,1)S(1)} collective-permute-done((bf16[64,1536]{1,0:T(8,128)(2,1)S(1)}, bf16[64,1536]{1,0:T(8,128)(2,1)S(1)}, u32[]{:S(2)}, u32[]{:S(2)}) %collective-permute-start.12) | collective-permute-done | bytes 196640 | tf_op jit(solution)/shard_map/ppermute | solution.py:44
  88.0 0.6 collective-permute-start.15
  88.6 1.5 %collective-permute-done.33 = bf16[64,1536]{1,0:T(8,128)(2,1)S(1)} collective-permute-done((bf16[64,1536]{1,0:T(8,128)(2,1)S(1)}, bf16[64,1536]{1,0:T(8,128)(2,1)S(1)}, u32[]{:S(2)}, u32[]{:S(2)}) %collective-permute-start.33) | collective-permute-done | bytes 196640 | tf_op jit(solution)/shard_map/ppermute | solution.py:44
  90.2 1.9 %collective-permute-start.35 = (bf16[64,768]{1,0:T(8,128)(2,1)S(1)}, bf16[64,768]{1,0:T(8,128)(2,1)S(1)}, u32[]{:S(2)}, u32[]{:S(2)}) collective-permute-start(bf16[64,768]{1,0:T(8,128)(2,1)S(1)} %slice.78), channel_id=1, source_target_pairs={{224,0},{240,16},{64,32},{80,48},{32,64},{48,80},{128,96},{144,112... | collective-permute-start | bytes 294920 | tf_op jit(solution)/shard_map/ppermute | solution.py:44
  92.1 0.4 collective-permute-done.34
  92.7 2.0 %collective-permute-done.14 = bf16[64,1536]{1,0:T(8,128)(2,1)S(1)} collective-permute-done((bf16[64,1536]{1,0:T(8,128)(2,1)S(1)}, bf16[64,1536]{1,0:T(8,128)(2,1)S(1)}, u32[]{:S(2)}, u32[]{:S(2)}) %collective-permute-start.14) | collective-permute-done | bytes 196640 | tf_op jit(solution)/shard_map/ppermute | solution.py:44
  94.6 1.7 %collective-permute-start.16 = (bf16[64,768]{1,0:T(8,128)(2,1)S(1)}, bf16[64,768]{1,0:T(8,128)(2,1)S(1)}, u32[]{:S(2)}, u32[]{:S(2)}) collective-permute-start(bf16[64,768]{1,0:T(8,128)(2,1)S(1)} %slice.71), channel_id=1, source_target_pairs={{224,0},{240,16},{64,32},{80,48},{32,64},{48,80},{128,96},{144,112... | collective-permute-start | bytes 294920 | tf_op jit(solution)/shard_map/ppermute | solution.py:44
  96.5 0.3 collective-permute-start.17
  96.9 1.2 collective-permute-done.35
  98.2 1.4 %fusion.23 = f32[512,768]{1,0:T(8,128)S(1)} fusion(bf16[512,1536]{1,0:T(8,128)(2,1)S(1)} %constant_dynamic-update-slice_fusion.16, bf16[768,1536]{1,0:T(8,128)(2,1)S(1)} %copy-done), kind=kOutput, calls=%fused_computation.68 | convolution fusion | flops 1207959552 | bytes 5505024 | tf_op jit(solution)/shard_map/dot_general | solution.py:30
  99.7 7.9 %collective-permute-start.37 = (f32[256,768]{1,0:T(8,128)S(1)}, f32[256,768]{1,0:T(8,128)S(1)}, u32[]{:S(2)}, u32[]{:S(2)}) collective-permute-start(f32[256,768]{1,0:T(8,128)S(1)} %slice.81), channel_id=1, source_target_pairs={{1,0},{0,1},{3,2},{2,3},{5,4},{4,5},{7,6},{6,7},{9,8},{8,9},{11,10... | collective-permute-start | bytes 2359304 | tf_op jit(solution)/shard_map/ppermute | solution.py:60
  107.6 1.4 %fusion.22 = f32[512,768]{1,0:T(8,128)S(1)} fusion(bf16[512,1536]{1,0:T(8,128)(2,1)S(1)} %constant_dynamic-update-slice_fusion.17, bf16[1536,768]{1,0:T(8,128)(2,1)S(1)} %copy-done.5), kind=kOutput, calls=%fused_computation.67 | convolution fusion | flops 1207959552 | bytes 5505024 | tf_op jit(solution)/shard_map/dot_general | solution.py:139
  109.1 2.0 %collective-permute-start.18 = (f32[256,768]{1,0:T(8,128)S(1)}, f32[256,768]{1,0:T(8,128)S(1)}, u32[]{:S(2)}, u32[]{:S(2)}) collective-permute-start(f32[256,768]{1,0:T(8,128)S(1)} %slice.74), channel_id=1, source_target_pairs={{1,0},{0,1},{3,2},{2,3},{5,4},{4,5},{7,6},{6,7},{9,8},{8,9},{11,10... | collective-permute-start | bytes 2359304 | tf_op jit(solution)/shard_map/ppermute | solution.py:60
  111.2 1.8 %collective-permute-done.18 = f32[256,768]{1,0:T(8,128)S(1)} collective-permute-done((f32[256,768]{1,0:T(8,128)S(1)}, f32[256,768]{1,0:T(8,128)S(1)}, u32[]{:S(2)}, u32[]{:S(2)}) %collective-permute-start.18) | collective-permute-done | bytes 786464 | tf_op jit(solution)/shard_map/ppermute | solution.py:60
  113.1 0.9 pad_maximum_fusion.2
  114.1 3.5 %all-to-all-start.1 = ((bf16[8,32,1536]{2,1,0:T(8,128)(2,1)}), bf16[8,32,1536]{2,1,0:T(8,128)(2,1)S(1)}, u32[]{:S(2)}, u32[]{:S(2)}) async-start(bf16[8,32,1536]{2,1,0:T(8,128)(2,1)} %bitcast.10), calls=%async_computation.1 | async-start | bytes 1572864 | tf_op jit(solution)/shard_map/all_to_all | solution.py:56
  117.6 4.6 %multiply_convert_fusion.1 = bf16[768,1536]{1,0:T(8,128)(2,1)} fusion(bf16[512,1536]{1,0:T(8,128)(2,1)} %copy-done.1, bf16[256,768]{1,0:T(8,128)(2,1)} %copy-done.6, bf16[256,768]{1,0:T(8,128)(2,1)} %copy-done.4), kind=kOutput, calls=%fused_computation.1 | convolution fusion | flops 1211891712 | bytes 4718592 | tf_op jit(solution)/shard_map/dot_general | solution.py:24
  122.2 2.8 %multiply_convert_fusion = bf16[1536,768]{1,0:T(8,128)(2,1)} fusion(bf16[512,1536]{1,0:T(8,128)(2,1)S(1)} %copy-done.3, bf16[256,768]{1,0:T(8,128)(2,1)S(1)} %copy-done.8, bf16[256,768]{1,0:T(8,128)(2,1)S(1)} %get-tuple-element.46), kind=kOutput, calls=%fused_computation | convolution fusion | flops 1211891712 | bytes 4718592 | tf_op jit(solution)/shard_map/dot_general | solution.py:24
  125.1 6.6 %all-to-all-done.1 = bf16[8,32,1536]{2,1,0:T(8,128)(2,1)S(1)} async-done(((bf16[8,32,1536]{2,1,0:T(8,128)(2,1)}), bf16[8,32,1536]{2,1,0:T(8,128)(2,1)S(1)}, u32[]{:S(2)}, u32[]{:S(2)}) %all-to-all-start.1) | async-done | bytes 786464 | tf_op jit(solution)/shard_map/all_to_all | solution.py:56
  131.8 0.6 fusion.21
  (85 shorter events, 3.3 us)
Async XLA Ops:
  0.6 25.2 %copy-start = (bf16[768,1536]{1,0:T(8,128)(2,1)S(1)}, bf16[768,1536]{1,0:T(8,128)(2,1)}, u32[]{:S(2)}) copy-start(bf16[768,1536]{1,0:T(8,128)(2,1)} %param.5) | copy-start | bytes 7077892
  22.5 4.7 %copy-start.4 = (bf16[256,768]{1,0:T(8,128)(2,1)}, bf16[256,768]{1,0:T(8,128)(2,1)S(1)}, u32[]{:S(2)}) copy-start(bf16[256,768]{1,0:T(8,128)(2,1)S(1)} %get-tuple-element.47) | copy-start | bytes 1179652
  22.5 3.3 %collective-permute-start = (bf16[256,768]{1,0:T(8,128)(2,1)S(1)}, bf16[256,768]{1,0:T(8,128)(2,1)S(1)}, u32[]{:S(2)}, u32[]{:S(2)}) collective-permute-start(bf16[256,768]{1,0:T(8,128)(2,1)S(1)} %get-tuple-element.47), channel_id=1, source_target_pairs={{1,0},{0,1},{3,2},{2,3},{5,4},{4,5},{7,6},{6,7},{9,8},{8,9},{11,10... | collective-permute-start | bytes 1179656 | tf_op jit(solution)/shard_map/ppermute | solution.py:60
  24.5 8.5 %copy-start.5 = (bf16[1536,768]{1,0:T(8,128)(2,1)S(1)}, bf16[1536,768]{1,0:T(8,128)(2,1)}, u32[]{:S(2)}) copy-start(bf16[1536,768]{1,0:T(8,128)(2,1)} %param.6) | copy-start | bytes 7077892
  24.5 8.5 %collective-permute-start.19 = (bf16[256,768]{1,0:T(8,128)(2,1)S(1)}, bf16[256,768]{1,0:T(8,128)(2,1)S(1)}, u32[]{:S(2)}, u32[]{:S(2)}) collective-permute-start(bf16[256,768]{1,0:T(8,128)(2,1)S(1)} %get-tuple-element.46), channel_id=1, source_target_pairs={{1,0},{0,1},{3,2},{2,3},{5,4},{4,5},{7,6},{6,7},{9,8},{8,9},{11,10... | collective-permute-start | bytes 1179656 | tf_op jit(solution)/shard_map/ppermute | solution.py:60
  25.8 1.4 %copy-start.6 = (bf16[256,768]{1,0:T(8,128)(2,1)}, bf16[256,768]{1,0:T(8,128)(2,1)S(1)}, u32[]{:S(2)}) copy-start(bf16[256,768]{1,0:T(8,128)(2,1)S(1)} %collective-permute-done) | copy-start | bytes 1179652
  27.3 9.4 %collective-permute-start.3 = (bf16[64,768]{1,0:T(8,128)(2,1)S(1)}, bf16[64,768]{1,0:T(8,128)(2,1)S(1)}, u32[]{:S(2)}, u32[]{:S(2)}) collective-permute-start(bf16[64,768]{1,0:T(8,128)(2,1)S(1)} %get-tuple-element.50), channel_id=1, source_target_pairs={{224,0},{240,16},{64,32},{80,48},{32,64},{48,80},{128,96},{144,112... | collective-permute-start | bytes 294920 | tf_op jit(solution)/shard_map/ppermute | solution.py:44
  33.0 3.8 %collective-permute-start.1 = (bf16[64,768]{1,0:T(8,128)(2,1)S(1)}, bf16[64,768]{1,0:T(8,128)(2,1)S(1)}, u32[]{:S(2)}, u32[]{:S(2)}) collective-permute-start(bf16[64,768]{1,0:T(8,128)(2,1)S(1)} %get-tuple-element.51), channel_id=1, source_target_pairs={{32,0},{48,16},{0,32},{16,48},{96,64},{112,80},{64,96},{80,112},{1... | collective-permute-start | bytes 294920 | tf_op jit(solution)/shard_map/ppermute | solution.py:44
  33.0 1.4 %copy-start.7 = (bf16[256,768]{1,0:T(8,128)(2,1)}, bf16[256,768]{1,0:T(8,128)(2,1)S(1)}, u32[]{:S(2)}) copy-start(bf16[256,768]{1,0:T(8,128)(2,1)S(1)} %collective-permute-done.19) | copy-start | bytes 1179652
  34.5 4.8 %collective-permute-start.22 = (bf16[64,768]{1,0:T(8,128)(2,1)S(1)}, bf16[64,768]{1,0:T(8,128)(2,1)S(1)}, u32[]{:S(2)}, u32[]{:S(2)}) collective-permute-start(bf16[64,768]{1,0:T(8,128)(2,1)S(1)} %get-tuple-element.48), channel_id=1, source_target_pairs={{224,0},{240,16},{64,32},{80,48},{32,64},{48,80},{128,96},{144,112... | collective-permute-start | bytes 294920 | tf_op jit(solution)/shard_map/ppermute | solution.py:44
  36.0 3.8 %collective-permute-start.20 = (bf16[64,768]{1,0:T(8,128)(2,1)S(1)}, bf16[64,768]{1,0:T(8,128)(2,1)S(1)}, u32[]{:S(2)}, u32[]{:S(2)}) collective-permute-start(bf16[64,768]{1,0:T(8,128)(2,1)S(1)} %get-tuple-element.49), channel_id=1, source_target_pairs={{32,0},{48,16},{0,32},{16,48},{96,64},{112,80},{64,96},{80,112},{1... | collective-permute-start | bytes 294920 | tf_op jit(solution)/shard_map/ppermute | solution.py:44
  36.8 6.2 %collective-permute-start.2 = (bf16[64,1536]{1,0:T(8,128)(2,1)S(1)}, bf16[64,1536]{1,0:T(8,128)(2,1)S(1)}, u32[]{:S(2)}, u32[]{:S(2)}) collective-permute-start(bf16[64,1536]{1,0:T(8,128)(2,1)S(1)} %get-tuple-element.45), channel_id=1, source_target_pairs={{224,0},{240,16},{64,32},{80,48},{32,64},{48,80},{128,96},{144,112... | collective-permute-start | bytes 589832 | tf_op jit(solution)/shard_map/ppermute | solution.py:44
  38.3 5.7 %collective-permute-start.4 = (bf16[64,1536]{1,0:T(8,128)(2,1)S(1)}, bf16[64,1536]{1,0:T(8,128)(2,1)S(1)}, u32[]{:S(2)}, u32[]{:S(2)}) collective-permute-start(bf16[64,1536]{1,0:T(8,128)(2,1)S(1)} %get-tuple-element.44), channel_id=1, source_target_pairs={{32,0},{48,16},{0,32},{16,48},{96,64},{112,80},{64,96},{80,112},{1... | collective-permute-start | bytes 589832 | tf_op jit(solution)/shard_map/ppermute | solution.py:44
  39.8 7.5 %collective-permute-start.21 = (bf16[64,1536]{1,0:T(8,128)(2,1)S(1)}, bf16[64,1536]{1,0:T(8,128)(2,1)S(1)}, u32[]{:S(2)}, u32[]{:S(2)}) collective-permute-start(bf16[64,1536]{1,0:T(8,128)(2,1)S(1)} %get-tuple-element.39), channel_id=1, source_target_pairs={{224,0},{240,16},{64,32},{80,48},{32,64},{48,80},{128,96},{144,112... | collective-permute-start | bytes 589832 | tf_op jit(solution)/shard_map/ppermute | solution.py:44
  40.9 7.4 %collective-permute-start.23 = (bf16[64,1536]{1,0:T(8,128)(2,1)S(1)}, bf16[64,1536]{1,0:T(8,128)(2,1)S(1)}, u32[]{:S(2)}, u32[]{:S(2)}) collective-permute-start(bf16[64,1536]{1,0:T(8,128)(2,1)S(1)} %get-tuple-element.38), channel_id=1, source_target_pairs={{32,0},{48,16},{0,32},{16,48},{96,64},{112,80},{64,96},{80,112},{1... | collective-permute-start | bytes 589832 | tf_op jit(solution)/shard_map/ppermute | solution.py:44
  44.1 8.3 %collective-permute-start.5 = (bf16[64,1536]{1,0:T(8,128)(2,1)S(1)}, bf16[64,1536]{1,0:T(8,128)(2,1)S(1)}, u32[]{:S(2)}, u32[]{:S(2)}) collective-permute-start(bf16[64,1536]{1,0:T(8,128)(2,1)S(1)} %get-tuple-element.43), channel_id=1, source_target_pairs={{32,0},{48,16},{0,32},{16,48},{96,64},{112,80},{64,96},{80,112},{1... | collective-permute-start | bytes 589832 | tf_op jit(solution)/shard_map/ppermute | solution.py:44
  45.3 7.2 %collective-permute-start.6 = (bf16[64,1536]{1,0:T(8,128)(2,1)S(1)}, bf16[64,1536]{1,0:T(8,128)(2,1)S(1)}, u32[]{:S(2)}, u32[]{:S(2)}) collective-permute-start(bf16[64,1536]{1,0:T(8,128)(2,1)S(1)} %get-tuple-element.42), channel_id=1, source_target_pairs={{224,0},{240,16},{64,32},{80,48},{32,64},{48,80},{128,96},{144,112... | collective-permute-start | bytes 589832 | tf_op jit(solution)/shard_map/ppermute | solution.py:44
  48.4 8.3 %collective-permute-start.24 = (bf16[64,1536]{1,0:T(8,128)(2,1)S(1)}, bf16[64,1536]{1,0:T(8,128)(2,1)S(1)}, u32[]{:S(2)}, u32[]{:S(2)}) collective-permute-start(bf16[64,1536]{1,0:T(8,128)(2,1)S(1)} %get-tuple-element.37), channel_id=1, source_target_pairs={{32,0},{48,16},{0,32},{16,48},{96,64},{112,80},{64,96},{80,112},{1... | collective-permute-start | bytes 589832 | tf_op jit(solution)/shard_map/ppermute | solution.py:44
  49.0 7.8 %collective-permute-start.25 = (bf16[64,1536]{1,0:T(8,128)(2,1)S(1)}, bf16[64,1536]{1,0:T(8,128)(2,1)S(1)}, u32[]{:S(2)}, u32[]{:S(2)}) collective-permute-start(bf16[64,1536]{1,0:T(8,128)(2,1)S(1)} %get-tuple-element.36), channel_id=1, source_target_pairs={{224,0},{240,16},{64,32},{80,48},{32,64},{48,80},{128,96},{144,112... | collective-permute-start | bytes 589832 | tf_op jit(solution)/shard_map/ppermute | solution.py:44
  52.6 8.1 %collective-permute-start.7 = (bf16[64,1536]{1,0:T(8,128)(2,1)S(1)}, bf16[64,1536]{1,0:T(8,128)(2,1)S(1)}, u32[]{:S(2)}, u32[]{:S(2)}) collective-permute-start(bf16[64,1536]{1,0:T(8,128)(2,1)S(1)} %get-tuple-element.41), channel_id=1, source_target_pairs={{224,0},{240,16},{64,32},{80,48},{32,64},{48,80},{128,96},{144,112... | collective-permute-start | bytes 589832 | tf_op jit(solution)/shard_map/ppermute | solution.py:44
  53.2 7.5 %collective-permute-start.8 = (bf16[64,1536]{1,0:T(8,128)(2,1)S(1)}, bf16[64,1536]{1,0:T(8,128)(2,1)S(1)}, u32[]{:S(2)}, u32[]{:S(2)}) collective-permute-start(bf16[64,1536]{1,0:T(8,128)(2,1)S(1)} %get-tuple-element.40), channel_id=1, source_target_pairs={{32,0},{48,16},{0,32},{16,48},{96,64},{112,80},{64,96},{80,112},{1... | collective-permute-start | bytes 589832 | tf_op jit(solution)/shard_map/ppermute | solution.py:44
  57.0 7.9 %collective-permute-start.26 = (bf16[64,1536]{1,0:T(8,128)(2,1)S(1)}, bf16[64,1536]{1,0:T(8,128)(2,1)S(1)}, u32[]{:S(2)}, u32[]{:S(2)}) collective-permute-start(bf16[64,1536]{1,0:T(8,128)(2,1)S(1)} %get-tuple-element.35), channel_id=1, source_target_pairs={{224,0},{240,16},{64,32},{80,48},{32,64},{48,80},{128,96},{144,112... | collective-permute-start | bytes 589832 | tf_op jit(solution)/shard_map/ppermute | solution.py:44
  57.5 7.4 %collective-permute-start.27 = (bf16[64,1536]{1,0:T(8,128)(2,1)S(1)}, bf16[64,1536]{1,0:T(8,128)(2,1)S(1)}, u32[]{:S(2)}, u32[]{:S(2)}) collective-permute-start(bf16[64,1536]{1,0:T(8,128)(2,1)S(1)} %get-tuple-element.34), channel_id=1, source_target_pairs={{32,0},{48,16},{0,32},{16,48},{96,64},{112,80},{64,96},{80,112},{1... | collective-permute-start | bytes 589832 | tf_op jit(solution)/shard_map/ppermute | solution.py:44
  60.8 4.7 %collective-permute-start.9 = (bf16[64,1536]{1,0:T(8,128)(2,1)S(1)}, bf16[64,1536]{1,0:T(8,128)(2,1)S(1)}, u32[]{:S(2)}, u32[]{:S(2)}) collective-permute-start(bf16[64,1536]{1,0:T(8,128)(2,1)S(1)} %get-tuple-element.32), channel_id=1, source_target_pairs={{16,0},{0,16},{48,32},{32,48},{80,64},{64,80},{112,96},{96,112},{1... | collective-permute-start | bytes 589832 | tf_op jit(solution)/shard_map/ppermute | solution.py:50
  65.0 5.5 %collective-permute-start.28 = (bf16[64,1536]{1,0:T(8,128)(2,1)S(1)}, bf16[64,1536]{1,0:T(8,128)(2,1)S(1)}, u32[]{:S(2)}, u32[]{:S(2)}) collective-permute-start(bf16[64,1536]{1,0:T(8,128)(2,1)S(1)} %fusion.11), channel_id=1, source_target_pairs={{16,0},{0,16},{48,32},{32,48},{80,64},{64,80},{112,96},{96,112},{1... | collective-permute-start | bytes 589832 | tf_op jit(solution)/shard_map/ppermute | solution.py:50
  70.9 4.6 %collective-permute-start.29 = (bf16[64,1536]{1,0:T(8,128)(2,1)S(1)}, bf16[64,1536]{1,0:T(8,128)(2,1)S(1)}, u32[]{:S(2)}, u32[]{:S(2)}) collective-permute-start(bf16[64,1536]{1,0:T(8,128)(2,1)S(1)} %get-tuple-element.31), channel_id=1, source_target_pairs={{32,0},{48,16},{0,32},{16,48},{96,64},{112,80},{64,96},{80,112},{1... | collective-permute-start | bytes 589832 | tf_op jit(solution)/shard_map/ppermute | solution.py:44
  71.6 5.7 %collective-permute-start.30 = (bf16[64,1536]{1,0:T(8,128)(2,1)S(1)}, bf16[64,1536]{1,0:T(8,128)(2,1)S(1)}, u32[]{:S(2)}, u32[]{:S(2)}) collective-permute-start(bf16[64,1536]{1,0:T(8,128)(2,1)S(1)} %get-tuple-element.31), channel_id=1, source_target_pairs={{224,0},{240,16},{64,32},{80,48},{32,64},{48,80},{128,96},{144,112... | collective-permute-start | bytes 589832 | tf_op jit(solution)/shard_map/ppermute | solution.py:44
  72.0 5.7 %collective-permute-start.10 = (bf16[64,1536]{1,0:T(8,128)(2,1)S(1)}, bf16[64,1536]{1,0:T(8,128)(2,1)S(1)}, u32[]{:S(2)}, u32[]{:S(2)}) collective-permute-start(bf16[64,1536]{1,0:T(8,128)(2,1)S(1)} %get-tuple-element.29), channel_id=1, source_target_pairs={{32,0},{48,16},{0,32},{16,48},{96,64},{112,80},{64,96},{80,112},{1... | collective-permute-start | bytes 589832 | tf_op jit(solution)/shard_map/ppermute | solution.py:44
  73.6 5.9 %collective-permute-start.11 = (bf16[64,1536]{1,0:T(8,128)(2,1)S(1)}, bf16[64,1536]{1,0:T(8,128)(2,1)S(1)}, u32[]{:S(2)}, u32[]{:S(2)}) collective-permute-start(bf16[64,1536]{1,0:T(8,128)(2,1)S(1)} %get-tuple-element.29), channel_id=1, source_target_pairs={{224,0},{240,16},{64,32},{80,48},{32,64},{48,80},{128,96},{144,112... | collective-permute-start | bytes 589832 | tf_op jit(solution)/shard_map/ppermute | solution.py:44
  75.6 8.2 %collective-permute-start.31 = (bf16[64,1536]{1,0:T(8,128)(2,1)S(1)}, bf16[64,1536]{1,0:T(8,128)(2,1)S(1)}, u32[]{:S(2)}, u32[]{:S(2)}) collective-permute-start(bf16[64,1536]{1,0:T(8,128)(2,1)S(1)} %collective-permute-done.29), channel_id=1, source_target_pairs={{224,0},{240,16},{64,32},{80,48},{32,64},{48,80},{128,96},{144,112... | collective-permute-start | bytes 589832 | tf_op jit(solution)/shard_map/ppermute | solution.py:44
  77.4 7.0 %collective-permute-start.32 = (bf16[64,1536]{1,0:T(8,128)(2,1)S(1)}, bf16[64,1536]{1,0:T(8,128)(2,1)S(1)}, u32[]{:S(2)}, u32[]{:S(2)}) collective-permute-start(bf16[64,1536]{1,0:T(8,128)(2,1)S(1)} %collective-permute-done.30), channel_id=1, source_target_pairs={{32,0},{48,16},{0,32},{16,48},{96,64},{112,80},{64,96},{80,112},{1... | collective-permute-start | bytes 589832 | tf_op jit(solution)/shard_map/ppermute | solution.py:44
  77.7 10.3 %collective-permute-start.12 = (bf16[64,1536]{1,0:T(8,128)(2,1)S(1)}, bf16[64,1536]{1,0:T(8,128)(2,1)S(1)}, u32[]{:S(2)}, u32[]{:S(2)}) collective-permute-start(bf16[64,1536]{1,0:T(8,128)(2,1)S(1)} %collective-permute-done.10), channel_id=1, source_target_pairs={{224,0},{240,16},{64,32},{80,48},{32,64},{48,80},{128,96},{144,112... | collective-permute-start | bytes 589832 | tf_op jit(solution)/shard_map/ppermute | solution.py:44
  79.5 8.6 %collective-permute-start.13 = (bf16[64,1536]{1,0:T(8,128)(2,1)S(1)}, bf16[64,1536]{1,0:T(8,128)(2,1)S(1)}, u32[]{:S(2)}, u32[]{:S(2)}) collective-permute-start(bf16[64,1536]{1,0:T(8,128)(2,1)S(1)} %collective-permute-done.11), channel_id=1, source_target_pairs={{32,0},{48,16},{0,32},{16,48},{96,64},{112,80},{64,96},{80,112},{1... | collective-permute-start | bytes 589832 | tf_op jit(solution)/shard_map/ppermute | solution.py:44
  83.8 6.4 %collective-permute-start.33 = (bf16[64,1536]{1,0:T(8,128)(2,1)S(1)}, bf16[64,1536]{1,0:T(8,128)(2,1)S(1)}, u32[]{:S(2)}, u32[]{:S(2)}) collective-permute-start(bf16[64,1536]{1,0:T(8,128)(2,1)S(1)} %collective-permute-done.31), channel_id=1, source_target_pairs={{32,0},{48,16},{0,32},{16,48},{96,64},{112,80},{64,96},{80,112},{1... | collective-permute-start | bytes 589832 | tf_op jit(solution)/shard_map/ppermute | solution.py:44
  84.3 8.2 %collective-permute-start.34 = (bf16[64,1536]{1,0:T(8,128)(2,1)S(1)}, bf16[64,1536]{1,0:T(8,128)(2,1)S(1)}, u32[]{:S(2)}, u32[]{:S(2)}) collective-permute-start(bf16[64,1536]{1,0:T(8,128)(2,1)S(1)} %collective-permute-done.32), channel_id=1, source_target_pairs={{224,0},{240,16},{64,32},{80,48},{32,64},{48,80},{128,96},{144,112... | collective-permute-start | bytes 589832 | tf_op jit(solution)/shard_map/ppermute | solution.py:44
  88.0 6.6 %collective-permute-start.14 = (bf16[64,1536]{1,0:T(8,128)(2,1)S(1)}, bf16[64,1536]{1,0:T(8,128)(2,1)S(1)}, u32[]{:S(2)}, u32[]{:S(2)}) collective-permute-start(bf16[64,1536]{1,0:T(8,128)(2,1)S(1)} %collective-permute-done.12), channel_id=1, source_target_pairs={{32,0},{48,16},{0,32},{16,48},{96,64},{112,80},{64,96},{80,112},{1... | collective-permute-start | bytes 589832 | tf_op jit(solution)/shard_map/ppermute | solution.py:44
  88.0 8.4 %collective-permute-start.15 = (bf16[64,1536]{1,0:T(8,128)(2,1)S(1)}, bf16[64,1536]{1,0:T(8,128)(2,1)S(1)}, u32[]{:S(2)}, u32[]{:S(2)}) collective-permute-start(bf16[64,1536]{1,0:T(8,128)(2,1)S(1)} %collective-permute-done.13), channel_id=1, source_target_pairs={{224,0},{240,16},{64,32},{80,48},{32,64},{48,80},{128,96},{144,112... | collective-permute-start | bytes 589832 | tf_op jit(solution)/shard_map/ppermute | solution.py:44
  90.2 7.9 %collective-permute-start.35 = (bf16[64,768]{1,0:T(8,128)(2,1)S(1)}, bf16[64,768]{1,0:T(8,128)(2,1)S(1)}, u32[]{:S(2)}, u32[]{:S(2)}) collective-permute-start(bf16[64,768]{1,0:T(8,128)(2,1)S(1)} %slice.78), channel_id=1, source_target_pairs={{224,0},{240,16},{64,32},{80,48},{32,64},{48,80},{128,96},{144,112... | collective-permute-start | bytes 294920 | tf_op jit(solution)/shard_map/ppermute | solution.py:44
  92.6 5.6 %collective-permute-start.36 = (bf16[64,768]{1,0:T(8,128)(2,1)S(1)}, bf16[64,768]{1,0:T(8,128)(2,1)S(1)}, u32[]{:S(2)}, u32[]{:S(2)}) collective-permute-start(bf16[64,768]{1,0:T(8,128)(2,1)S(1)} %slice.79), channel_id=1, source_target_pairs={{32,0},{48,16},{0,32},{16,48},{96,64},{112,80},{64,96},{80,112},{1... | collective-permute-start | bytes 294920 | tf_op jit(solution)/shard_map/ppermute | solution.py:44
  94.6 12.9 %collective-permute-start.16 = (bf16[64,768]{1,0:T(8,128)(2,1)S(1)}, bf16[64,768]{1,0:T(8,128)(2,1)S(1)}, u32[]{:S(2)}, u32[]{:S(2)}) collective-permute-start(bf16[64,768]{1,0:T(8,128)(2,1)S(1)} %slice.71), channel_id=1, source_target_pairs={{224,0},{240,16},{64,32},{80,48},{32,64},{48,80},{128,96},{144,112... | collective-permute-start | bytes 294920 | tf_op jit(solution)/shard_map/ppermute | solution.py:44
  96.5 11.1 %collective-permute-start.17 = (bf16[64,768]{1,0:T(8,128)(2,1)S(1)}, bf16[64,768]{1,0:T(8,128)(2,1)S(1)}, u32[]{:S(2)}, u32[]{:S(2)}) collective-permute-start(bf16[64,768]{1,0:T(8,128)(2,1)S(1)} %slice.72), channel_id=1, source_target_pairs={{32,0},{48,16},{0,32},{16,48},{96,64},{112,80},{64,96},{80,112},{1... | collective-permute-start | bytes 294920 | tf_op jit(solution)/shard_map/ppermute | solution.py:44
  98.2 1.4 %copy-start.1 = (bf16[512,1536]{1,0:T(8,128)(2,1)}, bf16[512,1536]{1,0:T(8,128)(2,1)S(1)}, u32[]{:S(2)}) copy-start(bf16[512,1536]{1,0:T(8,128)(2,1)S(1)} %constant_dynamic-update-slice_fusion.16) | copy-start | bytes 4718596
  99.7 11.4 %collective-permute-start.37 = (f32[256,768]{1,0:T(8,128)S(1)}, f32[256,768]{1,0:T(8,128)S(1)}, u32[]{:S(2)}, u32[]{:S(2)}) collective-permute-start(f32[256,768]{1,0:T(8,128)S(1)} %slice.81), channel_id=1, source_target_pairs={{1,0},{0,1},{3,2},{2,3},{5,4},{4,5},{7,6},{6,7},{9,8},{8,9},{11,10... | collective-permute-start | bytes 2359304 | tf_op jit(solution)/shard_map/ppermute | solution.py:60
  107.6 1.4 %copy-start.2 = (bf16[512,1536]{1,0:T(8,128)(2,1)}, bf16[512,1536]{1,0:T(8,128)(2,1)S(1)}, u32[]{:S(2)}) copy-start(bf16[512,1536]{1,0:T(8,128)(2,1)S(1)} %constant_dynamic-update-slice_fusion.17) | copy-start | bytes 4718596
  109.1 4.0 %collective-permute-start.18 = (f32[256,768]{1,0:T(8,128)S(1)}, f32[256,768]{1,0:T(8,128)S(1)}, u32[]{:S(2)}, u32[]{:S(2)}) collective-permute-start(f32[256,768]{1,0:T(8,128)S(1)} %slice.74), channel_id=1, source_target_pairs={{1,0},{0,1},{3,2},{2,3},{5,4},{4,5},{7,6},{6,7},{9,8},{8,9},{11,10... | collective-permute-start | bytes 2359304 | tf_op jit(solution)/shard_map/ppermute | solution.py:60
  114.1 17.6 %all-to-all-start.1 = ((bf16[8,32,1536]{2,1,0:T(8,128)(2,1)}), bf16[8,32,1536]{2,1,0:T(8,128)(2,1)S(1)}, u32[]{:S(2)}, u32[]{:S(2)}) async-start(bf16[8,32,1536]{2,1,0:T(8,128)(2,1)} %bitcast.10), calls=%async_computation.1 | async-start | bytes 1572864 | tf_op jit(solution)/shard_map/all_to_all | solution.py:56
  117.6 4.6 %copy-start.3 = (bf16[512,1536]{1,0:T(8,128)(2,1)S(1)}, bf16[512,1536]{1,0:T(8,128)(2,1)}, u32[]{:S(2)}) copy-start(bf16[512,1536]{1,0:T(8,128)(2,1)} %copy-done.2) | copy-start | bytes 4718596
  117.6 4.6 %copy-start.8 = (bf16[256,768]{1,0:T(8,128)(2,1)S(1)}, bf16[256,768]{1,0:T(8,128)(2,1)}, u32[]{:S(2)}) copy-start(bf16[256,768]{1,0:T(8,128)(2,1)} %copy-done.7) | copy-start | bytes 1179652

commit v3 on v2

--- a/solution.py
+++ b/solution.py
@@ -68,9 +68,11 @@
     return [jnp.concatenate([y, swap_core(y)], axis=0) for y in (x[:, :m], x[:, m:])]
 
 
-def add_core(x):
+def add_core(product, x):
     n = x.shape[0] // 2
-    return (x[:n] + swap_core(x[n:])).astype(bf16)
+    away = swap_core(product(x[n:]))
+    own = lax.optimization_barrier(product(x[:n]))
+    return (own + away).astype(bf16)
 
 
 def scatter_col(x):
@@ -129,16 +131,16 @@
 def local(tokens, up_weight, down_weight, out_grad):
     total = tokens.shape[0] * Y * XH * CORE
     scale = 1.0 / math.sqrt(total)
-    width = tokens.shape[1]
     token_panel, grad_panel = gather_col(jnp.concatenate([tokens, out_grad], axis=1))
     hidden = scatter_row(jnp.dot(token_panel, up_weight, preferred_element_type=f32))
     act_grad = scatter_row(contract_cols(grad_panel, down_weight))
     activ, slope = gelu_parts(hidden)
     act_panel = gather_row(activ.astype(bf16))
     dh_panel = gather_row((act_grad * slope).astype(bf16))
-    output = add_core(jnp.dot(act_panel, down_weight, preferred_element_type=f32))
-    token_grad = add_core(contract_cols(dh_panel, up_weight))
+    output = add_core(lambda x: jnp.dot(x, down_weight, preferred_element_type=f32), act_panel)
+    token_grad = add_core(lambda x: contract_cols(x, up_weight), dh_panel)
     both = scatter_col(jnp.concatenate([output, token_grad], axis=1))
+    width = tokens.shape[1]
     down_grad = (contract_rows(act_panel, grad_panel) * scale).astype(bf16)
     up_grad = (contract_rows(token_panel, dh_panel) * scale).astype(bf16)
     return (both[:, :width], both[:, width:], up_grad, down_grad)

time: 133 us -> 132 us (level)
    ppermute x4, waiting for transfers between devices: 2.9 us -> 1.3 us  [swap_core(): return lax.ppermute(x, 'col', [(i ^ 1, i) for i in range(Y * XH * CORE)])]
    dot_general x2 -> x3, matrix products: 2.84 us -> 3.04 us  [contract_cols(): lax.dot_general(left, right, (((1,), (1,)), ((), ())), preferred_element_...]
where the time goes in v3:
time: 132 us; the launch traced here: 131 us
  waiting for transfers between devices  47.1 us (36%)
  starting transfers between devices  44.3 us (34%)
  blocking collectives  20.8 us (16%)
  matrix products  13.4 us (10%)
  other arithmetic  3.37 us (3%)
  local copies, waits for them, and re-layouts  1.4 us (1%)
    ppermute x32, waiting for transfers between devices, swap_z(): lax.ppermute(x, 'row', [(pairs(z, Z) * XL + k, z * XL + k) for z in range...  34.1 us
    ppermute x32, starting transfers between devices, swap_z(): lax.ppermute(x, 'row', [(pairs(z, Z) * XL + k, z * XL + k) for z in range...  27.5 us
    all_to_all x1, blocking collectives, exchange_col(): return lax.all_to_all(x, 'col', 0, 0, axis_index_groups=groups, tiled=True)  20.8 us
    ppermute x4, starting transfers between devices, swap_core(): return lax.ppermute(x, 'col', [(i ^ 1, i) for i in range(Y * XH * CORE)])  12.3 us
    dot_general x2, matrix products, contract_rows(): lax.dot_general(left, right, (((0,), (0,)), ((), ())), preferred_element_...  7.44 us
    all_to_all x1, waiting for transfers between devices, exchange_col(): return lax.all_to_all(x, 'col', 0, 0, axis_index_groups=groups, tiled=True)  6.62 us
    ppermute x2, waiting for transfers between devices, swap_xl(): return lax.ppermute(x, 'row', [(i ^ 1, i) for i in range(Z * XL)])  5.07 us
    all_to_all x1, starting transfers between devices, exchange_col(): return lax.all_to_all(x, 'col', 0, 0, axis_index_groups=groups, tiled=True)  3.55 us
  transfers between devices with their start and end apart: 39, of which 27 were waited for; matrix products, arithmetic and copies ran while one was open for 11% of the time, Pallas kernels for 0%

profile of v3, /device:TPU:1, one launch (start us, length us, event | category | flops | bytes accessed | tf_op | source)
XLA Modules:
  0.0 131.4 jit_solution(15556592679473451508)
XLA Ops:
  0.6 1.0 pad_maximum_fusion.7
  1.7 20.8 %all_to_all.18 = bf16[8,32,1536]{2,1,0:T(8,128)(2,1)S(1)} all-to-all(bf16[8,32,1536]{2,1,0:T(8,128)(2,1)S(1)} %broadcast_in_dim.2), channel_id=1, replica_groups={{0,2,4,6,8,10,12,14},{1,3,5,7,9,11,13,15},{16,18,20,22,24,26,28,30},{17..., dimensions={0} | all-to-all | bytes 1572864 | tf_op jit(solution)/shard_map/all_to_all | solution.py:56
  22.5 2.0 %collective-permute-start = (bf16[256,768]{1,0:T(8,128)(2,1)S(1)}, bf16[256,768]{1,0:T(8,128)(2,1)S(1)}, u32[]{:S(2)}, u32[]{:S(2)}) collective-permute-start(bf16[256,768]{1,0:T(8,128)(2,1)S(1)} %get-tuple-element.47), channel_id=1, source_target_pairs={{1,0},{0,1},{3,2},{2,3},{5,4},{4,5},{7,6},{6,7},{9,8},{8,9},{11,10... | collective-permute-start | bytes 1179656 | tf_op jit(solution)/shard_map/ppermute | solution.py:60
  24.7 1.1 collective-permute-done
  25.8 1.4 %fusion.9 = f32[512,1536]{1,0:T(8,128)S(1)} fusion(bf16[768,1536]{1,0:T(8,128)(2,1)S(1)} %copy-done, bf16[256,768]{1,0:T(8,128)(2,1)S(1)} %collective-permute-done, bf16[256,768]{1,0:T(8,128)(2,1)S(1)} %get-tuple-element.47), kind=kOutput, calls=%fused_computation.18 | convolution fusion | flops 1209532416 | bytes 6291456 | tf_op jit(solution)/shard_map/dot_general | solution.py:135
  27.3 5.7 %collective-permute-start.3 = (bf16[64,768]{1,0:T(8,128)(2,1)S(1)}, bf16[64,768]{1,0:T(8,128)(2,1)S(1)}, u32[]{:S(2)}, u32[]{:S(2)}) collective-permute-start(bf16[64,768]{1,0:T(8,128)(2,1)S(1)} %get-tuple-element.50), channel_id=1, source_target_pairs={{224,0},{240,16},{64,32},{80,48},{32,64},{48,80},{128,96},{144,112... | collective-permute-start | bytes 294920 | tf_op jit(solution)/shard_map/ppermute | solution.py:44
  33.0 1.4 %fusion.8 = f32[512,1536]{1,0:T(8,128)S(1)} fusion(bf16[1536,768]{1,0:T(8,128)(2,1)S(1)} %copy-done.5, bf16[256,768]{1,0:T(8,128)(2,1)S(1)} %collective-permute-done.19, bf16[256,768]{1,0:T(8,128)(2,1)S(1)} %get-tuple-element.46), kind=kOutput, calls=%fused_computation.17 | convolution fusion | flops 1209532416 | bytes 6291456 | tf_op jit(solution)/shard_map/dot_general | solution.py:30
  34.5 1.5 %collective-permute-start.22 = (bf16[64,768]{1,0:T(8,128)(2,1)S(1)}, bf16[64,768]{1,0:T(8,128)(2,1)S(1)}, u32[]{:S(2)}, u32[]{:S(2)}) collective-permute-start(bf16[64,768]{1,0:T(8,128)(2,1)S(1)} %get-tuple-element.48), channel_id=1, source_target_pairs={{224,0},{240,16},{64,32},{80,48},{32,64},{48,80},{128,96},{144,112... | collective-permute-start | bytes 294920 | tf_op jit(solution)/shard_map/ppermute | solution.py:44
  36.0 0.7 collective-permute-start.20
  36.8 1.5 %collective-permute-start.2 = (bf16[64,1536]{1,0:T(8,128)(2,1)S(1)}, bf16[64,1536]{1,0:T(8,128)(2,1)S(1)}, u32[]{:S(2)}, u32[]{:S(2)}) collective-permute-start(bf16[64,1536]{1,0:T(8,128)(2,1)S(1)} %get-tuple-element.45), channel_id=1, source_target_pairs={{224,0},{240,16},{64,32},{80,48},{32,64},{48,80},{128,96},{144,112... | collective-permute-start | bytes 589832 | tf_op jit(solution)/shard_map/ppermute | solution.py:44
  38.4 0.9 collective-permute-done.22
  39.2 0.5 collective-permute-done.20
  39.8 1.0 collective-permute-start.21
  40.9 0.5 collective-permute-start.23
  41.4 1.6 %collective-permute-done.2 = bf16[64,1536]{1,0:T(8,128)(2,1)S(1)} collective-permute-done((bf16[64,1536]{1,0:T(8,128)(2,1)S(1)}, bf16[64,1536]{1,0:T(8,128)(2,1)S(1)}, u32[]{:S(2)}, u32[]{:S(2)}) %collective-permute-start.2) | collective-permute-done | bytes 196640 | tf_op jit(solution)/shard_map/ppermute | solution.py:44
  43.0 1.1 collective-permute-done.4
  44.1 1.1 collective-permute-start.5
  45.3 2.1 %collective-permute-done.21 = bf16[64,1536]{1,0:T(8,128)(2,1)S(1)} collective-permute-done((bf16[64,1536]{1,0:T(8,128)(2,1)S(1)}, bf16[64,1536]{1,0:T(8,128)(2,1)S(1)}, u32[]{:S(2)}, u32[]{:S(2)}) %collective-permute-start.21) | collective-permute-done | bytes 196640 | tf_op jit(solution)/shard_map/ppermute | solution.py:44
  47.4 0.9 collective-permute-done.23
  48.4 0.7 collective-permute-start.24
  49.0 0.4 collective-permute-start.25
  49.5 3.0 %collective-permute-done.5 = bf16[64,1536]{1,0:T(8,128)(2,1)S(1)} collective-permute-done((bf16[64,1536]{1,0:T(8,128)(2,1)S(1)}, bf16[64,1536]{1,0:T(8,128)(2,1)S(1)}, u32[]{:S(2)}, u32[]{:S(2)}) %collective-permute-start.5) | collective-permute-done | bytes 196640 | tf_op jit(solution)/shard_map/ppermute | solution.py:44
  52.6 0.6 collective-permute-start.7
  53.2 0.8 collective-permute-start.8
  54.0 2.7 %collective-permute-done.24 = bf16[64,1536]{1,0:T(8,128)(2,1)S(1)} collective-permute-done((bf16[64,1536]{1,0:T(8,128)(2,1)S(1)}, bf16[64,1536]{1,0:T(8,128)(2,1)S(1)}, u32[]{:S(2)}, u32[]{:S(2)}) %collective-permute-start.24) | collective-permute-done | bytes 196640 | tf_op jit(solution)/shard_map/ppermute | solution.py:44
  57.0 0.5 collective-permute-start.26
  57.5 0.7 collective-permute-start.27
  58.2 2.5 %collective-permute-done.7 = bf16[64,1536]{1,0:T(8,128)(2,1)S(1)} collective-permute-done((bf16[64,1536]{1,0:T(8,128)(2,1)S(1)}, bf16[64,1536]{1,0:T(8,128)(2,1)S(1)}, u32[]{:S(2)}, u32[]{:S(2)}) %collective-permute-start.7) | collective-permute-done | bytes 196640 | tf_op jit(solution)/shard_map/ppermute | solution.py:44
  60.8 0.5 collective-permute-start.9
  61.3 3.6 %collective-permute-done.26 = bf16[64,1536]{1,0:T(8,128)(2,1)S(1)} collective-permute-done((bf16[64,1536]{1,0:T(8,128)(2,1)S(1)}, bf16[64,1536]{1,0:T(8,128)(2,1)S(1)}, u32[]{:S(2)}, u32[]{:S(2)}) %collective-permute-start.26) | collective-permute-done | bytes 196640 | tf_op jit(solution)/shard_map/ppermute | solution.py:44
  65.0 0.4 collective-permute-start.28
  65.5 5.0 %collective-permute-done.28 = bf16[64,1536]{1,0:T(8,128)(2,1)S(1)} collective-permute-done((bf16[64,1536]{1,0:T(8,128)(2,1)S(1)}, bf16[64,1536]{1,0:T(8,128)(2,1)S(1)}, u32[]{:S(2)}, u32[]{:S(2)}) %collective-permute-start.28) | collective-permute-done | bytes 196640 | tf_op jit(solution)/shard_map/ppermute | solution.py:50
  70.6 0.4 constant_dynamic-update-slice_fusion.7
  70.9 0.7 collective-permute-start.29
  72.0 1.6 %collective-permute-start.10 = (bf16[64,1536]{1,0:T(8,128)(2,1)S(1)}, bf16[64,1536]{1,0:T(8,128)(2,1)S(1)}, u32[]{:S(2)}, u32[]{:S(2)}) collective-permute-start(bf16[64,1536]{1,0:T(8,128)(2,1)S(1)} %get-tuple-element.29), channel_id=1, source_target_pairs={{32,0},{48,16},{0,32},{16,48},{96,64},{112,80},{64,96},{80,112},{1... | collective-permute-start | bytes 589832 | tf_op jit(solution)/shard_map/ppermute | solution.py:44
  73.6 1.2 collective-permute-start.11
  74.8 0.8 collective-permute-done.29
  75.6 0.7 collective-permute-start.31
  76.3 1.1 collective-permute-done.30
  77.7 1.5 %collective-permute-start.12 = (bf16[64,1536]{1,0:T(8,128)(2,1)S(1)}, bf16[64,1536]{1,0:T(8,128)(2,1)S(1)}, u32[]{:S(2)}, u32[]{:S(2)}) collective-permute-start(bf16[64,1536]{1,0:T(8,128)(2,1)S(1)} %collective-permute-done.10), channel_id=1, source_target_pairs={{224,0},{240,16},{64,32},{80,48},{32,64},{48,80},{128,96},{144,112... | collective-permute-start | bytes 589832 | tf_op jit(solution)/shard_map/ppermute | solution.py:44
  79.5 0.5 collective-permute-start.13
  79.9 3.8 %collective-permute-done.31 = bf16[64,1536]{1,0:T(8,128)(2,1)S(1)} collective-permute-done((bf16[64,1536]{1,0:T(8,128)(2,1)S(1)}, bf16[64,1536]{1,0:T(8,128)(2,1)S(1)}, u32[]{:S(2)}, u32[]{:S(2)}) %collective-permute-start.31) | collective-permute-done | bytes 196640 | tf_op jit(solution)/shard_map/ppermute | solution.py:44
  83.8 0.5 collective-permute-done.32
  84.3 0.9 collective-permute-start.34
  85.3 2.7 %collective-permute-done.12 = bf16[64,1536]{1,0:T(8,128)(2,1)S(1)} collective-permute-done((bf16[64,1536]{1,0:T(8,128)(2,1)S(1)}, bf16[64,1536]{1,0:T(8,128)(2,1)S(1)}, u32[]{:S(2)}, u32[]{:S(2)}) %collective-permute-start.12) | collective-permute-done | bytes 196640 | tf_op jit(solution)/shard_map/ppermute | solution.py:44
  88.0 0.6 collective-permute-start.15
  88.6 1.5 %collective-permute-done.33 = bf16[64,1536]{1,0:T(8,128)(2,1)S(1)} collective-permute-done((bf16[64,1536]{1,0:T(8,128)(2,1)S(1)}, bf16[64,1536]{1,0:T(8,128)(2,1)S(1)}, u32[]{:S(2)}, u32[]{:S(2)}) %collective-permute-start.33) | collective-permute-done | bytes 196640 | tf_op jit(solution)/shard_map/ppermute | solution.py:44
  90.2 1.9 %collective-permute-start.35 = (bf16[64,768]{1,0:T(8,128)(2,1)S(1)}, bf16[64,768]{1,0:T(8,128)(2,1)S(1)}, u32[]{:S(2)}, u32[]{:S(2)}) collective-permute-start(bf16[64,768]{1,0:T(8,128)(2,1)S(1)} %slice.78), channel_id=1, source_target_pairs={{224,0},{240,16},{64,32},{80,48},{32,64},{48,80},{128,96},{144,112... | collective-permute-start | bytes 294920 | tf_op jit(solution)/shard_map/ppermute | solution.py:44
  92.1 0.4 collective-permute-done.34
  92.7 2.0 %collective-permute-done.14 = bf16[64,1536]{1,0:T(8,128)(2,1)S(1)} collective-permute-done((bf16[64,1536]{1,0:T(8,128)(2,1)S(1)}, bf16[64,1536]{1,0:T(8,128)(2,1)S(1)}, u32[]{:S(2)}, u32[]{:S(2)}) %collective-permute-start.14) | collective-permute-done | bytes 196640 | tf_op jit(solution)/shard_map/ppermute | solution.py:44
  94.6 1.7 %collective-permute-start.16 = (bf16[64,768]{1,0:T(8,128)(2,1)S(1)}, bf16[64,768]{1,0:T(8,128)(2,1)S(1)}, u32[]{:S(2)}, u32[]{:S(2)}) collective-permute-start(bf16[64,768]{1,0:T(8,128)(2,1)S(1)} %slice.71), channel_id=1, source_target_pairs={{224,0},{240,16},{64,32},{80,48},{32,64},{48,80},{128,96},{144,112... | collective-permute-start | bytes 294920 | tf_op jit(solution)/shard_map/ppermute | solution.py:44
  96.7 1.4 %collective-permute-done.35 = bf16[64,768]{1,0:T(8,128)(2,1)S(1)} collective-permute-done((bf16[64,768]{1,0:T(8,128)(2,1)S(1)}, bf16[64,768]{1,0:T(8,128)(2,1)S(1)}, u32[]{:S(2)}, u32[]{:S(2)}) %collective-permute-start.35) | collective-permute-done | bytes 98336 | tf_op jit(solution)/shard_map/ppermute | solution.py:44
  98.2 0.8 fusion
  99.0 8.1 %collective-permute-start.37 = (f32[256,768]{1,0:T(8,128)S(1)}, f32[256,768]{1,0:T(8,128)S(1)}, u32[]{:S(2)}, u32[]{:S(2)}) collective-permute-start(f32[256,768]{1,0:T(8,128)S(1)} %fusion), channel_id=1, source_target_pairs={{1,0},{0,1},{3,2},{2,3},{5,4},{4,5},{7,6},{6,7},{9,8},{8,9},{11,10... | collective-permute-start | bytes 2359304 | tf_op jit(solution)/shard_map/ppermute | solution.py:60
  107.2 0.8 fusion.4
  107.9 2.0 %collective-permute-start.18 = (f32[256,768]{1,0:T(8,128)S(1)}, f32[256,768]{1,0:T(8,128)S(1)}, u32[]{:S(2)}, u32[]{:S(2)}) collective-permute-start(f32[256,768]{1,0:T(8,128)S(1)} %fusion.4), channel_id=1, source_target_pairs={{1,0},{0,1},{3,2},{2,3},{5,4},{4,5},{7,6},{6,7},{9,8},{8,9},{11,10... | collective-permute-start | bytes 2359304 | tf_op jit(solution)/shard_map/ppermute | solution.py:60
  110.0 0.8 fusion.2
  110.8 0.8 fusion.6
  112.0 0.9 pad_maximum_fusion.2
  113.0 3.5 %all-to-all-start.1 = ((bf16[8,32,1536]{2,1,0:T(8,128)(2,1)}), bf16[8,32,1536]{2,1,0:T(8,128)(2,1)S(1)}, u32[]{:S(2)}, u32[]{:S(2)}) async-start(bf16[8,32,1536]{2,1,0:T(8,128)(2,1)} %bitcast.10), calls=%async_computation.1 | async-start | bytes 1572864 | tf_op jit(solution)/shard_map/all_to_all | solution.py:56
  116.5 4.6 %multiply_convert_fusion.1 = bf16[768,1536]{1,0:T(8,128)(2,1)} fusion(bf16[512,1536]{1,0:T(8,128)(2,1)} %copy-done.1, bf16[256,768]{1,0:T(8,128)(2,1)} %copy-done.6, bf16[256,768]{1,0:T(8,128)(2,1)} %copy-done.4), kind=kOutput, calls=%fused_computation.1 | convolution fusion | flops 1211891712 | bytes 4718592 | tf_op jit(solution)/shard_map/dot_general | solution.py:24
  121.1 2.8 %multiply_convert_fusion = bf16[1536,768]{1,0:T(8,128)(2,1)} fusion(bf16[512,1536]{1,0:T(8,128)(2,1)S(1)} %copy-done.3, bf16[256,768]{1,0:T(8,128)(2,1)S(1)} %copy-done.8, bf16[256,768]{1,0:T(8,128)(2,1)S(1)} %get-tuple-element.46), kind=kOutput, calls=%fused_computation | convolution fusion | flops 1211891712 | bytes 4718592 | tf_op jit(solution)/shard_map/dot_general | solution.py:24
  124.0 6.6 %all-to-all-done.1 = bf16[8,32,1536]{2,1,0:T(8,128)(2,1)S(1)} async-done(((bf16[8,32,1536]{2,1,0:T(8,128)(2,1)}), bf16[8,32,1536]{2,1,0:T(8,128)(2,1)S(1)}, u32[]{:S(2)}, u32[]{:S(2)}) %all-to-all-start.1) | async-done | bytes 786464 | tf_op jit(solution)/shard_map/all_to_all | solution.py:56
  130.7 0.6 fusion.27
  (85 shorter events, 3.5 us)
Async XLA Ops:
  0.6 25.2 %copy-start = (bf16[768,1536]{1,0:T(8,128)(2,1)S(1)}, bf16[768,1536]{1,0:T(8,128)(2,1)}, u32[]{:S(2)}) copy-start(bf16[768,1536]{1,0:T(8,128)(2,1)} %param.5) | copy-start | bytes 7077892
  22.5 4.7 %copy-start.4 = (bf16[256,768]{1,0:T(8,128)(2,1)}, bf16[256,768]{1,0:T(8,128)(2,1)S(1)}, u32[]{:S(2)}) copy-start(bf16[256,768]{1,0:T(8,128)(2,1)S(1)} %get-tuple-element.47) | copy-start | bytes 1179652
  22.5 3.3 %collective-permute-start = (bf16[256,768]{1,0:T(8,128)(2,1)S(1)}, bf16[256,768]{1,0:T(8,128)(2,1)S(1)}, u32[]{:S(2)}, u32[]{:S(2)}) collective-permute-start(bf16[256,768]{1,0:T(8,128)(2,1)S(1)} %get-tuple-element.47), channel_id=1, source_target_pairs={{1,0},{0,1},{3,2},{2,3},{5,4},{4,5},{7,6},{6,7},{9,8},{8,9},{11,10... | collective-permute-start | bytes 1179656 | tf_op jit(solution)/shard_map/ppermute | solution.py:60
  24.5 8.5 %copy-start.5 = (bf16[1536,768]{1,0:T(8,128)(2,1)S(1)}, bf16[1536,768]{1,0:T(8,128)(2,1)}, u32[]{:S(2)}) copy-start(bf16[1536,768]{1,0:T(8,128)(2,1)} %param.6) | copy-start | bytes 7077892
  24.5 8.5 %collective-permute-start.19 = (bf16[256,768]{1,0:T(8,128)(2,1)S(1)}, bf16[256,768]{1,0:T(8,128)(2,1)S(1)}, u32[]{:S(2)}, u32[]{:S(2)}) collective-permute-start(bf16[256,768]{1,0:T(8,128)(2,1)S(1)} %get-tuple-element.46), channel_id=1, source_target_pairs={{1,0},{0,1},{3,2},{2,3},{5,4},{4,5},{7,6},{6,7},{9,8},{8,9},{11,10... | collective-permute-start | bytes 1179656 | tf_op jit(solution)/shard_map/ppermute | solution.py:60
  25.8 1.4 %copy-start.6 = (bf16[256,768]{1,0:T(8,128)(2,1)}, bf16[256,768]{1,0:T(8,128)(2,1)S(1)}, u32[]{:S(2)}) copy-start(bf16[256,768]{1,0:T(8,128)(2,1)S(1)} %collective-permute-done) | copy-start | bytes 1179652
  27.3 9.4 %collective-permute-start.3 = (bf16[64,768]{1,0:T(8,128)(2,1)S(1)}, bf16[64,768]{1,0:T(8,128)(2,1)S(1)}, u32[]{:S(2)}, u32[]{:S(2)}) collective-permute-start(bf16[64,768]{1,0:T(8,128)(2,1)S(1)} %get-tuple-element.50), channel_id=1, source_target_pairs={{224,0},{240,16},{64,32},{80,48},{32,64},{48,80},{128,96},{144,112... | collective-permute-start | bytes 294920 | tf_op jit(solution)/shard_map/ppermute | solution.py:44
  33.0 3.8 %collective-permute-start.1 = (bf16[64,768]{1,0:T(8,128)(2,1)S(1)}, bf16[64,768]{1,0:T(8,128)(2,1)S(1)}, u32[]{:S(2)}, u32[]{:S(2)}) collective-permute-start(bf16[64,768]{1,0:T(8,128)(2,1)S(1)} %get-tuple-element.51), channel_id=1, source_target_pairs={{32,0},{48,16},{0,32},{16,48},{96,64},{112,80},{64,96},{80,112},{1... | collective-permute-start | bytes 294920 | tf_op jit(solution)/shard_map/ppermute | solution.py:44
  33.0 1.4 %copy-start.7 = (bf16[256,768]{1,0:T(8,128)(2,1)}, bf16[256,768]{1,0:T(8,128)(2,1)S(1)}, u32[]{:S(2)}) copy-start(bf16[256,768]{1,0:T(8,128)(2,1)S(1)} %collective-permute-done.19) | copy-start | bytes 1179652
  34.5 4.8 %collective-permute-start.22 = (bf16[64,768]{1,0:T(8,128)(2,1)S(1)}, bf16[64,768]{1,0:T(8,128)(2,1)S(1)}, u32[]{:S(2)}, u32[]{:S(2)}) collective-permute-start(bf16[64,768]{1,0:T(8,128)(2,1)S(1)} %get-tuple-element.48), channel_id=1, source_target_pairs={{224,0},{240,16},{64,32},{80,48},{32,64},{48,80},{128,96},{144,112... | collective-permute-start | bytes 294920 | tf_op jit(solution)/shard_map/ppermute | solution.py:44
  36.0 3.8 %collective-permute-start.20 = (bf16[64,768]{1,0:T(8,128)(2,1)S(1)}, bf16[64,768]{1,0:T(8,128)(2,1)S(1)}, u32[]{:S(2)}, u32[]{:S(2)}) collective-permute-start(bf16[64,768]{1,0:T(8,128)(2,1)S(1)} %get-tuple-element.49), channel_id=1, source_target_pairs={{32,0},{48,16},{0,32},{16,48},{96,64},{112,80},{64,96},{80,112},{1... | collective-permute-start | bytes 294920 | tf_op jit(solution)/shard_map/ppermute | solution.py:44
  36.8 6.2 %collective-permute-start.2 = (bf16[64,1536]{1,0:T(8,128)(2,1)S(1)}, bf16[64,1536]{1,0:T(8,128)(2,1)S(1)}, u32[]{:S(2)}, u32[]{:S(2)}) collective-permute-start(bf16[64,1536]{1,0:T(8,128)(2,1)S(1)} %get-tuple-element.45), channel_id=1, source_target_pairs={{224,0},{240,16},{64,32},{80,48},{32,64},{48,80},{128,96},{144,112... | collective-permute-start | bytes 589832 | tf_op jit(solution)/shard_map/ppermute | solution.py:44
  38.3 5.7 %collective-permute-start.4 = (bf16[64,1536]{1,0:T(8,128)(2,1)S(1)}, bf16[64,1536]{1,0:T(8,128)(2,1)S(1)}, u32[]{:S(2)}, u32[]{:S(2)}) collective-permute-start(bf16[64,1536]{1,0:T(8,128)(2,1)S(1)} %get-tuple-element.44), channel_id=1, source_target_pairs={{32,0},{48,16},{0,32},{16,48},{96,64},{112,80},{64,96},{80,112},{1... | collective-permute-start | bytes 589832 | tf_op jit(solution)/shard_map/ppermute | solution.py:44
  39.8 7.5 %collective-permute-start.21 = (bf16[64,1536]{1,0:T(8,128)(2,1)S(1)}, bf16[64,1536]{1,0:T(8,128)(2,1)S(1)}, u32[]{:S(2)}, u32[]{:S(2)}) collective-permute-start(bf16[64,1536]{1,0:T(8,128)(2,1)S(1)} %get-tuple-element.39), channel_id=1, source_target_pairs={{224,0},{240,16},{64,32},{80,48},{32,64},{48,80},{128,96},{144,112... | collective-permute-start | bytes 589832 | tf_op jit(solution)/shard_map/ppermute | solution.py:44
  40.9 7.4 %collective-permute-start.23 = (bf16[64,1536]{1,0:T(8,128)(2,1)S(1)}, bf16[64,1536]{1,0:T(8,128)(2,1)S(1)}, u32[]{:S(2)}, u32[]{:S(2)}) collective-permute-start(bf16[64,1536]{1,0:T(8,128)(2,1)S(1)} %get-tuple-element.38), channel_id=1, source_target_pairs={{32,0},{48,16},{0,32},{16,48},{96,64},{112,80},{64,96},{80,112},{1... | collective-permute-start | bytes 589832 | tf_op jit(solution)/shard_map/ppermute | solution.py:44
  44.1 8.3 %collective-permute-start.5 = (bf16[64,1536]{1,0:T(8,128)(2,1)S(1)}, bf16[64,1536]{1,0:T(8,128)(2,1)S(1)}, u32[]{:S(2)}, u32[]{:S(2)}) collective-permute-start(bf16[64,1536]{1,0:T(8,128)(2,1)S(1)} %get-tuple-element.43), channel_id=1, source_target_pairs={{32,0},{48,16},{0,32},{16,48},{96,64},{112,80},{64,96},{80,112},{1... | collective-permute-start | bytes 589832 | tf_op jit(solution)/shard_map/ppermute | solution.py:44
  45.3 7.2 %collective-permute-start.6 = (bf16[64,1536]{1,0:T(8,128)(2,1)S(1)}, bf16[64,1536]{1,0:T(8,128)(2,1)S(1)}, u32[]{:S(2)}, u32[]{:S(2)}) collective-permute-start(bf16[64,1536]{1,0:T(8,128)(2,1)S(1)} %get-tuple-element.42), channel_id=1, source_target_pairs={{224,0},{240,16},{64,32},{80,48},{32,64},{48,80},{128,96},{144,112... | collective-permute-start | bytes 589832 | tf_op jit(solution)/shard_map/ppermute | solution.py:44
  48.4 8.3 %collective-permute-start.24 = (bf16[64,1536]{1,0:T(8,128)(2,1)S(1)}, bf16[64,1536]{1,0:T(8,128)(2,1)S(1)}, u32[]{:S(2)}, u32[]{:S(2)}) collective-permute-start(bf16[64,1536]{1,0:T(8,128)(2,1)S(1)} %get-tuple-element.37), channel_id=1, source_target_pairs={{32,0},{48,16},{0,32},{16,48},{96,64},{112,80},{64,96},{80,112},{1... | collective-permute-start | bytes 589832 | tf_op jit(solution)/shard_map/ppermute | solution.py:44
  49.0 7.8 %collective-permute-start.25 = (bf16[64,1536]{1,0:T(8,128)(2,1)S(1)}, bf16[64,1536]{1,0:T(8,128)(2,1)S(1)}, u32[]{:S(2)}, u32[]{:S(2)}) collective-permute-start(bf16[64,1536]{1,0:T(8,128)(2,1)S(1)} %get-tuple-element.36), channel_id=1, source_target_pairs={{224,0},{240,16},{64,32},{80,48},{32,64},{48,80},{128,96},{144,112... | collective-permute-start | bytes 589832 | tf_op jit(solution)/shard_map/ppermute | solution.py:44
  52.6 8.1 %collective-permute-start.7 = (bf16[64,1536]{1,0:T(8,128)(2,1)S(1)}, bf16[64,1536]{1,0:T(8,128)(2,1)S(1)}, u32[]{:S(2)}, u32[]{:S(2)}) collective-permute-start(bf16[64,1536]{1,0:T(8,128)(2,1)S(1)} %get-tuple-element.41), channel_id=1, source_target_pairs={{224,0},{240,16},{64,32},{80,48},{32,64},{48,80},{128,96},{144,112... | collective-permute-start | bytes 589832 | tf_op jit(solution)/shard_map/ppermute | solution.py:44
  53.2 7.5 %collective-permute-start.8 = (bf16[64,1536]{1,0:T(8,128)(2,1)S(1)}, bf16[64,1536]{1,0:T(8,128)(2,1)S(1)}, u32[]{:S(2)}, u32[]{:S(2)}) collective-permute-start(bf16[64,1536]{1,0:T(8,128)(2,1)S(1)} %get-tuple-element.40), channel_id=1, source_target_pairs={{32,0},{48,16},{0,32},{16,48},{96,64},{112,80},{64,96},{80,112},{1... | collective-permute-start | bytes 589832 | tf_op jit(solution)/shard_map/ppermute | solution.py:44
  57.0 7.9 %collective-permute-start.26 = (bf16[64,1536]{1,0:T(8,128)(2,1)S(1)}, bf16[64,1536]{1,0:T(8,128)(2,1)S(1)}, u32[]{:S(2)}, u32[]{:S(2)}) collective-permute-start(bf16[64,1536]{1,0:T(8,128)(2,1)S(1)} %get-tuple-element.35), channel_id=1, source_target_pairs={{224,0},{240,16},{64,32},{80,48},{32,64},{48,80},{128,96},{144,112... | collective-permute-start | bytes 589832 | tf_op jit(solution)/shard_map/ppermute | solution.py:44
  57.5 7.4 %collective-permute-start.27 = (bf16[64,1536]{1,0:T(8,128)(2,1)S(1)}, bf16[64,1536]{1,0:T(8,128)(2,1)S(1)}, u32[]{:S(2)}, u32[]{:S(2)}) collective-permute-start(bf16[64,1536]{1,0:T(8,128)(2,1)S(1)} %get-tuple-element.34), channel_id=1, source_target_pairs={{32,0},{48,16},{0,32},{16,48},{96,64},{112,80},{64,96},{80,112},{1... | collective-permute-start | bytes 589832 | tf_op jit(solution)/shard_map/ppermute | solution.py:44
  60.8 4.7 %collective-permute-start.9 = (bf16[64,1536]{1,0:T(8,128)(2,1)S(1)}, bf16[64,1536]{1,0:T(8,128)(2,1)S(1)}, u32[]{:S(2)}, u32[]{:S(2)}) collective-permute-start(bf16[64,1536]{1,0:T(8,128)(2,1)S(1)} %get-tuple-element.32), channel_id=1, source_target_pairs={{16,0},{0,16},{48,32},{32,48},{80,64},{64,80},{112,96},{96,112},{1... | collective-permute-start | bytes 589832 | tf_op jit(solution)/shard_map/ppermute | solution.py:50
  65.0 5.5 %collective-permute-start.28 = (bf16[64,1536]{1,0:T(8,128)(2,1)S(1)}, bf16[64,1536]{1,0:T(8,128)(2,1)S(1)}, u32[]{:S(2)}, u32[]{:S(2)}) collective-permute-start(bf16[64,1536]{1,0:T(8,128)(2,1)S(1)} %fusion.17), channel_id=1, source_target_pairs={{16,0},{0,16},{48,32},{32,48},{80,64},{64,80},{112,96},{96,112},{1... | collective-permute-start | bytes 589832 | tf_op jit(solution)/shard_map/ppermute | solution.py:50
  70.9 4.6 %collective-permute-start.29 = (bf16[64,1536]{1,0:T(8,128)(2,1)S(1)}, bf16[64,1536]{1,0:T(8,128)(2,1)S(1)}, u32[]{:S(2)}, u32[]{:S(2)}) collective-permute-start(bf16[64,1536]{1,0:T(8,128)(2,1)S(1)} %get-tuple-element.31), channel_id=1, source_target_pairs={{32,0},{48,16},{0,32},{16,48},{96,64},{112,80},{64,96},{80,112},{1... | collective-permute-start | bytes 589832 | tf_op jit(solution)/shard_map/ppermute | solution.py:44
  71.6 5.7 %collective-permute-start.30 = (bf16[64,1536]{1,0:T(8,128)(2,1)S(1)}, bf16[64,1536]{1,0:T(8,128)(2,1)S(1)}, u32[]{:S(2)}, u32[]{:S(2)}) collective-permute-start(bf16[64,1536]{1,0:T(8,128)(2,1)S(1)} %get-tuple-element.31), channel_id=1, source_target_pairs={{224,0},{240,16},{64,32},{80,48},{32,64},{48,80},{128,96},{144,112... | collective-permute-start | bytes 589832 | tf_op jit(solution)/shard_map/ppermute | solution.py:44
  72.0 5.7 %collective-permute-start.10 = (bf16[64,1536]{1,0:T(8,128)(2,1)S(1)}, bf16[64,1536]{1,0:T(8,128)(2,1)S(1)}, u32[]{:S(2)}, u32[]{:S(2)}) collective-permute-start(bf16[64,1536]{1,0:T(8,128)(2,1)S(1)} %get-tuple-element.29), channel_id=1, source_target_pairs={{32,0},{48,16},{0,32},{16,48},{96,64},{112,80},{64,96},{80,112},{1... | collective-permute-start | bytes 589832 | tf_op jit(solution)/shard_map/ppermute | solution.py:44
  73.6 5.9 %collective-permute-start.11 = (bf16[64,1536]{1,0:T(8,128)(2,1)S(1)}, bf16[64,1536]{1,0:T(8,128)(2,1)S(1)}, u32[]{:S(2)}, u32[]{:S(2)}) collective-permute-start(bf16[64,1536]{1,0:T(8,128)(2,1)S(1)} %get-tuple-element.29), channel_id=1, source_target_pairs={{224,0},{240,16},{64,32},{80,48},{32,64},{48,80},{128,96},{144,112... | collective-permute-start | bytes 589832 | tf_op jit(solution)/shard_map/ppermute | solution.py:44
  75.6 8.2 %collective-permute-start.31 = (bf16[64,1536]{1,0:T(8,128)(2,1)S(1)}, bf16[64,1536]{1,0:T(8,128)(2,1)S(1)}, u32[]{:S(2)}, u32[]{:S(2)}) collective-permute-start(bf16[64,1536]{1,0:T(8,128)(2,1)S(1)} %collective-permute-done.29), channel_id=1, source_target_pairs={{224,0},{240,16},{64,32},{80,48},{32,64},{48,80},{128,96},{144,112... | collective-permute-start | bytes 589832 | tf_op jit(solution)/shard_map/ppermute | solution.py:44
  77.4 7.0 %collective-permute-start.32 = (bf16[64,1536]{1,0:T(8,128)(2,1)S(1)}, bf16[64,1536]{1,0:T(8,128)(2,1)S(1)}, u32[]{:S(2)}, u32[]{:S(2)}) collective-permute-start(bf16[64,1536]{1,0:T(8,128)(2,1)S(1)} %collective-permute-done.30), channel_id=1, source_target_pairs={{32,0},{48,16},{0,32},{16,48},{96,64},{112,80},{64,96},{80,112},{1... | collective-permute-start | bytes 589832 | tf_op jit(solution)/shard_map/ppermute | solution.py:44
  77.7 10.3 %collective-permute-start.12 = (bf16[64,1536]{1,0:T(8,128)(2,1)S(1)}, bf16[64,1536]{1,0:T(8,128)(2,1)S(1)}, u32[]{:S(2)}, u32[]{:S(2)}) collective-permute-start(bf16[64,1536]{1,0:T(8,128)(2,1)S(1)} %collective-permute-done.10), channel_id=1, source_target_pairs={{224,0},{240,16},{64,32},{80,48},{32,64},{48,80},{128,96},{144,112... | collective-permute-start | bytes 589832 | tf_op jit(solution)/shard_map/ppermute | solution.py:44
  79.5 8.6 %collective-permute-start.13 = (bf16[64,1536]{1,0:T(8,128)(2,1)S(1)}, bf16[64,1536]{1,0:T(8,128)(2,1)S(1)}, u32[]{:S(2)}, u32[]{:S(2)}) collective-permute-start(bf16[64,1536]{1,0:T(8,128)(2,1)S(1)} %collective-permute-done.11), channel_id=1, source_target_pairs={{32,0},{48,16},{0,32},{16,48},{96,64},{112,80},{64,96},{80,112},{1... | collective-permute-start | bytes 589832 | tf_op jit(solution)/shard_map/ppermute | solution.py:44
  83.8 6.4 %collective-permute-start.33 = (bf16[64,1536]{1,0:T(8,128)(2,1)S(1)}, bf16[64,1536]{1,0:T(8,128)(2,1)S(1)}, u32[]{:S(2)}, u32[]{:S(2)}) collective-permute-start(bf16[64,1536]{1,0:T(8,128)(2,1)S(1)} %collective-permute-done.31), channel_id=1, source_target_pairs={{32,0},{48,16},{0,32},{16,48},{96,64},{112,80},{64,96},{80,112},{1... | collective-permute-start | bytes 589832 | tf_op jit(solution)/shard_map/ppermute | solution.py:44
  84.3 8.2 %collective-permute-start.34 = (bf16[64,1536]{1,0:T(8,128)(2,1)S(1)}, bf16[64,1536]{1,0:T(8,128)(2,1)S(1)}, u32[]{:S(2)}, u32[]{:S(2)}) collective-permute-start(bf16[64,1536]{1,0:T(8,128)(2,1)S(1)} %collective-permute-done.32), channel_id=1, source_target_pairs={{224,0},{240,16},{64,32},{80,48},{32,64},{48,80},{128,96},{144,112... | collective-permute-start | bytes 589832 | tf_op jit(solution)/shard_map/ppermute | solution.py:44
  88.0 6.6 %collective-permute-start.14 = (bf16[64,1536]{1,0:T(8,128)(2,1)S(1)}, bf16[64,1536]{1,0:T(8,128)(2,1)S(1)}, u32[]{:S(2)}, u32[]{:S(2)}) collective-permute-start(bf16[64,1536]{1,0:T(8,128)(2,1)S(1)} %collective-permute-done.12), channel_id=1, source_target_pairs={{32,0},{48,16},{0,32},{16,48},{96,64},{112,80},{64,96},{80,112},{1... | collective-permute-start | bytes 589832 | tf_op jit(solution)/shard_map/ppermute | solution.py:44
  88.0 8.4 %collective-permute-start.15 = (bf16[64,1536]{1,0:T(8,128)(2,1)S(1)}, bf16[64,1536]{1,0:T(8,128)(2,1)S(1)}, u32[]{:S(2)}, u32[]{:S(2)}) collective-permute-start(bf16[64,1536]{1,0:T(8,128)(2,1)S(1)} %collective-permute-done.13), channel_id=1, source_target_pairs={{224,0},{240,16},{64,32},{80,48},{32,64},{48,80},{128,96},{144,112... | collective-permute-start | bytes 589832 | tf_op jit(solution)/shard_map/ppermute | solution.py:44
  90.2 7.9 %collective-permute-start.35 = (bf16[64,768]{1,0:T(8,128)(2,1)S(1)}, bf16[64,768]{1,0:T(8,128)(2,1)S(1)}, u32[]{:S(2)}, u32[]{:S(2)}) collective-permute-start(bf16[64,768]{1,0:T(8,128)(2,1)S(1)} %slice.78), channel_id=1, source_target_pairs={{224,0},{240,16},{64,32},{80,48},{32,64},{48,80},{128,96},{144,112... | collective-permute-start | bytes 294920 | tf_op jit(solution)/shard_map/ppermute | solution.py:44
  92.6 5.6 %collective-permute-start.36 = (bf16[64,768]{1,0:T(8,128)(2,1)S(1)}, bf16[64,768]{1,0:T(8,128)(2,1)S(1)}, u32[]{:S(2)}, u32[]{:S(2)}) collective-permute-start(bf16[64,768]{1,0:T(8,128)(2,1)S(1)} %slice.79), channel_id=1, source_target_pairs={{32,0},{48,16},{0,32},{16,48},{96,64},{112,80},{64,96},{80,112},{1... | collective-permute-start | bytes 294920 | tf_op jit(solution)/shard_map/ppermute | solution.py:44
  94.6 12.4 %collective-permute-start.16 = (bf16[64,768]{1,0:T(8,128)(2,1)S(1)}, bf16[64,768]{1,0:T(8,128)(2,1)S(1)}, u32[]{:S(2)}, u32[]{:S(2)}) collective-permute-start(bf16[64,768]{1,0:T(8,128)(2,1)S(1)} %slice.71), channel_id=1, source_target_pairs={{224,0},{240,16},{64,32},{80,48},{32,64},{48,80},{128,96},{144,112... | collective-permute-start | bytes 294920 | tf_op jit(solution)/shard_map/ppermute | solution.py:44
  96.5 10.6 %collective-permute-start.17 = (bf16[64,768]{1,0:T(8,128)(2,1)S(1)}, bf16[64,768]{1,0:T(8,128)(2,1)S(1)}, u32[]{:S(2)}, u32[]{:S(2)}) collective-permute-start(bf16[64,768]{1,0:T(8,128)(2,1)S(1)} %slice.72), channel_id=1, source_target_pairs={{32,0},{48,16},{0,32},{16,48},{96,64},{112,80},{64,96},{80,112},{1... | collective-permute-start | bytes 294920 | tf_op jit(solution)/shard_map/ppermute | solution.py:44
  98.2 11.8 %copy-start.1 = (bf16[512,1536]{1,0:T(8,128)(2,1)}, bf16[512,1536]{1,0:T(8,128)(2,1)S(1)}, u32[]{:S(2)}) copy-start(bf16[512,1536]{1,0:T(8,128)(2,1)S(1)} %constant_dynamic-update-slice_fusion.16) | copy-start | bytes 4718596
  99.0 12.6 %collective-permute-start.37 = (f32[256,768]{1,0:T(8,128)S(1)}, f32[256,768]{1,0:T(8,128)S(1)}, u32[]{:S(2)}, u32[]{:S(2)}) collective-permute-start(f32[256,768]{1,0:T(8,128)S(1)} %fusion), channel_id=1, source_target_pairs={{1,0},{0,1},{3,2},{2,3},{5,4},{4,5},{7,6},{6,7},{9,8},{8,9},{11,10... | collective-permute-start | bytes 2359304 | tf_op jit(solution)/shard_map/ppermute | solution.py:60
  107.1 3.6 %copy-start.2 = (bf16[512,1536]{1,0:T(8,128)(2,1)}, bf16[512,1536]{1,0:T(8,128)(2,1)S(1)}, u32[]{:S(2)}) copy-start(bf16[512,1536]{1,0:T(8,128)(2,1)S(1)} %constant_dynamic-update-slice_fusion.17) | copy-start | bytes 4718596
  107.9 3.9 %collective-permute-start.18 = (f32[256,768]{1,0:T(8,128)S(1)}, f32[256,768]{1,0:T(8,128)S(1)}, u32[]{:S(2)}, u32[]{:S(2)}) collective-permute-start(f32[256,768]{1,0:T(8,128)S(1)} %fusion.4), channel_id=1, source_target_pairs={{1,0},{0,1},{3,2},{2,3},{5,4},{4,5},{7,6},{6,7},{9,8},{8,9},{11,10... | collective-permute-start | bytes 2359304 | tf_op jit(solution)/shard_map/ppermute | solution.py:60
  113.0 17.6 %all-to-all-start.1 = ((bf16[8,32,1536]{2,1,0:T(8,128)(2,1)}), bf16[8,32,1536]{2,1,0:T(8,128)(2,1)S(1)}, u32[]{:S(2)}, u32[]{:S(2)}) async-start(bf16[8,32,1536]{2,1,0:T(8,128)(2,1)} %bitcast.10), calls=%async_computation.1 | async-start | bytes 1572864 | tf_op jit(solution)/shard_map/all_to_all | solution.py:56
  116.5 4.6 %copy-start.3 = (bf16[512,1536]{1,0:T(8,128)(2,1)S(1)}, bf16[512,1536]{1,0:T(8,128)(2,1)}, u32[]{:S(2)}) copy-start(bf16[512,1536]{1,0:T(8,128)(2,1)} %copy-done.2) | copy-start | bytes 4718596
  116.5 4.6 %copy-start.8 = (bf16[256,768]{1,0:T(8,128)(2,1)S(1)}, bf16[256,768]{1,0:T(8,128)(2,1)}, u32[]{:S(2)}) copy-start(bf16[256,768]{1,0:T(8,128)(2,1)} %copy-done.7) | copy-start | bytes 1179652

commit v4 on v3

--- a/solution.py
+++ b/solution.py
@@ -65,7 +65,10 @@
     x = jnp.broadcast_to(x[None], (n,) + x.shape).reshape(n * x.shape[0], x.shape[1])
     x = exchange_col(x)
     m = x.shape[1] // 2
-    return [jnp.concatenate([y, swap_core(y)], axis=0) for y in (x[:, :m], x[:, m:])]
+    first, second = x[:, :m], x[:, m:]
+    first = jnp.concatenate([first, swap_core(first)], axis=0)
+    first, second = lax.optimization_barrier((first, second))
+    return first, jnp.concatenate([second, swap_core(second)], axis=0)
 
 
 def add_core(product, x):
@@ -76,8 +79,16 @@
 
 
 def scatter_col(x):
-    x = exchange_col(x).astype(f32)
-    return jnp.sum(x.reshape(Y * XH, -1, x.shape[1]), axis=0).astype(bf16)
+    x = exchange_col(x)
+    x = x.reshape(Y * XH, -1, x.shape[1])
+    m = x.shape[2] // 2
+    sums = []
+    for y in (x[:, :, :m], x[:, :, m:]):
+        total = y[0].astype(f32)
+        for k in range(1, Y * XH):
+            total = total + y[k].astype(f32)
+        sums.append(total.astype(bf16))
+    return sums
 
 
 def block_at(r, n):
@@ -139,11 +150,10 @@
     dh_panel = gather_row((act_grad * slope).astype(bf16))
     output = add_core(lambda x: jnp.dot(x, down_weight, preferred_element_type=f32), act_panel)
     token_grad = add_core(lambda x: contract_cols(x, up_weight), dh_panel)
-    both = scatter_col(jnp.concatenate([output, token_grad], axis=1))
-    width = tokens.shape[1]
+    output, token_grad = scatter_col(jnp.concatenate([output, token_grad], axis=1))
     down_grad = (contract_rows(act_panel, grad_panel) * scale).astype(bf16)
     up_grad = (contract_rows(token_panel, dh_panel) * scale).astype(bf16)
-    return (both[:, :width], both[:, width:], up_grad, down_grad)
+    return (output, token_grad, up_grad, down_grad)
 
 
 def solution(mesh):

time: 132 us -> 155 us (1.17)
  starting transfers between devices: 44.3 us -> 56.4 us
  other arithmetic: 3.37 us -> 12.6 us
  matrix products: 13.4 us -> 15.3 us
    ppermute x4, starting transfers between devices: 12.3 us -> 21.3 us  [swap_core(): return lax.ppermute(x, 'col', [(i ^ 1, i) for i in range(Y * XH * CORE)])]
    convert_element_type x6, other arithmetic: 0.47 us -> 6.11 us  [scatter_row(): two = swap_z((block(-sign * s) + two).astype(bf16), ways[1])]
    ppermute x32, starting transfers between devices: 27.5 us -> 30.5 us  [swap_z(): lax.ppermute(x, 'row', [(pairs(z, Z) * XL + k, z * XL + k) for z in range...]
    ppermute x2, waiting for transfers between devices: 5.07 us -> 2.94 us  [swap_xl(): return lax.ppermute(x, 'row', [(i ^ 1, i) for i in range(Z * XL)])]
    convert_element_type x2, other arithmetic: 0.14 us -> 2.11 us  [scatter_row(): return total + swap_xl(total.astype(bf16)).astype(f32)]
    dot_general x1, matrix products: 1.38 us -> 3.33 us  [local(): jnp.dot(token_panel, up_weight, preferred_element_type=f32)]
    unnamed x18 -> x21, local copies, waits for them, and re-layouts: 0.04 us -> 1.68 us
  transfers between devices with their start and end apart: 39 -> 39, of which waited for: 27 -> 21; matrix products, arithmetic and copies ran while one was open for 11% -> 13% of each run, Pallas kernels for 0% -> 0%
where the time goes in v4:
time: 155 us; the launch traced here: 154 us
  starting transfers between devices  56.4 us (36%)
  waiting for transfers between devices  45.9 us (30%)
  blocking collectives  20.8 us (13%)
  matrix products  15.3 us (10%)
  other arithmetic  12.6 us (8%)
  local copies, waits for them, and re-layouts  2.41 us (2%)
    ppermute x32, waiting for transfers between devices, swap_z(): lax.ppermute(x, 'row', [(pairs(z, Z) * XL + k, z * XL + k) for z in range...  35 us
    ppermute x32, starting transfers between devices, swap_z(): lax.ppermute(x, 'row', [(pairs(z, Z) * XL + k, z * XL + k) for z in range...  30.5 us
    ppermute x4, starting transfers between devices, swap_core(): return lax.ppermute(x, 'col', [(i ^ 1, i) for i in range(Y * XH * CORE)])  21.3 us
    all_to_all x1, blocking collectives, exchange_col(): return lax.all_to_all(x, 'col', 0, 0, axis_index_groups=groups, tiled=True)  20.8 us
    dot_general x2, matrix products, contract_rows(): lax.dot_general(left, right, (((0,), (0,)), ((), ())), preferred_element_...  7.41 us
    all_to_all x1, waiting for transfers between devices, exchange_col(): return lax.all_to_all(x, 'col', 0, 0, axis_index_groups=groups, tiled=True)  6.42 us
    convert_element_type x6, other arithmetic, scatter_row(): two = swap_z((block(-sign * s) + two).astype(bf16), ways[1])  6.11 us
    all_to_all x1, starting transfers between devices, exchange_col(): return lax.all_to_all(x, 'col', 0, 0, axis_index_groups=groups, tiled=True)  3.55 us
  transfers between devices with their start and end apart: 39, of which 21 were waited for; matrix products, arithmetic and copies ran while one was open for 13% of the time, Pallas kernels for 0%

profile of v4, /device:TPU:1, one launch (start us, length us, event | category | flops | bytes accessed | tf_op | source)
XLA Modules:
  0.0 154.5 jit_solution(8288874905945312598)
XLA Ops:
  0.6 1.0 pad_maximum_fusion.2
  1.7 20.8 %all_to_all.18 = bf16[8,32,1536]{2,1,0:T(8,128)(2,1)S(1)} all-to-all(bf16[8,32,1536]{2,1,0:T(8,128)(2,1)S(1)} %broadcast_in_dim.2), channel_id=1, replica_groups={{0,2,4,6,8,10,12,14},{1,3,5,7,9,11,13,15},{16,18,20,22,24,26,28,30},{17..., dimensions={0} | all-to-all | bytes 1572864 | tf_op jit(solution)/shard_map/all_to_all | solution.py:56
  22.5 2.0 %collective-permute-start = (bf16[256,768]{1,0:T(8,128)(2,1)S(1)}, bf16[256,768]{1,0:T(8,128)(2,1)S(1)}, u32[]{:S(2)}, u32[]{:S(2)}) collective-permute-start(bf16[256,768]{1,0:T(8,128)(2,1)S(1)} %get-tuple-element.53), channel_id=1, source_target_pairs={{1,0},{0,1},{3,2},{2,3},{5,4},{4,5},{7,6},{6,7},{9,8},{8,9},{11,10... | collective-permute-start | bytes 1179656 | tf_op jit(solution)/shard_map/ppermute | solution.py:60
  24.5 1.3 collective-permute-done
  25.9 3.3 %fusion.23 = f32[512,1536]{1,0:T(8,128)S(1)} fusion(bf16[512,768]{1,0:T(8,128)(2,1)S(1)} %pad_maximum_fusion, bf16[768,1536]{1,0:T(8,128)(2,1)} %param.5), kind=kOutput, calls=%fused_computation.71 | convolution fusion | flops 1207959552 | bytes 6291456 | tf_op jit(solution)/shard_map/dot_general | solution.py:146
  29.2 1.6 %copy-done.2 = f32[512,1536]{1,0:T(8,128)} copy-done((f32[512,1536]{1,0:T(8,128)}, f32[512,1536]{1,0:T(8,128)S(1)}, u32[]{:S(2)}) %copy-start.2) | copy-done | bytes 3145752
  30.9 5.7 %collective-permute-start.3 = (bf16[64,768]{1,0:T(8,128)(2,1)S(1)}, bf16[64,768]{1,0:T(8,128)(2,1)S(1)}, u32[]{:S(2)}, u32[]{:S(2)}) collective-permute-start(bf16[64,768]{1,0:T(8,128)(2,1)S(1)} %get-tuple-element.56), channel_id=1, source_target_pairs={{224,0},{240,16},{64,32},{80,48},{32,64},{48,80},{128,96},{144,112... | collective-permute-start | bytes 294920 | tf_op jit(solution)/shard_map/ppermute | solution.py:44
  36.6 2.9 %collective-permute-done.3 = bf16[64,768]{1,0:T(8,128)(2,1)S(1)} collective-permute-done((bf16[64,768]{1,0:T(8,128)(2,1)S(1)}, bf16[64,768]{1,0:T(8,128)(2,1)S(1)}, u32[]{:S(2)}, u32[]{:S(2)}) %collective-permute-start.3) | collective-permute-done | bytes 98336 | tf_op jit(solution)/shard_map/ppermute | solution.py:44
  39.4 0.6 collective-permute-done.1
  40.0 1.2 add_convert_fusion.12
  41.2 1.8 %collective-permute-start.2 = (bf16[64,1536]{1,0:T(8,128)(2,1)S(1)}, bf16[64,1536]{1,0:T(8,128)(2,1)S(1)}, u32[]{:S(2)}, u32[]{:S(2)}) collective-permute-start(bf16[64,1536]{1,0:T(8,128)(2,1)S(1)} %get-tuple-element.49), channel_id=1, source_target_pairs={{224,0},{240,16},{64,32},{80,48},{32,64},{48,80},{128,96},{144,112... | collective-permute-start | bytes 589832 | tf_op jit(solution)/shard_map/ppermute | solution.py:44
  43.0 1.5 collective-permute-start.19
  44.5 2.5 %collective-permute-done.2 = bf16[64,1536]{1,0:T(8,128)(2,1)S(1)} collective-permute-done((bf16[64,1536]{1,0:T(8,128)(2,1)S(1)}, bf16[64,1536]{1,0:T(8,128)(2,1)S(1)}, u32[]{:S(2)}, u32[]{:S(2)}) %collective-permute-start.2) | collective-permute-done | bytes 196640 | tf_op jit(solution)/shard_map/ppermute | solution.py:44
  47.0 0.9 collective-permute-done.4
  47.9 1.2 add_convert_fusion.10
  49.5 1.3 collective-permute-start.6
  50.9 1.4 fusion.24
  52.4 1.5 collective-permute-start.22
  53.8 1.4 collective-permute-done.6
  55.2 1.2 add_convert_fusion.8
  56.4 1.4 collective-permute-start.7
  57.8 0.6 collective-permute-done.22
  58.5 1.5 collective-permute-start.21
  60.2 2.1 %collective-permute-done.7 = bf16[64,1536]{1,0:T(8,128)(2,1)S(1)} collective-permute-done((bf16[64,1536]{1,0:T(8,128)(2,1)S(1)}, bf16[64,1536]{1,0:T(8,128)(2,1)S(1)}, u32[]{:S(2)}, u32[]{:S(2)}) %collective-permute-start.7) | collective-permute-done | bytes 196640 | tf_op jit(solution)/shard_map/ppermute | solution.py:44
  62.8 1.7 %collective-permute-done.21 = bf16[64,1536]{1,0:T(8,128)(2,1)} collective-permute-done((bf16[64,1536]{1,0:T(8,128)(2,1)S(1)}, bf16[64,1536]{1,0:T(8,128)(2,1)}, u32[]{:S(2)}, u32[]{:S(2)}) %collective-permute-start.21) | collective-permute-done | bytes 196640 | tf_op jit(solution)/shard_map/ppermute | solution.py:44
  65.0 1.3 add_convert_fusion.4
  66.4 0.5 collective-permute-start.24
  66.9 1.4 collective-permute-start.25
  68.3 1.1 fusion.19
  69.3 0.6 collective-permute-start.9
  69.9 1.8 %collective-permute-done.24 = bf16[64,1536]{1,0:T(8,128)(2,1)S(1)} collective-permute-done((bf16[64,1536]{1,0:T(8,128)(2,1)S(1)}, bf16[64,1536]{1,0:T(8,128)(2,1)S(1)}, u32[]{:S(2)}, u32[]{:S(2)}) %collective-permute-start.24) | collective-permute-done | bytes 196640 | tf_op jit(solution)/shard_map/ppermute | solution.py:44
  71.8 0.8 collective-permute-done.25
  72.6 1.2 add_convert_fusion.2
  73.8 1.5 collective-permute-start.26
  75.5 1.5 %collective-permute-start.10 = (bf16[64,1536]{1,0:T(8,128)(2,1)S(1)}, bf16[64,1536]{1,0:T(8,128)(2,1)S(1)}, u32[]{:S(2)}, u32[]{:S(2)}) collective-permute-start(bf16[64,1536]{1,0:T(8,128)(2,1)S(1)} %get-tuple-element.33), channel_id=1, source_target_pairs={{32,0},{48,16},{0,32},{16,48},{96,64},{112,80},{64,96},{80,112},{1... | collective-permute-start | bytes 589832 | tf_op jit(solution)/shard_map/ppermute | solution.py:44
  77.1 1.3 collective-permute-start.11
  78.4 3.0 %collective-permute-done.26 = bf16[64,1536]{1,0:T(8,128)(2,1)S(1)} collective-permute-done((bf16[64,1536]{1,0:T(8,128)(2,1)S(1)}, bf16[64,1536]{1,0:T(8,128)(2,1)S(1)}, u32[]{:S(2)}, u32[]{:S(2)}) %collective-permute-start.26) | collective-permute-done | bytes 196640 | tf_op jit(solution)/shard_map/ppermute | solution.py:44
  81.4 1.1 fusion.15
  82.9 1.0 collective-permute-start.12
  84.1 2.9 %collective-permute-done.28 = bf16[64,1536]{1,0:T(8,128)(2,1)S(1)} collective-permute-done((bf16[64,1536]{1,0:T(8,128)(2,1)S(1)}, bf16[64,1536]{1,0:T(8,128)(2,1)S(1)}, u32[]{:S(2)}, u32[]{:S(2)}) %collective-permute-start.28) | collective-permute-done | bytes 196640 | tf_op jit(solution)/shard_map/ppermute | solution.py:50
  87.1 1.4 constant_dynamic-update-slice_fusion.7
  88.8 1.6 %collective-permute-start.30 = (bf16[64,1536]{1,0:T(8,128)(2,1)S(1)}, bf16[64,1536]{1,0:T(8,128)(2,1)S(1)}, u32[]{:S(2)}, u32[]{:S(2)}) collective-permute-start(bf16[64,1536]{1,0:T(8,128)(2,1)S(1)} %get-tuple-element.35), channel_id=1, source_target_pairs={{224,0},{240,16},{64,32},{80,48},{32,64},{48,80},{128,96},{144,112... | collective-permute-start | bytes 589832 | tf_op jit(solution)/shard_map/ppermute | solution.py:44
  90.7 1.1 collective-permute-start.15
  91.9 6.0 %collective-permute-done.14 = bf16[64,1536]{1,0:T(8,128)(2,1)S(1)} collective-permute-done((bf16[64,1536]{1,0:T(8,128)(2,1)S(1)}, bf16[64,1536]{1,0:T(8,128)(2,1)S(1)}, u32[]{:S(2)}, u32[]{:S(2)}) %collective-permute-start.14) | collective-permute-done | bytes 196640 | tf_op jit(solution)/shard_map/ppermute | solution.py:44
  97.9 1.1 collective-permute-start.16
  99.1 1.8 %collective-permute-start.31 = (bf16[64,1536]{1,0:T(8,128)(2,1)S(1)}, bf16[64,1536]{1,0:T(8,128)(2,1)S(1)}, u32[]{:S(2)}, u32[]{:S(2)}) collective-permute-start(bf16[64,1536]{1,0:T(8,128)(2,1)S(1)} %collective-permute-done.29), channel_id=1, source_target_pairs={{224,0},{240,16},{64,32},{80,48},{32,64},{48,80},{128,96},{144,112... | collective-permute-start | bytes 589832 | tf_op jit(solution)/shard_map/ppermute | solution.py:44
  100.9 0.6 collective-permute-start.32
  101.6 2.3 %collective-permute-done.16 = bf16[64,768]{1,0:T(8,128)(2,1)S(1)} collective-permute-done((bf16[64,768]{1,0:T(8,128)(2,1)S(1)}, bf16[64,768]{1,0:T(8,128)(2,1)S(1)}, u32[]{:S(2)}, u32[]{:S(2)}) %collective-permute-start.16) | collective-permute-done | bytes 98336 | tf_op jit(solution)/shard_map/ppermute | solution.py:44
  103.9 0.8 fusion.4
  104.7 13.8 %collective-permute-start.18 = (f32[256,768]{1,0:T(8,128)S(1)}, f32[256,768]{1,0:T(8,128)S(1)}, u32[]{:S(2)}, u32[]{:S(2)}) collective-permute-start(f32[256,768]{1,0:T(8,128)S(1)} %fusion.4), channel_id=1, source_target_pairs={{1,0},{0,1},{3,2},{2,3},{5,4},{4,5},{7,6},{6,7},{9,8},{8,9},{11,10... | collective-permute-start | bytes 2359304 | tf_op jit(solution)/shard_map/ppermute | solution.py:60
  118.6 1.1 collective-permute-start.34
  119.7 3.8 %collective-permute-done.33 = bf16[64,1536]{1,0:T(8,128)(2,1)S(1)} collective-permute-done((bf16[64,1536]{1,0:T(8,128)(2,1)S(1)}, bf16[64,1536]{1,0:T(8,128)(2,1)S(1)}, u32[]{:S(2)}, u32[]{:S(2)}) %collective-permute-start.33) | collective-permute-done | bytes 196640 | tf_op jit(solution)/shard_map/ppermute | solution.py:44
  123.5 1.3 collective-permute-start.35
  125.1 3.4 %collective-permute-done.35 = bf16[64,768]{1,0:T(8,128)(2,1)S(1)} collective-permute-done((bf16[64,768]{1,0:T(8,128)(2,1)S(1)}, bf16[64,768]{1,0:T(8,128)(2,1)S(1)}, u32[]{:S(2)}, u32[]{:S(2)}) %collective-permute-start.35) | collective-permute-done | bytes 98336 | tf_op jit(solution)/shard_map/ppermute | solution.py:44
  128.5 0.8 fusion
  129.3 4.0 %collective-permute-start.37 = (f32[256,768]{1,0:T(8,128)S(1)}, f32[256,768]{1,0:T(8,128)S(1)}, u32[]{:S(2)}, u32[]{:S(2)}) collective-permute-start(f32[256,768]{1,0:T(8,128)S(1)} %fusion), channel_id=1, source_target_pairs={{1,0},{0,1},{3,2},{2,3},{5,4},{4,5},{7,6},{6,7},{9,8},{8,9},{11,10... | collective-permute-start | bytes 2359304 | tf_op jit(solution)/shard_map/ppermute | solution.py:60
  133.4 0.8 fusion.6
  134.2 0.8 fusion.2
  135.4 0.9 pad_maximum_fusion.1
  136.3 3.5 %all-to-all-start.1 = ((bf16[8,32,1536]{2,1,0:T(8,128)(2,1)}), bf16[8,32,1536]{2,1,0:T(8,128)(2,1)S(1)}, u32[]{:S(2)}, u32[]{:S(2)}) async-start(bf16[8,32,1536]{2,1,0:T(8,128)(2,1)} %bitcast.18), calls=%async_computation.1 | async-start | bytes 1572864 | tf_op jit(solution)/shard_map/all_to_all | solution.py:56
  139.9 4.6 %multiply_convert_fusion = bf16[1536,768]{1,0:T(8,128)(2,1)} fusion(bf16[512,1536]{1,0:T(8,128)(2,1)} %copy-done.5, bf16[512,768]{1,0:T(8,128)(2,1)} %copy-done.8), kind=kOutput, calls=%fused_computation | convolution fusion | flops 1210318848 | bytes 4718592 | tf_op jit(solution)/shard_map/dot_general | solution.py:24
  144.5 2.8 %multiply_convert_fusion.1 = bf16[768,1536]{1,0:T(8,128)(2,1)} fusion(bf16[512,768]{1,0:T(8,128)(2,1)S(1)} %copy-done.7, bf16[512,1536]{1,0:T(8,128)(2,1)S(1)} %copy-done.4), kind=kOutput, calls=%fused_computation.1 | convolution fusion | flops 1210318848 | bytes 4718592 | tf_op jit(solution)/shard_map/dot_general | solution.py:24
  147.3 6.4 %all-to-all-done.1 = bf16[8,32,1536]{2,1,0:T(8,128)(2,1)S(1)} async-done(((bf16[8,32,1536]{2,1,0:T(8,128)(2,1)}), bf16[8,32,1536]{2,1,0:T(8,128)(2,1)S(1)}, u32[]{:S(2)}, u32[]{:S(2)}) %all-to-all-start.1) | async-done | bytes 786464 | tf_op jit(solution)/shard_map/all_to_all | solution.py:56
  153.7 0.7 fusion.17
  (89 shorter events, 4.6 us)
Async XLA Ops:
  0.6 50.2 %copy-start = (bf16[1536,768]{1,0:T(8,128)(2,1)S(1)}, bf16[1536,768]{1,0:T(8,128)(2,1)}, u32[]{:S(2)}) copy-start(bf16[1536,768]{1,0:T(8,128)(2,1)} %param.6) | copy-start | bytes 7077892
  22.5 3.3 %collective-permute-start = (bf16[256,768]{1,0:T(8,128)(2,1)S(1)}, bf16[256,768]{1,0:T(8,128)(2,1)S(1)}, u32[]{:S(2)}, u32[]{:S(2)}) collective-permute-start(bf16[256,768]{1,0:T(8,128)(2,1)S(1)} %get-tuple-element.53), channel_id=1, source_target_pairs={{1,0},{0,1},{3,2},{2,3},{5,4},{4,5},{7,6},{6,7},{9,8},{8,9},{11,10... | collective-permute-start | bytes 1179656 | tf_op jit(solution)/shard_map/ppermute | solution.py:60
  25.9 3.3 %copy-start.6 = (bf16[512,768]{1,0:T(8,128)(2,1)}, bf16[512,768]{1,0:T(8,128)(2,1)S(1)}, u32[]{:S(2)}) copy-start(bf16[512,768]{1,0:T(8,128)(2,1)S(1)} %pad_maximum_fusion) | copy-start | bytes 2359300
  29.2 1.6 %copy-start.2 = (f32[512,1536]{1,0:T(8,128)}, f32[512,1536]{1,0:T(8,128)S(1)}, u32[]{:S(2)}) copy-start(f32[512,1536]{1,0:T(8,128)S(1)} %fusion.23) | copy-start | bytes 9437188
  30.9 8.5 %collective-permute-start.3 = (bf16[64,768]{1,0:T(8,128)(2,1)S(1)}, bf16[64,768]{1,0:T(8,128)(2,1)S(1)}, u32[]{:S(2)}, u32[]{:S(2)}) collective-permute-start(bf16[64,768]{1,0:T(8,128)(2,1)S(1)} %get-tuple-element.56), channel_id=1, source_target_pairs={{224,0},{240,16},{64,32},{80,48},{32,64},{48,80},{128,96},{144,112... | collective-permute-start | bytes 294920 | tf_op jit(solution)/shard_map/ppermute | solution.py:44
  36.6 3.5 %collective-permute-start.1 = (bf16[64,768]{1,0:T(8,128)(2,1)S(1)}, bf16[64,768]{1,0:T(8,128)(2,1)S(1)}, u32[]{:S(2)}, u32[]{:S(2)}) collective-permute-start(bf16[64,768]{1,0:T(8,128)(2,1)S(1)} %get-tuple-element.57), channel_id=1, source_target_pairs={{32,0},{48,16},{0,32},{16,48},{96,64},{112,80},{64,96},{80,112},{1... | collective-permute-start | bytes 294920 | tf_op jit(solution)/shard_map/ppermute | solution.py:44
  41.2 5.8 %collective-permute-start.2 = (bf16[64,1536]{1,0:T(8,128)(2,1)S(1)}, bf16[64,1536]{1,0:T(8,128)(2,1)S(1)}, u32[]{:S(2)}, u32[]{:S(2)}) collective-permute-start(bf16[64,1536]{1,0:T(8,128)(2,1)S(1)} %get-tuple-element.49), channel_id=1, source_target_pairs={{224,0},{240,16},{64,32},{80,48},{32,64},{48,80},{128,96},{144,112... | collective-permute-start | bytes 589832 | tf_op jit(solution)/shard_map/ppermute | solution.py:44
  43.0 4.9 %collective-permute-start.4 = (bf16[64,1536]{1,0:T(8,128)(2,1)S(1)}, bf16[64,1536]{1,0:T(8,128)(2,1)S(1)}, u32[]{:S(2)}, u32[]{:S(2)}) collective-permute-start(bf16[64,1536]{1,0:T(8,128)(2,1)S(1)} %get-tuple-element.48), channel_id=1, source_target_pairs={{32,0},{48,16},{0,32},{16,48},{96,64},{112,80},{64,96},{80,112},{1... | collective-permute-start | bytes 589832 | tf_op jit(solution)/shard_map/ppermute | solution.py:44
  43.0 7.8 %collective-permute-start.19 = (bf16[256,768]{1,0:T(8,128)(2,1)S(1)}, bf16[256,768]{1,0:T(8,128)(2,1)S(1)}, u32[]{:S(2)}, u32[]{:S(2)}) collective-permute-start(bf16[256,768]{1,0:T(8,128)(2,1)S(1)} %get-tuple-element.25), channel_id=1, source_target_pairs={{1,0},{0,1},{3,2},{2,3},{5,4},{4,5},{7,6},{6,7},{9,8},{8,9},{11,10... | collective-permute-start | bytes 1179656 | tf_op jit(solution)/shard_map/ppermute | solution.py:60
  49.1 4.7 %collective-permute-start.5 = (bf16[64,1536]{1,0:T(8,128)(2,1)S(1)}, bf16[64,1536]{1,0:T(8,128)(2,1)S(1)}, u32[]{:S(2)}, u32[]{:S(2)}) collective-permute-start(bf16[64,1536]{1,0:T(8,128)(2,1)S(1)} %get-tuple-element.47), channel_id=1, source_target_pairs={{32,0},{48,16},{0,32},{16,48},{96,64},{112,80},{64,96},{80,112},{1... | collective-permute-start | bytes 589832 | tf_op jit(solution)/shard_map/ppermute | solution.py:44
  49.5 5.7 %collective-permute-start.6 = (bf16[64,1536]{1,0:T(8,128)(2,1)S(1)}, bf16[64,1536]{1,0:T(8,128)(2,1)S(1)}, u32[]{:S(2)}, u32[]{:S(2)}) collective-permute-start(bf16[64,1536]{1,0:T(8,128)(2,1)S(1)} %get-tuple-element.46), channel_id=1, source_target_pairs={{224,0},{240,16},{64,32},{80,48},{32,64},{48,80},{128,96},{144,112... | collective-permute-start | bytes 589832 | tf_op jit(solution)/shard_map/ppermute | solution.py:44
  50.8 1.4 copy-start.8
  52.3 6.2 %copy-start.1 = (f32[512,1536]{1,0:T(8,128)}, f32[512,1536]{1,0:T(8,128)S(1)}, u32[]{:S(2)}) copy-start(f32[512,1536]{1,0:T(8,128)S(1)} %fusion.24) | copy-start | bytes 9437188
  52.4 6.1 %collective-permute-start.22 = (bf16[64,768]{1,0:T(8,128)(2,1)S(1)}, bf16[64,768]{1,0:T(8,128)(2,1)S(1)}, u32[]{:S(2)}, u32[]{:S(2)}) collective-permute-start(bf16[64,768]{1,0:T(8,128)(2,1)S(1)} %get-tuple-element.54), channel_id=1, source_target_pairs={{224,0},{240,16},{64,32},{80,48},{32,64},{48,80},{128,96},{144,112... | collective-permute-start | bytes 294920 | tf_op jit(solution)/shard_map/ppermute | solution.py:44
  53.8 4.7 %collective-permute-start.20 = (bf16[64,768]{1,0:T(8,128)(2,1)S(1)}, bf16[64,768]{1,0:T(8,128)(2,1)S(1)}, u32[]{:S(2)}, u32[]{:S(2)}) collective-permute-start(bf16[64,768]{1,0:T(8,128)(2,1)S(1)} %get-tuple-element.55), channel_id=1, source_target_pairs={{32,0},{48,16},{0,32},{16,48},{96,64},{112,80},{64,96},{80,112},{1... | collective-permute-start | bytes 294920 | tf_op jit(solution)/shard_map/ppermute | solution.py:44
  56.4 5.9 %collective-permute-start.7 = (bf16[64,1536]{1,0:T(8,128)(2,1)S(1)}, bf16[64,1536]{1,0:T(8,128)(2,1)S(1)}, u32[]{:S(2)}, u32[]{:S(2)}) collective-permute-start(bf16[64,1536]{1,0:T(8,128)(2,1)S(1)} %get-tuple-element.45), channel_id=1, source_target_pairs={{224,0},{240,16},{64,32},{80,48},{32,64},{48,80},{128,96},{144,112... | collective-permute-start | bytes 589832 | tf_op jit(solution)/shard_map/ppermute | solution.py:44
  57.8 5.0 %collective-permute-start.8 = (bf16[64,1536]{1,0:T(8,128)(2,1)S(1)}, bf16[64,1536]{1,0:T(8,128)(2,1)S(1)}, u32[]{:S(2)}, u32[]{:S(2)}) collective-permute-start(bf16[64,1536]{1,0:T(8,128)(2,1)S(1)} %get-tuple-element.44), channel_id=1, source_target_pairs={{32,0},{48,16},{0,32},{16,48},{96,64},{112,80},{64,96},{80,112},{1... | collective-permute-start | bytes 589832 | tf_op jit(solution)/shard_map/ppermute | solution.py:44
  58.5 6.0 %collective-permute-start.21 = (bf16[64,1536]{1,0:T(8,128)(2,1)S(1)}, bf16[64,1536]{1,0:T(8,128)(2,1)}, u32[]{:S(2)}, u32[]{:S(2)}) collective-permute-start(bf16[64,1536]{1,0:T(8,128)(2,1)S(1)} %get-tuple-element.43), channel_id=1, source_target_pairs={{224,0},{240,16},{64,32},{80,48},{32,64},{48,80},{128,96},{144,112... | collective-permute-start | bytes 589832 | tf_op jit(solution)/shard_map/ppermute | solution.py:44
  60.0 5.0 %collective-permute-start.23 = (bf16[64,1536]{1,0:T(8,128)(2,1)S(1)}, bf16[64,1536]{1,0:T(8,128)(2,1)}, u32[]{:S(2)}, u32[]{:S(2)}) collective-permute-start(bf16[64,1536]{1,0:T(8,128)(2,1)S(1)} %get-tuple-element.42), channel_id=1, source_target_pairs={{32,0},{48,16},{0,32},{16,48},{96,64},{112,80},{64,96},{80,112},{1... | collective-permute-start | bytes 589832 | tf_op jit(solution)/shard_map/ppermute | solution.py:44
  66.4 5.4 %collective-permute-start.24 = (bf16[64,1536]{1,0:T(8,128)(2,1)S(1)}, bf16[64,1536]{1,0:T(8,128)(2,1)S(1)}, u32[]{:S(2)}, u32[]{:S(2)}) collective-permute-start(bf16[64,1536]{1,0:T(8,128)(2,1)S(1)} %get-tuple-element.41), channel_id=1, source_target_pairs={{32,0},{48,16},{0,32},{16,48},{96,64},{112,80},{64,96},{80,112},{1... | collective-permute-start | bytes 589832 | tf_op jit(solution)/shard_map/ppermute | solution.py:44
  66.9 5.7 %collective-permute-start.25 = (bf16[64,1536]{1,0:T(8,128)(2,1)S(1)}, bf16[64,1536]{1,0:T(8,128)(2,1)S(1)}, u32[]{:S(2)}, u32[]{:S(2)}) collective-permute-start(bf16[64,1536]{1,0:T(8,128)(2,1)S(1)} %get-tuple-element.40), channel_id=1, source_target_pairs={{224,0},{240,16},{64,32},{80,48},{32,64},{48,80},{128,96},{144,112... | collective-permute-start | bytes 589832 | tf_op jit(solution)/shard_map/ppermute | solution.py:44
  69.3 5.9 %collective-permute-start.9 = (bf16[64,1536]{1,0:T(8,128)(2,1)S(1)}, bf16[64,1536]{1,0:T(8,128)(2,1)S(1)}, u32[]{:S(2)}, u32[]{:S(2)}) collective-permute-start(bf16[64,1536]{1,0:T(8,128)(2,1)S(1)} %get-tuple-element.36), channel_id=1, source_target_pairs={{16,0},{0,16},{48,32},{32,48},{80,64},{64,80},{112,96},{96,112},{1... | collective-permute-start | bytes 589832 | tf_op jit(solution)/shard_map/ppermute | solution.py:50
  73.8 7.6 %collective-permute-start.26 = (bf16[64,1536]{1,0:T(8,128)(2,1)S(1)}, bf16[64,1536]{1,0:T(8,128)(2,1)S(1)}, u32[]{:S(2)}, u32[]{:S(2)}) collective-permute-start(bf16[64,1536]{1,0:T(8,128)(2,1)S(1)} %get-tuple-element.39), channel_id=1, source_target_pairs={{224,0},{240,16},{64,32},{80,48},{32,64},{48,80},{128,96},{144,112... | collective-permute-start | bytes 589832 | tf_op jit(solution)/shard_map/ppermute | solution.py:44
  75.3 6.1 %collective-permute-start.27 = (bf16[64,1536]{1,0:T(8,128)(2,1)S(1)}, bf16[64,1536]{1,0:T(8,128)(2,1)S(1)}, u32[]{:S(2)}, u32[]{:S(2)}) collective-permute-start(bf16[64,1536]{1,0:T(8,128)(2,1)S(1)} %get-tuple-element.38), channel_id=1, source_target_pairs={{32,0},{48,16},{0,32},{16,48},{96,64},{112,80},{64,96},{80,112},{1... | collective-permute-start | bytes 589832 | tf_op jit(solution)/shard_map/ppermute | solution.py:44
  75.5 7.3 %collective-permute-start.10 = (bf16[64,1536]{1,0:T(8,128)(2,1)S(1)}, bf16[64,1536]{1,0:T(8,128)(2,1)S(1)}, u32[]{:S(2)}, u32[]{:S(2)}) collective-permute-start(bf16[64,1536]{1,0:T(8,128)(2,1)S(1)} %get-tuple-element.33), channel_id=1, source_target_pairs={{32,0},{48,16},{0,32},{16,48},{96,64},{112,80},{64,96},{80,112},{1... | collective-permute-start | bytes 589832 | tf_op jit(solution)/shard_map/ppermute | solution.py:44
  77.1 6.9 %collective-permute-start.11 = (bf16[64,1536]{1,0:T(8,128)(2,1)S(1)}, bf16[64,1536]{1,0:T(8,128)(2,1)S(1)}, u32[]{:S(2)}, u32[]{:S(2)}) collective-permute-start(bf16[64,1536]{1,0:T(8,128)(2,1)S(1)} %get-tuple-element.33), channel_id=1, source_target_pairs={{224,0},{240,16},{64,32},{80,48},{32,64},{48,80},{128,96},{144,112... | collective-permute-start | bytes 589832 | tf_op jit(solution)/shard_map/ppermute | solution.py:44
  82.4 4.6 %collective-permute-start.28 = (bf16[64,1536]{1,0:T(8,128)(2,1)S(1)}, bf16[64,1536]{1,0:T(8,128)(2,1)S(1)}, u32[]{:S(2)}, u32[]{:S(2)}) collective-permute-start(bf16[64,1536]{1,0:T(8,128)(2,1)S(1)} %fusion.15), channel_id=1, source_target_pairs={{16,0},{0,16},{48,32},{32,48},{80,64},{64,80},{112,96},{96,112},{1... | collective-permute-start | bytes 589832 | tf_op jit(solution)/shard_map/ppermute | solution.py:50
  82.9 7.5 %collective-permute-start.12 = (bf16[64,1536]{1,0:T(8,128)(2,1)S(1)}, bf16[64,1536]{1,0:T(8,128)(2,1)S(1)}, u32[]{:S(2)}, u32[]{:S(2)}) collective-permute-start(bf16[64,1536]{1,0:T(8,128)(2,1)S(1)} %collective-permute-done.10), channel_id=1, source_target_pairs={{224,0},{240,16},{64,32},{80,48},{32,64},{48,80},{128,96},{144,112... | collective-permute-start | bytes 589832 | tf_op jit(solution)/shard_map/ppermute | solution.py:44
  84.0 6.8 %collective-permute-start.13 = (bf16[64,1536]{1,0:T(8,128)(2,1)S(1)}, bf16[64,1536]{1,0:T(8,128)(2,1)S(1)}, u32[]{:S(2)}, u32[]{:S(2)}) collective-permute-start(bf16[64,1536]{1,0:T(8,128)(2,1)S(1)} %collective-permute-done.11), channel_id=1, source_target_pairs={{32,0},{48,16},{0,32},{16,48},{96,64},{112,80},{64,96},{80,112},{1... | collective-permute-start | bytes 589832 | tf_op jit(solution)/shard_map/ppermute | solution.py:44
  88.5 10.6 %collective-permute-start.29 = (bf16[64,1536]{1,0:T(8,128)(2,1)S(1)}, bf16[64,1536]{1,0:T(8,128)(2,1)S(1)}, u32[]{:S(2)}, u32[]{:S(2)}) collective-permute-start(bf16[64,1536]{1,0:T(8,128)(2,1)S(1)} %get-tuple-element.35), channel_id=1, source_target_pairs={{32,0},{48,16},{0,32},{16,48},{96,64},{112,80},{64,96},{80,112},{1... | collective-permute-start | bytes 589832 | tf_op jit(solution)/shard_map/ppermute | solution.py:44
  88.8 12.2 %collective-permute-start.30 = (bf16[64,1536]{1,0:T(8,128)(2,1)S(1)}, bf16[64,1536]{1,0:T(8,128)(2,1)S(1)}, u32[]{:S(2)}, u32[]{:S(2)}) collective-permute-start(bf16[64,1536]{1,0:T(8,128)(2,1)S(1)} %get-tuple-element.35), channel_id=1, source_target_pairs={{224,0},{240,16},{64,32},{80,48},{32,64},{48,80},{128,96},{144,112... | collective-permute-start | bytes 589832 | tf_op jit(solution)/shard_map/ppermute | solution.py:44
  90.4 7.5 %collective-permute-start.14 = (bf16[64,1536]{1,0:T(8,128)(2,1)S(1)}, bf16[64,1536]{1,0:T(8,128)(2,1)S(1)}, u32[]{:S(2)}, u32[]{:S(2)}) collective-permute-start(bf16[64,1536]{1,0:T(8,128)(2,1)S(1)} %collective-permute-done.12), channel_id=1, source_target_pairs={{32,0},{48,16},{0,32},{16,48},{96,64},{112,80},{64,96},{80,112},{1... | collective-permute-start | bytes 589832 | tf_op jit(solution)/shard_map/ppermute | solution.py:44
  90.7 8.3 %collective-permute-start.15 = (bf16[64,1536]{1,0:T(8,128)(2,1)S(1)}, bf16[64,1536]{1,0:T(8,128)(2,1)S(1)}, u32[]{:S(2)}, u32[]{:S(2)}) collective-permute-start(bf16[64,1536]{1,0:T(8,128)(2,1)S(1)} %collective-permute-done.13), channel_id=1, source_target_pairs={{224,0},{240,16},{64,32},{80,48},{32,64},{48,80},{128,96},{144,112... | collective-permute-start | bytes 589832 | tf_op jit(solution)/shard_map/ppermute | solution.py:44
  97.9 5.9 %collective-permute-start.16 = (bf16[64,768]{1,0:T(8,128)(2,1)S(1)}, bf16[64,768]{1,0:T(8,128)(2,1)S(1)}, u32[]{:S(2)}, u32[]{:S(2)}) collective-permute-start(bf16[64,768]{1,0:T(8,128)(2,1)S(1)} %slice.146), channel_id=1, source_target_pairs={{224,0},{240,16},{64,32},{80,48},{32,64},{48,80},{128,96},{144,112... | collective-permute-start | bytes 294920 | tf_op jit(solution)/shard_map/ppermute | solution.py:44
  99.0 4.9 %collective-permute-start.17 = (bf16[64,768]{1,0:T(8,128)(2,1)S(1)}, bf16[64,768]{1,0:T(8,128)(2,1)S(1)}, u32[]{:S(2)}, u32[]{:S(2)}) collective-permute-start(bf16[64,768]{1,0:T(8,128)(2,1)S(1)} %slice.147), channel_id=1, source_target_pairs={{32,0},{48,16},{0,32},{16,48},{96,64},{112,80},{64,96},{80,112},{1... | collective-permute-start | bytes 294920 | tf_op jit(solution)/shard_map/ppermute | solution.py:44
  99.1 19.4 %collective-permute-start.31 = (bf16[64,1536]{1,0:T(8,128)(2,1)S(1)}, bf16[64,1536]{1,0:T(8,128)(2,1)S(1)}, u32[]{:S(2)}, u32[]{:S(2)}) collective-permute-start(bf16[64,1536]{1,0:T(8,128)(2,1)S(1)} %collective-permute-done.29), channel_id=1, source_target_pairs={{224,0},{240,16},{64,32},{80,48},{32,64},{48,80},{128,96},{144,112... | collective-permute-start | bytes 589832 | tf_op jit(solution)/shard_map/ppermute | solution.py:44
  100.9 17.6 %collective-permute-start.32 = (bf16[64,1536]{1,0:T(8,128)(2,1)S(1)}, bf16[64,1536]{1,0:T(8,128)(2,1)S(1)}, u32[]{:S(2)}, u32[]{:S(2)}) collective-permute-start(bf16[64,1536]{1,0:T(8,128)(2,1)S(1)} %collective-permute-done.30), channel_id=1, source_target_pairs={{32,0},{48,16},{0,32},{16,48},{96,64},{112,80},{64,96},{80,112},{1... | collective-permute-start | bytes 589832 | tf_op jit(solution)/shard_map/ppermute | solution.py:44
  103.9 29.4 %copy-start.5 = (bf16[512,1536]{1,0:T(8,128)(2,1)}, bf16[512,1536]{1,0:T(8,128)(2,1)S(1)}, u32[]{:S(2)}) copy-start(bf16[512,1536]{1,0:T(8,128)(2,1)S(1)} %constant_dynamic-update-slice_fusion.19) | copy-start | bytes 4718596
  104.7 23.8 %copy-start.9 = (bf16[768,1536]{1,0:T(8,128)(2,1)S(1)}, bf16[768,1536]{1,0:T(8,128)(2,1)}, u32[]{:S(2)}) copy-start(bf16[768,1536]{1,0:T(8,128)(2,1)} %param.5) | copy-start | bytes 7077892
  104.7 30.2 %collective-permute-start.18 = (f32[256,768]{1,0:T(8,128)S(1)}, f32[256,768]{1,0:T(8,128)S(1)}, u32[]{:S(2)}, u32[]{:S(2)}) collective-permute-start(f32[256,768]{1,0:T(8,128)S(1)} %fusion.4), channel_id=1, source_target_pairs={{1,0},{0,1},{3,2},{2,3},{5,4},{4,5},{7,6},{6,7},{9,8},{8,9},{11,10... | collective-permute-start | bytes 2359304 | tf_op jit(solution)/shard_map/ppermute | solution.py:60
  118.5 4.9 %collective-permute-start.33 = (bf16[64,1536]{1,0:T(8,128)(2,1)S(1)}, bf16[64,1536]{1,0:T(8,128)(2,1)S(1)}, u32[]{:S(2)}, u32[]{:S(2)}) collective-permute-start(bf16[64,1536]{1,0:T(8,128)(2,1)S(1)} %collective-permute-done.31), channel_id=1, source_target_pairs={{32,0},{48,16},{0,32},{16,48},{96,64},{112,80},{64,96},{80,112},{1... | collective-permute-start | bytes 589832 | tf_op jit(solution)/shard_map/ppermute | solution.py:44
  118.6 6.2 %collective-permute-start.34 = (bf16[64,1536]{1,0:T(8,128)(2,1)S(1)}, bf16[64,1536]{1,0:T(8,128)(2,1)S(1)}, u32[]{:S(2)}, u32[]{:S(2)}) collective-permute-start(bf16[64,1536]{1,0:T(8,128)(2,1)S(1)} %collective-permute-done.32), channel_id=1, source_target_pairs={{224,0},{240,16},{64,32},{80,48},{32,64},{48,80},{128,96},{144,112... | collective-permute-start | bytes 589832 | tf_op jit(solution)/shard_map/ppermute | solution.py:44
  123.5 5.0 %collective-permute-start.35 = (bf16[64,768]{1,0:T(8,128)(2,1)S(1)}, bf16[64,768]{1,0:T(8,128)(2,1)S(1)}, u32[]{:S(2)}, u32[]{:S(2)}) collective-permute-start(bf16[64,768]{1,0:T(8,128)(2,1)S(1)} %slice.152), channel_id=1, source_target_pairs={{224,0},{240,16},{64,32},{80,48},{32,64},{48,80},{128,96},{144,112... | collective-permute-start | bytes 294920 | tf_op jit(solution)/shard_map/ppermute | solution.py:44
  124.8 3.7 %collective-permute-start.36 = (bf16[64,768]{1,0:T(8,128)(2,1)S(1)}, bf16[64,768]{1,0:T(8,128)(2,1)S(1)}, u32[]{:S(2)}, u32[]{:S(2)}) collective-permute-start(bf16[64,768]{1,0:T(8,128)(2,1)S(1)} %slice.153), channel_id=1, source_target_pairs={{32,0},{48,16},{0,32},{16,48},{96,64},{112,80},{64,96},{80,112},{1... | collective-permute-start | bytes 294920 | tf_op jit(solution)/shard_map/ppermute | solution.py:44
  128.5 5.6 %copy-start.3 = (bf16[512,1536]{1,0:T(8,128)(2,1)}, bf16[512,1536]{1,0:T(8,128)(2,1)S(1)}, u32[]{:S(2)}) copy-start(bf16[512,1536]{1,0:T(8,128)(2,1)S(1)} %constant_dynamic-update-slice_fusion.18) | copy-start | bytes 4718596
  129.3 5.9 %collective-permute-start.37 = (f32[256,768]{1,0:T(8,128)S(1)}, f32[256,768]{1,0:T(8,128)S(1)}, u32[]{:S(2)}, u32[]{:S(2)}) collective-permute-start(f32[256,768]{1,0:T(8,128)S(1)} %fusion), channel_id=1, source_target_pairs={{1,0},{0,1},{3,2},{2,3},{5,4},{4,5},{7,6},{6,7},{9,8},{8,9},{11,10... | collective-permute-start | bytes 2359304 | tf_op jit(solution)/shard_map/ppermute | solution.py:60
  136.3 17.4 %all-to-all-start.1 = ((bf16[8,32,1536]{2,1,0:T(8,128)(2,1)}), bf16[8,32,1536]{2,1,0:T(8,128)(2,1)S(1)}, u32[]{:S(2)}, u32[]{:S(2)}) async-start(bf16[8,32,1536]{2,1,0:T(8,128)(2,1)} %bitcast.18), calls=%async_computation.1 | async-start | bytes 1572864 | tf_op jit(solution)/shard_map/all_to_all | solution.py:56
  139.9 4.6 %copy-start.4 = (bf16[512,1536]{1,0:T(8,128)(2,1)S(1)}, bf16[512,1536]{1,0:T(8,128)(2,1)}, u32[]{:S(2)}) copy-start(bf16[512,1536]{1,0:T(8,128)(2,1)} %copy-done.3) | copy-start | bytes 4718596
  139.9 4.6 %copy-start.7 = (bf16[512,768]{1,0:T(8,128)(2,1)S(1)}, bf16[512,768]{1,0:T(8,128)(2,1)}, u32[]{:S(2)}) copy-start(bf16[512,768]{1,0:T(8,128)(2,1)} %copy-done.6) | copy-start | bytes 2359300
